TPU v7x, 256 devices: a whole 4x4x8 slice. The times are simulated.
256 devices in a mesh: fsdp: 64 (over y, z, x_hi), tp: 4 (over x_lo, core).
Axes of the slice: x: 4 (x_hi: 2, x_lo: 2; x = x_hi * 2 + x_lo), y: 4, z: 8, core: 2. Of those that a mesh axis runs over, the one named last changes fastest.
Arguments:
- tokens_in: bfloat16 [98304, 5120], P(('fsdp', 'tp')), may hold values from -6 to 6
- cotangent: bfloat16 [98304, 2048], P('fsdp', 'tp'), may hold values from -6 to 6
- weight: bfloat16 [5120, 2048], P('fsdp', 'tp'), may hold values from -0.078125 to 0.078125
- hidden_rows: bfloat16 [256, 5120], P('fsdp'), may hold values from -6 to 6
- queries: bfloat16 [256, 5120], P('fsdp', 'tp')
- cache: bfloat16 [256, 1024, 2048], P('fsdp', None, 'tp')
- lengths: int32 [256], P('fsdp'), may hold values from 2 to 1024, as said below
Outputs:
- new_weight: bfloat16 [5120, 2048], P('fsdp', 'tp')
- attention: bfloat16 [256, 5120], P('fsdp', 'tp')
Inputs may be any that keep to these rules, and one draw needn't show every extreme that they name: `lengths`: each row has at least two live positions; some row has all 1024 live.
All inputs are finite; a program needn't handle non-finite values.
Results may differ from a plain program's by a relative error of at most 0.007.
Values may be sent and summed in bfloat16 or wider, within the bound.
No kernel may reach another device: no remote copies, remote signals or barrier semaphores. Data moves between devices by JAX's collectives and lax.ppermute only.
A program may use at most 128 MiB of HBM per device.

v0:
```python
import math

import jax
import jax.numpy as jnp
from jax import lax
from jax.sharding import PartitionSpec as P

KVH = 8
HD = 128


def attend(queries, cache, fresh, lengths, heads_kv, head_size):
    rows = cache.shape[0]
    span = cache.shape[1]
    group = queries.shape[1] // (heads_kv * head_size)
    query = queries.reshape(rows, heads_kv, group, head_size)
    stored = cache.reshape(rows, span, heads_kv, 2, head_size)
    latest = fresh.reshape(rows, heads_kv, 2, head_size)
    scores = jnp.einsum(
        "rjgd,rcjd->rjgc", query, stored[:, :, :, 0, :], preferred_element_type=jnp.float32
    ) / math.sqrt(head_size)
    newest = jnp.einsum(
        "rjgd,rjd->rjg", query, latest[:, :, 0, :], preferred_element_type=jnp.float32
    ) / math.sqrt(head_size)
    live = jnp.arange(span, dtype=jnp.int32)[None, :] < lengths[:, None]
    scores = jnp.where(live[:, None, None, :], scores, jnp.float32(-1e30))
    top = jnp.maximum(jnp.max(scores, axis=-1), newest)
    past_exp = jnp.exp(scores - top[..., None])
    new_exp = jnp.exp(newest - top)
    total = jnp.sum(past_exp, axis=-1) + new_exp
    past_prob = (past_exp / total[..., None]).astype(jnp.bfloat16)
    new_prob = (new_exp / total).astype(jnp.bfloat16)
    mixed = jnp.einsum(
        "rjgc,rcjd->rjgd", past_prob, stored[:, :, :, 1, :], preferred_element_type=jnp.float32
    )
    mixed = mixed + new_prob.astype(jnp.float32)[..., None] * latest[:, :, None, 1, :].astype(
        jnp.float32
    )
    return mixed.reshape(rows, -1).astype(jnp.bfloat16)


def local(tokens_in, cotangent, weight, hidden_rows, queries, cache, lengths):
    gathered = lax.all_gather(tokens_in, "tp", axis=0, tiled=True)
    grad = lax.psum_scatter(
        lax.dot_general(
            gathered, cotangent, (((0,), (0,)), ((), ())), preferred_element_type=jnp.float32
        ),
        "fsdp",
        scatter_dimension=0,
        tiled=True,
    )
    total_tokens = tokens_in.shape[0] * lax.axis_size("tp") * lax.axis_size("fsdp")
    factor = 0.01 / math.sqrt(total_tokens)
    new_weight = (weight.astype(jnp.float32) - factor * grad).astype(jnp.bfloat16)
    columns = lax.all_gather(new_weight, "fsdp", axis=0, tiled=True)
    fresh = jnp.dot(hidden_rows, columns, preferred_element_type=jnp.float32).astype(jnp.bfloat16)
    local_heads = KVH // lax.axis_size("tp")
    attention = attend(queries, cache, fresh, lengths, local_heads, HD)
    return (new_weight, attention)


def solution(mesh):
    in_specs = (
        P(("fsdp", "tp"), None),
        P("fsdp", "tp"),
        P("fsdp", "tp"),
        P("fsdp", None),
        P("fsdp", "tp"),
        P("fsdp", None, "tp"),
        P("fsdp"),
    )
    out_specs = (P("fsdp", "tp"), P("fsdp", "tp"))
    return jax.shard_map(local, mesh=mesh, in_specs=in_specs, out_specs=out_specs, check_vma=False)
```

profile of v0, /device:TPU:2, one launch (start us, length us, event | category | flops | bytes accessed | tf_op | source)
XLA Modules:
  0.0 702.2 jit_solution(13413807853053349763)
XLA Ops:
  7.2 0.0 copy-start
  7.2 0.0 all-gather.3.cloned.1.call-start
  7.2 0.7 all-gather.3.cloned.1.call-update
  7.9 0.0 reduce-scatter.2.cloned.1.call-start
  8.0 148.1 %all-gather.3.cloned.1.call-done = bf16[1536,5120]{1,0:T(8,128)(2,1)} async-done(((bf16[384,5120]{1,0:T(8,128)(2,1)}), bf16[1536,5120]{1,0:T(8,128)(2,1)}) %all-gather.3.cloned.1.call-update) | async-done | bytes 15728656 | tf_op jit(solution)/shard_map/all_gather | solution.py:43
  156.1 0.0 copy-done
  156.1 14.2 %fusion.15 = f32[5120,512]{1,0:T(8,128)} fusion(bf16[1536,5120]{1,0:T(8,128)(2,1)} %all-gather.3.cloned.1.call-done, bf16[1536,512]{1,0:T(8,128)(2,1)S(1)} %copy-done), kind=kOutput, calls=%fused_computation.27 | convolution fusion | flops 8053063680 | bytes 27787264 | tf_op jit(solution)/shard_map/dot_general | solution.py:45
  170.2 0.0 copy-start.1
  170.2 0.0 copy-start.3
  170.2 0.0 reduce-scatter.2.cloned.1.call-update
  170.2 0.0 all-gather.5.cloned.1.call-start
  170.3 388.1 %reduce-scatter.2.cloned.1.call-done = f32[80,512]{1,0:T(8,128)} async-done(((f32[5120,512]{1,0:T(8,128)}), f32[80,512]{1,0:T(8,128)}) %reduce-scatter.2.cloned.1.call-update) | async-done | bytes 163856 | tf_op jit(solution)/shard_map/reduce_scatter | solution.py:44
  558.4 0.0 copy-done.1
  558.4 1.6 subtract_convert_fusion
  560.0 0.0 all-gather.5.cloned.1.call-update
  560.0 0.0 copy-done.3
  560.0 0.0 copy-start.4
  560.0 0.0 copy-start.2
  560.1 6.3 copy.9
  566.4 0.0 copy-done.4
  566.4 0.1 iota_compare_fusion
  566.5 2.1 fusion.14
  568.5 120.5 %all-gather.5.cloned.1.call-done = bf16[5120,512]{1,0:T(8,128)(2,1)} async-done(((bf16[80,512]{1,0:T(8,128)(2,1)}), bf16[5120,512]{1,0:T(8,128)(2,1)}) %all-gather.5.cloned.1.call-update) | async-done | bytes 5242896 | tf_op jit(solution)/shard_map/all_gather | solution.py:55
  689.0 0.0 copy-done.2
  689.0 3.3 fusion.6
  692.4 0.1 fusion.10
  692.5 0.2 fusion.7
  692.7 2.3 fusion.5
  695.0 0.6 convert_element_type.36
  (6 shorter events, 0.1 us)
Async XLA Ops:
  7.2 148.9 %copy-start = (bf16[1536,512]{1,0:T(8,128)(2,1)S(1)}, bf16[1536,512]{1,0:T(8,128)(2,1)}, u32[]{:S(2)}) copy-start(bf16[1536,512]{1,0:T(8,128)(2,1)} %param.8) | copy-start | bytes 4718596
  7.2 148.9 %all-gather.3.cloned.1.call-start = ((), (), s32[]{:S(2)}) async-start(), calls=%async_computation.1 | async-start | bytes 19660800 | tf_op jit(solution)/shard_map/all_gather | solution.py:43
  7.9 550.5 %reduce-scatter.2.cloned.1.call-start = ((), (), s32[]{:S(2)}) async-start(), calls=%async_computation.2 | async-start | bytes 10649600 | tf_op jit(solution)/shard_map/reduce_scatter | solution.py:44
  170.2 388.2 %copy-start.1 = (bf16[80,512]{1,0:T(8,128)(2,1)S(1)}, bf16[80,512]{1,0:T(8,128)(2,1)}, u32[]{:S(2)}) copy-start(bf16[80,512]{1,0:T(8,128)(2,1)} %param.9) | copy-start | bytes 245764
  170.2 389.8 %copy-start.3 = (bf16[4,1280]{1,0:T(4,128)(2,1)S(1)}, bf16[4,1280]{1,0:T(4,128)(2,1)}, u32[]{:S(2)}) copy-start(bf16[4,1280]{1,0:T(4,128)(2,1)} %param.11) | copy-start | bytes 30724
  170.2 518.8 %all-gather.5.cloned.1.call-start = ((), (), s32[]{:S(2)}) async-start(), calls=%async_computation.3 | async-start | bytes 5324800 | tf_op jit(solution)/shard_map/all_gather | solution.py:55
  560.0 6.4 copy-start.4
  560.0 129.0 %copy-start.2 = (bf16[4,5120]{1,0:T(4,128)(2,1)S(1)}, bf16[4,5120]{1,0:T(4,128)(2,1)}, u32[]{:S(2)}) copy-start(bf16[4,5120]{1,0:T(4,128)(2,1)} %param.10) | copy-start | bytes 122884
Sparse Core Ops, SparseCore 0:
  9.8 146.1 all-gather.2
  170.4 387.9 reduce-scatter.1
  562.6 126.4 all-gather.4
where the time goes:
time: 703 us; the launch traced here: 702 us
  waiting for transfers between devices  657 us (93%)
  matrix products  21.9 us (3%)
  between operations  13.8 us (2%)
  local copies, waits for them, and re-layouts  7.03 us (1%)
    reduce_scatter x1, waiting for transfers between devices, local(): lax.psum_scatter(lax.dot_general(gathered, cotangent, (((0,), (0,)), ((),...  388 us
    all_gather x1, waiting for transfers between devices, local(): gathered = lax.all_gather(tokens_in, 'tp', axis=0, tiled=True)  148 us
    all_gather x1, waiting for transfers between devices, local(): columns = lax.all_gather(new_weight, 'fsdp', axis=0, tiled=True)  121 us
    dot_general x1, matrix products, local(): lax.dot_general(gathered, cotangent, (((0,), (0,)), ((), ())), preferred_...  14.2 us
  transfers between devices with their start and end apart: 3, of which 3 were waited for; matrix products, arithmetic and copies ran while one was open for 1% of the time, Pallas kernels for 0%

commit v1 on v0

v1 whole, which is shorter than its diff:
```python
import functools
import math

import jax
import jax.numpy as jnp
import numpy as np
from jax import lax
from jax.experimental import pallas as pl
from jax.experimental.pallas import tpu as pltpu
from jax.sharding import Mesh
from jax.sharding import PartitionSpec as P

KVH = 8
HD = 128
F32 = jnp.float32
BF16 = jnp.bfloat16
X = ("xh", "xl")
VMEM = pl.BlockSpec(memory_space=pltpu.VMEM)


def shift(value, axis, size, by):
    return lax.ppermute(value, axis, [(i, (i + by) % size) for i in range(size)])


def swap(value, axis, size, bits):
    return lax.ppermute(value, axis, [(i, i ^ bits) for i in range(size)])


def pick(array, index, axis=0):
    return lax.dynamic_index_in_dim(array, index, axis, keepdims=False)


def add(a, b):
    return (a.astype(F32) + b.astype(F32)).astype(BF16)


def product_kernel(split, rows, place, a_ref, b_ref, ca_ref, cb_ref, *outs):
    by_y, by_x = outs[:4], outs[4:]
    turn = pl.program_id(0)
    contract = (((0,), (0,)), ((), ()))
    total = lax.dot_general(a_ref[...], ca_ref[...], contract, preferred_element_type=F32)
    total += lax.dot_general(b_ref[...], cb_ref[...], contract, preferred_element_type=F32)
    total = total.astype(BF16)
    part = total.shape[1] // 2
    for k in range(4):

        @pl.when(turn == k)
        def _(k=k):
            by_y[k][...] = total[:, :part]

    def store(near, far):
        for i in range(total.shape[0] // (2 * rows)):
            here = slice(i * rows, (i + 1) * rows)
            for target, at in ((near, 2 * i), (far, 2 * i + 1)):
                for out in target:
                    out[here, :] = total[at * rows : (at + 1) * rows, part:]

    first = place[1]
    if split:
        for low in (True, False):
            for flip in (0, 1):

                @pl.when(((turn < 2) == low) & (first == flip))
                def _(low=low, flip=flip):
                    pair = ((by_x[0],), (by_x[1] if low else by_x[2],))
                    store(*(pair if flip == 0 else pair[::-1]))
    else:
        for flip in (0, 1):

            @pl.when(first == flip)
            def _(flip=flip):
                pair = ((by_x[0],), (by_x[1],))
                store(*(pair if flip == 0 else pair[::-1]))


def product(split, rows, place, own, other, own_cot, other_cot):
    tokens, width = own.shape
    columns = own_cot.shape[1]
    part = columns // 2
    steps = 2
    tall = width // (4 * steps)

    def within(first, last):
        def index(turn, step, place):
            at = (turn - first) * steps + step
            return (jnp.clip(at, 0, (last - first) * steps - 1), 0)

        return index

    token_spec = pl.BlockSpec((tokens, tall), lambda t, s, place: (0, ((place[0] + t) % 4) * steps + s))
    whole = pl.BlockSpec((tokens, columns), lambda t, s, place: (0, 0))
    y_specs = [pl.BlockSpec((tall, part), within(k, k + 1)) for k in range(4)]
    y_shapes = [jax.ShapeDtypeStruct((width // 4, part), BF16)] * 4
    spans = ((0, 4), (0, 2), (2, 4)) if split else ((0, 4), (0, 4))
    x_specs = [pl.BlockSpec((tall // 2, part), within(*span)) for span in spans]
    x_shapes = [jax.ShapeDtypeStruct((width // 8 * (b - a), part), BF16) for a, b in spans]
    return pl.pallas_call(
        functools.partial(product_kernel, split, rows),
        grid_spec=pltpu.PrefetchScalarGridSpec(
            num_scalar_prefetch=1,
            grid=(4, steps),
            in_specs=[token_spec, token_spec, whole, whole],
            out_specs=y_specs + x_specs,
        ),
        out_shape=y_shapes + x_shapes,
        compiler_params=pltpu.CompilerParams(vmem_limit_bytes=24 << 20),
        cost_estimate=pl.CostEstimate(
            flops=4 * tokens * width * columns, bytes_accessed=6 * tokens * width, transcendentals=0
        ),
        name="product",
    )(place, own, other, own_cot, other_cot)


def past_kernel(heads, lengths, query_ref, cache_ref, sum_ref, top_ref, mass_ref):
    span = cache_ref.shape[1]
    live = lax.broadcasted_iota(jnp.int32, (8, span), 1) < lengths[pl.program_id(0)]
    for j in range(heads):
        keys = cache_ref[0, :, 2 * j * HD : (2 * j + 1) * HD]
        values = cache_ref[0, :, (2 * j + 1) * HD : (2 * j + 2) * HD]
        scores = lax.dot_general(
            query_ref[0, j], keys, (((1,), (1,)), ((), ())), preferred_element_type=F32
        ) / math.sqrt(HD)
        scores = jnp.where(live, scores, jnp.float32(-1e30))
        top = jnp.max(scores, axis=1, keepdims=True)
        weights = jnp.exp(scores - top)
        mass = jnp.sum(weights, axis=1, keepdims=True)
        sum_ref[0, j] = jnp.dot(weights.astype(BF16), values, preferred_element_type=F32)
        top_ref[0, j] = jnp.broadcast_to(top, (8, HD))
        mass_ref[0, j] = jnp.broadcast_to(mass, (8, HD))


def attend_past(query, cache, lengths):
    rows, heads = query.shape[:2]
    span, columns = cache.shape[1:]
    small = pl.BlockSpec((1, heads, 8, HD), lambda r, lengths: (r, 0, 0, 0))
    shape = jax.ShapeDtypeStruct((rows, heads, 8, HD), F32)
    return pl.pallas_call(
        functools.partial(past_kernel, heads),
        grid_spec=pltpu.PrefetchScalarGridSpec(
            num_scalar_prefetch=1,
            grid=(rows,),
            in_specs=[small, pl.BlockSpec((1, span, columns), lambda r, lengths: (r, 0, 0))],
            out_specs=[small] * 3,
        ),
        out_shape=[shape] * 3,
        compiler_params=pltpu.CompilerParams(vmem_limit_bytes=16 << 20),
        cost_estimate=pl.CostEstimate(
            flops=32 * rows * span * columns,
            bytes_accessed=2 * rows * span * columns,
            transcendentals=8 * rows * heads * span,
        ),
        name="past",
    )(lengths, query, cache)


def finish_kernel(factor, rows, weight_ref, query_ref, sum_ref, top_ref, mass_ref, *refs):
    parts, (weight_out, attention_out) = refs[:-2], refs[-2:]
    total = parts[0][...].astype(F32)
    for ref in parts[1:]:
        total += ref[...].astype(F32)
    weight_out[...] = (weight_ref[...].astype(F32) - factor * total[:rows]).astype(BF16)
    fresh = total[rows:].astype(BF16).astype(F32)
    for r in range(query_ref.shape[0]):
        for j in range(query_ref.shape[1]):
            key = fresh[r : r + 1, 2 * j * HD : (2 * j + 1) * HD]
            value = fresh[r : r + 1, (2 * j + 1) * HD : (2 * j + 2) * HD]
            newest = jnp.sum(query_ref[r, j].astype(F32) * key, axis=1, keepdims=True) / math.sqrt(HD)
            old = top_ref[r, j]
            top = jnp.maximum(old, newest)
            past = jnp.exp(old - top)
            new = jnp.exp(newest - top)
            mixed = (sum_ref[r, j] * past + new * value) / (mass_ref[r, j] * past + new)
            attention_out[r, j] = mixed.astype(BF16)


def local(tokens_in, cotangent, weight, hidden_rows, queries, cache, lengths):
    y, z, xh, xl, c = (lax.axis_index(name) for name in ("y", "z", "xh", "xl", "c"))
    ny, nz, nh, nl, nc = (lax.axis_size(name) for name in ("y", "z", "xh", "xl", "c"))
    x = xh * nl + xl
    nx = nh * nl
    tokens, width = tokens_in.shape
    columns = cotangent.shape[1]
    part = columns // 2
    rows = weight.shape[0]
    factor = 0.01 / math.sqrt(tokens * nc * nl * nh * ny * nz)

    other_tokens = swap(tokens_in, "c", nc, 1)
    blocks = cotangent.reshape(nl, nc, tokens, columns)
    mine = pick(blocks, xl)
    got = swap(pick(blocks, 1 - xl), "xl", nl, 1)
    cots = [(pick(block, c), pick(block, 1 - c)) for block in (mine, got)]

    near_half = pick(hidden_rows.reshape(-1, nc, width // nc), c, 1)
    for axis, size, bits in (("z", nz, 1), ("z", nz, 2), ("z", nz, 4), ("y", ny, 1), ("y", ny, 2), ("xh", nh, 1)):
        near_half = jnp.concatenate([near_half, swap(near_half, axis, size, bits)], axis=0)
    far_half = swap(near_half, "c", nc, 1)
    hidden = jnp.concatenate(
        [jnp.where(c == 0, near_half, far_half), jnp.where(c == 0, far_half, near_half)], axis=1
    )

    place = jnp.stack([y, xh]).astype(jnp.int32)
    own = product(True, rows, place, tokens_in, other_tokens, *cots[0])
    place = jnp.stack([y, jnp.where(xl == 0, xh, 1 - xh)]).astype(jnp.int32)
    oth = product(False, rows, place, tokens_in, other_tokens, *cots[1])
    own_y, (own_x0, own_x2a, own_x2b) = own[:4], own[4:]
    oth_y, (oth_x1, oth_x3) = oth[:4], oth[4:]

    up = shift(own_y[2], "y", ny, 1)
    down = shift(own_y[3], "y", ny, -1)
    far = shift(oth_y[2], "y", ny, -1)
    ups = shift(jnp.stack([add(own_y[1], up), oth_y[1]]), "y", ny, 1)
    downs = shift(add(oth_y[3], far), "y", ny, -1)
    after_y = (
        (own_y[0].astype(F32) + ups[0].astype(F32) + down.astype(F32)).astype(BF16),
        (oth_y[0].astype(F32) + ups[1].astype(F32) + downs.astype(F32)).astype(BF16),
    )
    after_y = [a.reshape(nz, nh, rows, part) for a in after_y]

    half = own_x2a.shape[0]
    up = shift(own_x2a, X, nx, 1)
    down = shift(own_x2b, X, nx, -1)
    ups = shift(jnp.concatenate([add(oth_x1[:half], up), oth_x1[half:]]), X, nx, 1)
    downs = shift(jnp.concatenate([oth_x3[:half], add(oth_x3[half:], down)]), X, nx, -1)
    after_x = (own_x0.astype(F32) + ups.astype(F32) + downs.astype(F32)).astype(BF16)
    after_x = after_x.reshape(ny, nz, rows, part)

    def to_x(k):
        return pick(after_y[k % 2], ((x + k) % nx) // nl, 1)

    first = to_x(0).astype(F32)
    second = after_x[0].astype(F32)
    for k in (2, 1, 3):
        first += shift(to_x(k), X, nx, k).astype(F32)
        second += shift(after_x[k], "y", ny, k).astype(F32)
    both = jnp.concatenate([first.astype(BF16), second.astype(BF16)], axis=2)

    def scores(values):
        return lax.dot_general(
            hidden, values, (((1,), (1,)), ((), ())), preferred_element_type=F32
        ).astype(BF16)

    near_scores, far_scores = scores(tokens_in), scores(other_tokens)

    def share(pair):
        return -factor * (
            jnp.dot(near_scores, pair[0], preferred_element_type=F32)
            + jnp.dot(far_scores, pair[1], preferred_element_type=F32)
        )

    at = ((y * nz + z) * nh + xh) * rows
    old = jnp.dot(
        lax.dynamic_slice_in_dim(hidden, at, rows, 1), weight, preferred_element_type=F32
    )
    fresh = share(cots[0]) + old
    fresh = fresh + swap(share(cots[1]).astype(BF16), "xl", nl, 1).astype(F32)
    for axis, size, bits in (("xh", nh, 1), ("y", ny, 2), ("y", ny, 1)):
        split = fresh.shape[0] // 2
        fresh = fresh[:split] + swap(fresh[split:].astype(BF16), axis, size, bits).astype(F32)
    fresh = fresh.astype(BF16).reshape(nz, -1, columns)

    joined = [jnp.concatenate([pick(both, z ^ k), fresh[k]], axis=0) for k in range(nz)]
    parts = joined[:1] + [swap(joined[k], "z", nz, k) for k in range(1, nz)]

    heads = KVH // (nl * nc)
    count = queries.shape[0]
    query = queries.reshape(count, heads, -1, HD)
    group = query.shape[2]
    query = jnp.pad(query, ((0, 0), (0, 0), (0, 8 - group), (0, 0)))
    past = attend_past(query, cache, lengths)
    new_weight, attention = pl.pallas_call(
        functools.partial(finish_kernel, factor, rows),
        in_specs=[VMEM] * (5 + nz),
        out_specs=[VMEM] * 2,
        out_shape=[
            jax.ShapeDtypeStruct(weight.shape, BF16),
            jax.ShapeDtypeStruct(query.shape, BF16),
        ],
        name="finish",
    )(weight, query, *past, *parts)
    return (new_weight, attention[:, :, :group].reshape(count, -1))


def solution(mesh):
    names = ("y", "z", "xh", "xl", "c")
    fine = Mesh(np.asarray(mesh.devices).reshape(4, 8, 2, 2, 2), names)
    fsdp, tp = names[:3], names[3:]
    in_specs = (
        P(names, None),
        P(fsdp, tp),
        P(fsdp, tp),
        P(fsdp, None),
        P(fsdp, tp),
        P(fsdp, None, tp),
        P(fsdp),
    )
    out_specs = (P(fsdp, tp), P(fsdp, tp))
    return jax.shard_map(local, mesh=fine, in_specs=in_specs, out_specs=out_specs, check_vma=False)
```

time: 703 us -> 221 us (0.31)
  waiting for transfers between devices: 657 us -> 101 us
  starting transfers between devices: 0.12 us -> 64.5 us
  Pallas kernels: 0 us -> 25.4 us
  matrix products: 21.9 us -> 6.65 us
  between operations: 13.8 us -> 1.27 us
  local copies, waits for them, and re-layouts: 7.03 us -> 14.5 us
    reduce_scatter x1 -> x0, waiting for transfers between devices: 388 us -> none  [local(): lax.psum_scatter(lax.dot_general(gathered, cotangent, (((0,), (0,)), ((),...]
    all_gather x2 -> x0, waiting for transfers between devices: 269 us -> none  [the longest x1 148 us: local(): gathered = lax.all_gather(tokens_in, 'tp', axis=0, tiled=True)]
    ppermute x0 -> x35, waiting for transfers between devices: none -> 101 us  [the longest x20 59 us: swap(): return lax.ppermute(value, axis, [(i, i ^ bits) for i in range(size)])]
    ppermute x0 -> x35, starting transfers between devices: none -> 64.5 us  [the longest x20 42.5 us: swap(): return lax.ppermute(value, axis, [(i, i ^ bits) for i in range(size)])]
    pallas_call x0 -> x4, Pallas kernels: none -> 25.4 us  [the longest x2 20.1 us: product(): pl.pallas_call(functools.partial(product_kernel, split, rows), grid_spec=...]
    dot_general x5 -> x7, matrix products: 21.9 us -> 6.65 us  [the longest x2 5.18 us: scores(): lax.dot_general(hidden, values, (((1,), (1,)), ((), ())), preferred_eleme...]
  transfers between devices with their start and end apart: 3 -> 35, of which waited for: 3 -> 19; matrix products, arithmetic and copies ran while one was open for 1% -> 7% of each run, Pallas kernels for 0% -> 11%
where the time goes in v1:
time: 221 us; the launch traced here: 219 us
  waiting for transfers between devices  101 us (46%)
  starting transfers between devices  64.5 us (29%)
  Pallas kernels  25.4 us (11%)
  local copies, waits for them, and re-layouts  14.5 us (7%)
  matrix products  6.65 us (3%)
  other arithmetic  5.21 us (2%)
    ppermute x20, waiting for transfers between devices, swap(): return lax.ppermute(value, axis, [(i, i ^ bits) for i in range(size)])  59 us
    ppermute x20, starting transfers between devices, swap(): return lax.ppermute(value, axis, [(i, i ^ bits) for i in range(size)])  42.5 us
    ppermute x15, waiting for transfers between devices, shift(): lax.ppermute(value, axis, [(i, (i + by) % size) for i in range(size)])  42.3 us
    ppermute x15, starting transfers between devices, shift(): lax.ppermute(value, axis, [(i, (i + by) % size) for i in range(size)])  22 us
    pallas_call x2, Pallas kernels, product(): pl.pallas_call(functools.partial(product_kernel, split, rows), grid_spec=...  20.1 us
    dot_general x2, matrix products, scores(): lax.dot_general(hidden, values, (((1,), (1,)), ((), ())), preferred_eleme...  5.18 us
    unnamed x42, local copies, waits for them, and re-layouts  4.96 us
    concatenate x3, local copies, waits for them, and re-layouts, local(): jnp.concatenate([near_half, swap(near_half, axis, size, bits)], axis=0)  4.6 us
  transfers between devices with their start and end apart: 35, of which 19 were waited for; matrix products, arithmetic and copies ran while one was open for 7% of the time, Pallas kernels for 11%

profile of v1, /device:TPU:2, one launch (start us, length us, event | category | flops | bytes accessed | tf_op | source)
XLA Modules:
  0.0 218.8 jit_solution(1093741559597248745)
XLA Ops:
  0.6 0.8 copy-done
  1.4 2.0 collective-permute-start.17
  3.4 1.9 collective-permute-done.17
  5.3 3.4 %collective-permute-start.18 = (bf16[8,2560]{1,0:T(8,128)(2,1)S(1)}, bf16[8,2560]{1,0:T(8,128)(2,1)S(1)}, u32[]{:S(2)}, u32[]{:S(2)}) collective-permute-start(bf16[8,2560]{1,0:T(8,128)(2,1)S(1)} %pad_maximum_fusion.20), channel_id=1, source_target_pairs={{0,16},{8,24},{16,0},{24,8},{32,48},{40,56},{48,32},{56,40},{1,17}... | collective-permute-start | bytes 122888 | tf_op jit(solution)/shard_map/ppermute | solution.py:26
  8.7 2.0 collective-permute-done.18
  10.7 7.0 %collective-permute-start.19 = (bf16[16,2560]{1,0:T(8,128)(2,1)S(1)}, bf16[16,2560]{1,0:T(8,128)(2,1)S(1)}, u32[]{:S(2)}, u32[]{:S(2)}) collective-permute-start(bf16[16,2560]{1,0:T(8,128)(2,1)S(1)} %pad_maximum_fusion.19), channel_id=1, source_target_pairs={{0,32},{8,40},{16,48},{24,56},{32,0},{40,8},{48,16},{56,24},{1,33}... | collective-permute-start | bytes 245768 | tf_op jit(solution)/shard_map/ppermute | solution.py:26
  17.7 2.5 %collective-permute-done.19 = bf16[16,2560]{1,0:T(8,128)(2,1)S(1)} collective-permute-done((bf16[16,2560]{1,0:T(8,128)(2,1)S(1)}, bf16[16,2560]{1,0:T(8,128)(2,1)S(1)}, u32[]{:S(2)}, u32[]{:S(2)}) %collective-permute-start.19) | collective-permute-done | bytes 81952 | tf_op jit(solution)/shard_map/ppermute | solution.py:26
  20.3 1.7 collective-permute-start.20
  22.0 3.7 %collective-permute-done.20 = bf16[32,2560]{1,0:T(8,128)(2,1)S(1)} collective-permute-done((bf16[32,2560]{1,0:T(8,128)(2,1)S(1)}, bf16[32,2560]{1,0:T(8,128)(2,1)S(1)}, u32[]{:S(2)}, u32[]{:S(2)}) %collective-permute-start.20) | collective-permute-done | bytes 163872 | tf_op jit(solution)/shard_map/ppermute | solution.py:26
  25.8 4.4 %collective-permute-start.21 = (bf16[64,2560]{1,0:T(8,128)(2,1)S(1)}, bf16[64,2560]{1,0:T(8,128)(2,1)S(1)}, u32[]{:S(2)}, u32[]{:S(2)}) collective-permute-start(bf16[64,2560]{1,0:T(8,128)(2,1)S(1)} %concatenate.65), channel_id=1, source_target_pairs={{0,128},{64,192},{128,0},{192,64},{1,129},{65,193},{129,1},{193,65... | collective-permute-start | bytes 983048 | tf_op jit(solution)/shard_map/ppermute | solution.py:26
  30.2 5.1 %collective-permute-done.21 = bf16[64,2560]{1,0:T(8,128)(2,1)S(1)} collective-permute-done((bf16[64,2560]{1,0:T(8,128)(2,1)S(1)}, bf16[64,2560]{1,0:T(8,128)(2,1)S(1)}, u32[]{:S(2)}, u32[]{:S(2)}) %collective-permute-start.21) | collective-permute-done | bytes 327712 | tf_op jit(solution)/shard_map/ppermute | solution.py:26
  35.8 2.2 %collective-permute-start.22 = (bf16[128,2560]{1,0:T(8,128)(2,1)S(1)}, bf16[128,2560]{1,0:T(8,128)(2,1)}, u32[]{:S(2)}, u32[]{:S(2)}) collective-permute-start(bf16[128,2560]{1,0:T(8,128)(2,1)S(1)} %concatenate.66), channel_id=1, source_target_pairs={{0,4},{4,0},{1,5},{5,1},{2,6},{6,2},{3,7},{7,3},{8,12},{12,8},{9,1... | collective-permute-start | bytes 1966088 | tf_op jit(solution)/shard_map/ppermute | solution.py:26
  38.0 12.3 %collective-permute-done.22 = bf16[128,2560]{1,0:T(8,128)(2,1)} collective-permute-done((bf16[128,2560]{1,0:T(8,128)(2,1)S(1)}, bf16[128,2560]{1,0:T(8,128)(2,1)}, u32[]{:S(2)}, u32[]{:S(2)}) %collective-permute-start.22) | collective-permute-done | bytes 655392 | tf_op jit(solution)/shard_map/ppermute | solution.py:26
  50.3 4.0 %concatenate.67 = bf16[256,2560]{1,0:T(8,128)(2,1)S(1)} concatenate(bf16[4,2560]{1,0:T(4,128)(2,1)} %copy-done.10, bf16[4,2560]{1,0:T(4,128)(2,1)} %copy-done.11, bf16[8,2560]{1,0:T(8,128)(2,1)S(1)} %collective-permute-done.18, bf16[16,2560]{1,0:T(8,128)(2,1)S(1)} %collective-permute-done.19, bf16[32,2560]{1,0:T(8,128)(2,1)S(1)} %collective-permute-done.20, ...), dimensions={0} | concatenate | bytes 2621440 | tf_op jit(solution)/shard_map/concatenate | solution.py:195
  54.5 0.9 dynamic-slice_bitcast_fusion
  55.9 1.2 dynamic-slice_bitcast_fusion.3
  57.1 18.5 %collective-permute-done.2 = bf16[2,384,512]{2,1,0:T(8,128)(2,1)} collective-permute-done((bf16[2,384,512]{2,1,0:T(8,128)(2,1)}, bf16[2,384,512]{2,1,0:T(8,128)(2,1)}, u32[]{:S(2)}, u32[]{:S(2)}) %collective-permute-start.2) | collective-permute-done | bytes 786464 | tf_op jit(solution)/shard_map/ppermute | solution.py:26
  75.6 1.2 dynamic-slice_bitcast_fusion.2
  76.8 1.6 broadcast_select_fusion.1
  78.5 0.8 copy-done.7
  79.3 1.5 fusion.10
  81.2 3.6 %fusion.11 = bf16[256,384]{1,0:T(8,128)(2,1)S(1)} fusion(bf16[384,5120]{1,0:T(8,128)(2,1)} %collective-permute-done.b_ref, bf16[256,2560]{1,0:T(8,128)(2,1)S(1)} %get-tuple-element.39, bf16[256,2560]{1,0:T(8,128)(2,1)S(1)} %get-tuple-element.38), kind=kOutput, calls=%fused_computation.45 | convolution fusion | flops 1011974144 | bytes 6750208 | tf_op jit(solution)/shard_map/dot_general | solution.py:238
  85.4 0.6 collective-permute-start.24
  86.4 7.0 %collective-permute-done.24 = bf16[256,512]{1,0:T(8,128)(2,1)S(1)} collective-permute-done((bf16[256,512]{1,0:T(8,128)(2,1)S(1)}, bf16[256,512]{1,0:T(8,128)(2,1)S(1)}, u32[]{:S(2)}, u32[]{:S(2)}) %collective-permute-start.24) | collective-permute-done | bytes 262176 | tf_op jit(solution)/shard_map/ppermute | solution.py:26
  93.7 2.2 %collective-permute-start.25 = (bf16[128,512]{1,0:T(8,128)(2,1)S(1)}, bf16[128,512]{1,0:T(8,128)(2,1)S(1)}, u32[]{:S(2)}, u32[]{:S(2)}) collective-permute-start(bf16[128,512]{1,0:T(8,128)(2,1)S(1)} %slice.151), channel_id=1, source_target_pairs={{0,4},{4,0},{1,5},{5,1},{2,6},{6,2},{3,7},{7,3},{8,12},{12,8},{9,1... | collective-permute-start | bytes 393224 | tf_op jit(solution)/shard_map/ppermute | solution.py:26
  96.2 2.2 copy-done.1
  98.3 3.3 %past.1 = (f32[4,2,8,128]{3,2,1,0:T(8,128)S(1)}, f32[4,2,8,128]{3,2,1,0:T(8,128)S(1)}, f32[4,2,8,128]{3,2,1,0:T(8,128)S(1)}) custom-call(s32[4]{0:T(128)S(1)} %copy-done.6, bf16[4,2,8,128]{3,2,1,0:T(8,128)(2,1)S(1)} %pad.4.query_ref, bf16[4,1024,512]{2,1,0:T(8,128)(2,1)S(1)} %copy-done.1), custom_call_target="tpu_custom_call" | custom-call | flops 67108864 | bytes 4194304 | tf_op jit(solution)/shard_map/past/pallas_call | solution.py:137
  102.3 1.5 collective-permute-start.26
  103.9 10.1 %product.2 = (bf16[1280,256]{1,0:T(8,128)(2,1)S(1)}, bf16[1280,256]{1,0:T(8,128)(2,1)S(1)}, bf16[1280,256]{1,0:T(8,128)(2,1)S(1)}, bf16[1280,256]{1,0:T(8,128)(2...) custom-call(s32[2]{0:T(128)S(1)} %pad_add_fusion.place, ...), custom_call_target="tpu_custom_call" | custom-call | flops 4026531840 | bytes 11796480 | tf_op jit(solution)/shard_map/product/pallas_call | solution.py:97
  114.0 1.5 collective-permute-start.12
  115.5 0.8 collective-permute-start.27
  116.3 10.0 %product.3 = (bf16[1280,256]{1,0:T(8,128)(2,1)S(1)}, bf16[1280,256]{1,0:T(8,128)(2,1)S(1)}, bf16[1280,256]{1,0:T(8,128)(2,1)S(1)}, bf16[1280,256]{1,0:T(8,128)(2...) custom-call(s32[2]{0:T(128)S(1)} %pad_add_fusion.1.place, bf16[384,5120]{1,0:T(8,128)(2,1)S(1)} %copy-done.8, ...), custom_call_target="tpu_custom_call" | custom-call | flops 4026531840 | bytes 11796480 | tf_op jit(solution)/shard_map/product/pallas_call | solution.py:97
  126.4 0.7 collective-permute-start.10
  127.1 1.8 collective-permute-start.4
  129.1 3.0 %collective-permute-start.6 = (bf16[1280,256]{1,0:T(8,128)(2,1)S(1)}, bf16[1280,256]{1,0:T(8,128)(2,1)S(1)}, u32[]{:S(2)}, u32[]{:S(2)}) collective-permute-start(bf16[1280,256]{1,0:T(8,128)(2,1)S(1)} %get-tuple-element.30), channel_id=1, source_target_pairs={{0,192},{64,0},{128,64},{192,128},{1,193},{65,1},{129,65},{193,129... | collective-permute-start | bytes 1966088 | tf_op jit(solution)/shard_map/ppermute | solution.py:22
  132.5 1.5 collective-permute-start.13
  134.0 6.8 %collective-permute-done.10 = bf16[1280,256]{1,0:T(8,128)(2,1)S(1)} collective-permute-done((bf16[1280,256]{1,0:T(8,128)(2,1)S(1)}, bf16[1280,256]{1,0:T(8,128)(2,1)S(1)}, u32[]{:S(2)}, u32[]{:S(2)}) %collective-permute-start.10) | collective-permute-done | bytes 655392 | tf_op jit(solution)/shard_map/ppermute | solution.py:22
  141.1 0.9 collective-permute-start.11
  142.0 1.9 collective-permute-done.1
  144.3 11.5 %collective-permute-done.6 = bf16[1280,256]{1,0:T(8,128)(2,1)S(1)} collective-permute-done((bf16[1280,256]{1,0:T(8,128)(2,1)S(1)}, bf16[1280,256]{1,0:T(8,128)(2,1)S(1)}, u32[]{:S(2)}, u32[]{:S(2)}) %collective-permute-start.6) | collective-permute-done | bytes 655392 | tf_op jit(solution)/shard_map/ppermute | solution.py:22
  156.0 2.5 %collective-permute-start.7 = (bf16[1280,256]{1,0:T(8,128)(2,1)S(1)}, bf16[1280,256]{1,0:T(8,128)(2,1)S(1)}, u32[]{:S(2)}, u32[]{:S(2)}) collective-permute-start(bf16[1280,256]{1,0:T(8,128)(2,1)S(1)} %add_convert_fusion.3), channel_id=1, source_target_pairs={{0,192},{64,0},{128,64},{192,128},{1,193},{65,1},{129,65},{193,129... | collective-permute-start | bytes 1966088 | tf_op jit(solution)/shard_map/ppermute | solution.py:22
  158.5 1.3 collective-permute-done.13
  159.8 9.4 %collective-permute-done.11 = bf16[2560,256]{1,0:T(8,128)(2,1)S(1)} collective-permute-done((bf16[2560,256]{1,0:T(8,128)(2,1)S(1)}, bf16[2560,256]{1,0:T(8,128)(2,1)S(1)}, u32[]{:S(2)}, u32[]{:S(2)}) %collective-permute-start.11) | collective-permute-done | bytes 1310752 | tf_op jit(solution)/shard_map/ppermute | solution.py:22
  169.3 0.5 add_convert_fusion
  169.9 1.9 collective-permute-start.16
  172.0 2.0 collective-permute-start.14
  174.0 0.5 fusion.5
  174.6 3.0 %collective-permute-start.9 = (bf16[8,80,256]{2,1,0:T(8,128)(2,1)S(1)}, bf16[8,80,256]{2,1,0:T(8,128)(2,1)S(1)}, u32[]{:S(2)}, u32[]{:S(2)}) collective-permute-start(bf16[8,80,256]{2,1,0:T(8,128)(2,1)S(1)} %get-tuple-element.59), channel_id=1, source_target_pairs={{0,6},{2,0},{4,2},{6,4},{1,7},{3,1},{5,3},{7,5},{8,14},{10,8},{12,... | collective-permute-start | bytes 983048 | tf_op jit(solution)/shard_map/ppermute | solution.py:22
  177.6 5.6 %collective-permute-done.16 = bf16[8,80,256]{2,1,0:T(8,128)(2,1)S(1)} collective-permute-done((bf16[8,80,256]{2,1,0:T(8,128)(2,1)S(1)}, bf16[8,80,256]{2,1,0:T(8,128)(2,1)S(1)}, u32[]{:S(2)}, u32[]{:S(2)}) %collective-permute-start.16) | collective-permute-done | bytes 327712 | tf_op jit(solution)/shard_map/ppermute | solution.py:22
  183.2 2.6 %collective-permute-start.5 = (bf16[8,80,256]{2,1,0:T(8,128)(2,1)S(1)}, bf16[8,80,256]{2,1,0:T(8,128)(2,1)S(1)}, u32[]{:S(2)}, u32[]{:S(2)}) collective-permute-start(bf16[8,80,256]{2,1,0:T(8,128)(2,1)S(1)} %dynamic-slice_bitcast_fusion.7), channel_id=1, source_target_pairs={{0,4},{2,6},{4,0},{6,2},{1,5},{3,7},{5,1},{7,3},{8,12},{10,14},{12... | collective-permute-start | bytes 983048 | tf_op jit(solution)/shard_map/ppermute | solution.py:22
  185.8 0.6 collective-permute-done.15
  186.6 5.2 %collective-permute-done.5 = bf16[8,80,256]{2,1,0:T(8,128)(2,1)S(1)} collective-permute-done((bf16[8,80,256]{2,1,0:T(8,128)(2,1)S(1)}, bf16[8,80,256]{2,1,0:T(8,128)(2,1)S(1)}, u32[]{:S(2)}, u32[]{:S(2)}) %collective-permute-start.5) | collective-permute-done | bytes 327712 | tf_op jit(solution)/shard_map/ppermute | solution.py:22
  192.0 1.4 collective-permute-start.28
  193.4 3.0 %collective-permute-start.29 = (bf16[84,512]{1,0:T(8,128)(2,1)S(1)}, bf16[84,512]{1,0:T(8,128)(2,1)S(1)}, u32[]{:S(2)}, u32[]{:S(2)}) collective-permute-start(bf16[84,512]{1,0:T(8,128)(2,1)S(1)} %pad_maximum_fusion.13), channel_id=1, source_target_pairs={{0,16},{8,24},{16,0},{24,8},{32,48},{40,56},{48,32},{56,40},{1,17}... | collective-permute-start | bytes 258056 | tf_op jit(solution)/shard_map/ppermute | solution.py:26
  196.7 6.2 %collective-permute-start.31 = (bf16[84,512]{1,0:T(8,128)(2,1)S(1)}, bf16[84,512]{1,0:T(8,128)(2,1)S(1)}, u32[]{:S(2)}, u32[]{:S(2)}) collective-permute-start(bf16[84,512]{1,0:T(8,128)(2,1)S(1)} %pad_maximum_fusion.15), channel_id=1, source_target_pairs={{0,32},{8,40},{16,48},{24,56},{32,0},{40,8},{48,16},{56,24},{1,33}... | collective-permute-start | bytes 258056 | tf_op jit(solution)/shard_map/ppermute | solution.py:26
  203.2 4.2 %collective-permute-start.33 = (bf16[84,512]{1,0:T(8,128)(2,1)S(1)}, bf16[84,512]{1,0:T(8,128)(2,1)S(1)}, u32[]{:S(2)}, u32[]{:S(2)}) collective-permute-start(bf16[84,512]{1,0:T(8,128)(2,1)S(1)} %pad_maximum_fusion.17), channel_id=1, source_target_pairs={{0,48},{8,56},{16,32},{24,40},{32,16},{40,24},{48,0},{56,8},{1,49}... | collective-permute-start | bytes 258056 | tf_op jit(solution)/shard_map/ppermute | solution.py:26
  207.4 0.8 collective-permute-start.34
  208.2 0.6 pad_maximum_fusion.11.refs_0_
  208.9 2.1 collective-permute-done.32.refs_5_
  211.0 0.9 collective-permute-done.33.refs_6_
  211.9 2.9 %collective-permute-done.34.refs_7_ = bf16[84,512]{1,0:T(8,128)(2,1)S(1)} collective-permute-done((bf16[84,512]{1,0:T(8,128)(2,1)S(1)}, bf16[84,512]{1,0:T(8,128)(2,1)S(1)}, u32[]{:S(2)}, u32[]{:S(2)}) %collective-permute-start.34) | collective-permute-done | bytes 86048 | tf_op jit(solution)/shard_map/ppermute | solution.py:26
  214.9 0.6 copy-done.19
  215.4 2.0 finish.1
  217.5 1.3 reshape.65
  (108 shorter events, 6.4 us)
Async XLA Ops:
  0.6 0.8 copy-start
  1.4 33.9 %copy-start.10 = (bf16[4,2560]{1,0:T(4,128)(2,1)}, bf16[4,2560]{1,0:T(4,128)(2,1)S(1)}, u32[]{:S(2)}) copy-start(bf16[4,2560]{1,0:T(4,128)(2,1)S(1)} %dynamic-slice_bitcast_fusion.8) | copy-start | bytes 61444
  1.4 3.9 %collective-permute-start.17 = (bf16[4,2560]{1,0:T(4,128)(2,1)S(1)}, bf16[4,2560]{1,0:T(4,128)(2,1)S(1)}, u32[]{:S(2)}, u32[]{:S(2)}) collective-permute-start(bf16[4,2560]{1,0:T(4,128)(2,1)S(1)} %dynamic-slice_bitcast_fusion.8), channel_id=1, source_target_pairs={{0,8},{8,0},{16,24},{24,16},{32,40},{40,32},{48,56},{56,48},{1,9},... | collective-permute-start | bytes 61448 | tf_op jit(solution)/shard_map/ppermute | solution.py:26
  5.3 30.0 %copy-start.11 = (bf16[4,2560]{1,0:T(4,128)(2,1)}, bf16[4,2560]{1,0:T(4,128)(2,1)S(1)}, u32[]{:S(2)}) copy-start(bf16[4,2560]{1,0:T(4,128)(2,1)S(1)} %collective-permute-done.17) | copy-start | bytes 61444
  5.3 5.3 %collective-permute-start.18 = (bf16[8,2560]{1,0:T(8,128)(2,1)S(1)}, bf16[8,2560]{1,0:T(8,128)(2,1)S(1)}, u32[]{:S(2)}, u32[]{:S(2)}) collective-permute-start(bf16[8,2560]{1,0:T(8,128)(2,1)S(1)} %pad_maximum_fusion.20), channel_id=1, source_target_pairs={{0,16},{8,24},{16,0},{24,8},{32,48},{40,56},{48,32},{56,40},{1,17}... | collective-permute-start | bytes 122888 | tf_op jit(solution)/shard_map/ppermute | solution.py:26
  10.7 9.5 %collective-permute-start.19 = (bf16[16,2560]{1,0:T(8,128)(2,1)S(1)}, bf16[16,2560]{1,0:T(8,128)(2,1)S(1)}, u32[]{:S(2)}, u32[]{:S(2)}) collective-permute-start(bf16[16,2560]{1,0:T(8,128)(2,1)S(1)} %pad_maximum_fusion.19), channel_id=1, source_target_pairs={{0,32},{8,40},{16,48},{24,56},{32,0},{40,8},{48,16},{56,24},{1,33}... | collective-permute-start | bytes 245768 | tf_op jit(solution)/shard_map/ppermute | solution.py:26
  20.3 5.4 %collective-permute-start.20 = (bf16[32,2560]{1,0:T(8,128)(2,1)S(1)}, bf16[32,2560]{1,0:T(8,128)(2,1)S(1)}, u32[]{:S(2)}, u32[]{:S(2)}) collective-permute-start(bf16[32,2560]{1,0:T(8,128)(2,1)S(1)} %pad_maximum_fusion.10), channel_id=1, source_target_pairs={{0,64},{64,0},{128,192},{192,128},{1,65},{65,1},{129,193},{193,129... | collective-permute-start | bytes 491528 | tf_op jit(solution)/shard_map/ppermute | solution.py:26
  22.0 59.2 %collective-permute-start = (bf16[384,5120]{1,0:T(8,128)(2,1)}, bf16[384,5120]{1,0:T(8,128)(2,1)}, u32[]{:S(2)}, u32[]{:S(2)}) collective-permute-start(bf16[384,5120]{1,0:T(8,128)(2,1)} %a_ref.3), channel_id=1, source_target_pairs={{0,1},{1,0},{2,3},{3,2},{4,5},{5,4},{6,7},{7,6},{8,9},{9,8},{10,11... | collective-permute-start | bytes 11796488 | tf_op jit(solution)/shard_map/ppermute | solution.py:26
  25.8 9.4 %collective-permute-start.21 = (bf16[64,2560]{1,0:T(8,128)(2,1)S(1)}, bf16[64,2560]{1,0:T(8,128)(2,1)S(1)}, u32[]{:S(2)}, u32[]{:S(2)}) collective-permute-start(bf16[64,2560]{1,0:T(8,128)(2,1)S(1)} %concatenate.65), channel_id=1, source_target_pairs={{0,128},{64,192},{128,0},{192,64},{1,129},{65,193},{129,1},{193,65... | collective-permute-start | bytes 983048 | tf_op jit(solution)/shard_map/ppermute | solution.py:26
  35.8 18.7 %copy-start.9 = (bf16[1536,512]{1,0:T(8,128)(2,1)S(1)}, bf16[1536,512]{1,0:T(8,128)(2,1)}, u32[]{:S(2)}) copy-start(bf16[1536,512]{1,0:T(8,128)(2,1)} %param.8) | copy-start | bytes 4718596
  35.8 14.6 %collective-permute-start.22 = (bf16[128,2560]{1,0:T(8,128)(2,1)S(1)}, bf16[128,2560]{1,0:T(8,128)(2,1)}, u32[]{:S(2)}, u32[]{:S(2)}) collective-permute-start(bf16[128,2560]{1,0:T(8,128)(2,1)S(1)} %concatenate.66), channel_id=1, source_target_pairs={{0,4},{4,0},{1,5},{5,1},{2,6},{6,2},{3,7},{7,3},{8,12},{12,8},{9,1... | collective-permute-start | bytes 1966088 | tf_op jit(solution)/shard_map/ppermute | solution.py:26
  54.3 22.5 %collective-permute-start.23 = (bf16[256,2560]{1,0:T(8,128)(2,1)S(1)}, bf16[256,2560]{1,0:T(8,128)(2,1)}, u32[]{:S(2)}, u32[]{:S(2)}) collective-permute-start(bf16[256,2560]{1,0:T(8,128)(2,1)S(1)} %concatenate.67), channel_id=1, source_target_pairs={{0,1},{1,0},{2,3},{3,2},{4,5},{5,4},{6,7},{7,6},{8,9},{9,8},{10,11... | collective-permute-start | bytes 3932168 | tf_op jit(solution)/shard_map/ppermute | solution.py:26
  55.4 20.2 %collective-permute-start.2 = (bf16[2,384,512]{2,1,0:T(8,128)(2,1)}, bf16[2,384,512]{2,1,0:T(8,128)(2,1)}, u32[]{:S(2)}, u32[]{:S(2)}) collective-permute-start(bf16[2,384,512]{2,1,0:T(8,128)(2,1)} %dynamic-slice_bitcast_fusion), channel_id=1, source_target_pairs={{0,2},{2,0},{1,3},{3,1},{4,6},{6,4},{5,7},{7,5},{8,10},{10,8},{9,1... | collective-permute-start | bytes 2359304 | tf_op jit(solution)/shard_map/ppermute | solution.py:26
  76.8 2.5 %copy-start.7 = (bf16[384,5120]{1,0:T(8,128)(2,1)S(1)}, bf16[384,5120]{1,0:T(8,128)(2,1)}, u32[]{:S(2)}) copy-start(bf16[384,5120]{1,0:T(8,128)(2,1)} %a_ref.3) | copy-start | bytes 11796484
  85.1 8.3 %copy-start.12 = (bf16[80,512]{1,0:T(8,128)(2,1)S(1)}, bf16[80,512]{1,0:T(8,128)(2,1)}, u32[]{:S(2)}) copy-start(bf16[80,512]{1,0:T(8,128)(2,1)} %weight_ref.1) | copy-start | bytes 245764
  85.4 8.0 %collective-permute-start.24 = (bf16[256,512]{1,0:T(8,128)(2,1)S(1)}, bf16[256,512]{1,0:T(8,128)(2,1)S(1)}, u32[]{:S(2)}, u32[]{:S(2)}) collective-permute-start(bf16[256,512]{1,0:T(8,128)(2,1)S(1)} %fusion.9), channel_id=1, source_target_pairs={{0,2},{2,0},{1,3},{3,1},{4,6},{6,4},{5,7},{7,5},{8,10},{10,8},{9,1... | collective-permute-start | bytes 786440 | tf_op jit(solution)/shard_map/ppermute | solution.py:26
  86.3 9.7 %copy-start.20 = (bf16[4,1280]{1,0:T(4,128)(2,1)S(1)}, bf16[4,1280]{1,0:T(4,128)(2,1)}, u32[]{:S(2)}) copy-start(bf16[4,1280]{1,0:T(4,128)(2,1)} %param.11) | copy-start | bytes 30724
  86.4 9.8 %copy-start.6 = (s32[4]{0:T(128)S(1)}, s32[4]{0:T(128)}, u32[]{:S(2)}) copy-start(s32[4]{0:T(128)} %lengths.1) | copy-start | bytes 52
  93.7 8.0 %collective-permute-start.25 = (bf16[128,512]{1,0:T(8,128)(2,1)S(1)}, bf16[128,512]{1,0:T(8,128)(2,1)S(1)}, u32[]{:S(2)}, u32[]{:S(2)}) collective-permute-start(bf16[128,512]{1,0:T(8,128)(2,1)S(1)} %slice.151), channel_id=1, source_target_pairs={{0,4},{4,0},{1,5},{5,1},{2,6},{6,2},{3,7},{7,3},{8,12},{12,8},{9,1... | collective-permute-start | bytes 393224 | tf_op jit(solution)/shard_map/ppermute | solution.py:26
  96.1 5.6 %copy-start.2 = (bf16[4,2,8,128]{3,2,1,0:T(8,128)(2,1)}, bf16[4,2,8,128]{3,2,1,0:T(8,128)(2,1)S(1)}, u32[]{:S(2)}) copy-start(bf16[4,2,8,128]{3,2,1,0:T(8,128)(2,1)S(1)} %pad.4.query_ref) | copy-start | bytes 49156
  96.2 2.2 %copy-start.1 = (bf16[4,1024,512]{2,1,0:T(8,128)(2,1)S(1)}, bf16[4,1024,512]{2,1,0:T(8,128)(2,1)}, u32[]{:S(2)}) copy-start(bf16[4,1024,512]{2,1,0:T(8,128)(2,1)} %cache_ref.1) | copy-start | bytes 12582916
  98.3 5.5 %copy-start.8 = (bf16[384,5120]{1,0:T(8,128)(2,1)S(1)}, bf16[384,5120]{1,0:T(8,128)(2,1)}, u32[]{:S(2)}) copy-start(bf16[384,5120]{1,0:T(8,128)(2,1)} %a_ref.3) | copy-start | bytes 11796484
  101.7 0.6 copy-start.3
  101.7 0.6 copy-start.4
  101.7 0.6 copy-start.5
  102.3 13.1 %collective-permute-start.26 = (bf16[64,512]{1,0:T(8,128)(2,1)S(1)}, bf16[64,512]{1,0:T(8,128)(2,1)S(1)}, u32[]{:S(2)}, u32[]{:S(2)}) collective-permute-start(bf16[64,512]{1,0:T(8,128)(2,1)S(1)} %slice.152), channel_id=1, source_target_pairs={{0,128},{64,192},{128,0},{192,64},{1,129},{65,193},{129,1},{193,65... | collective-permute-start | bytes 196616 | tf_op jit(solution)/shard_map/ppermute | solution.py:26
  114.0 18.2 %collective-permute-start.12 = (bf16[1280,256]{1,0:T(8,128)(2,1)S(1)}, bf16[1280,256]{1,0:T(8,128)(2,1)S(1)}, u32[]{:S(2)}, u32[]{:S(2)}) collective-permute-start(bf16[1280,256]{1,0:T(8,128)(2,1)S(1)} %get-tuple-element.35), channel_id=1, source_target_pairs={{0,6},{2,0},{4,2},{6,4},{1,7},{3,1},{5,3},{7,5},{8,14},{10,8},{12,... | collective-permute-start | bytes 1966088 | tf_op jit(solution)/shard_map/ppermute | solution.py:22
  115.5 13.6 %collective-permute-start.27 = (bf16[32,512]{1,0:T(8,128)(2,1)S(1)}, bf16[32,512]{1,0:T(8,128)(2,1)S(1)}, u32[]{:S(2)}, u32[]{:S(2)}) collective-permute-start(bf16[32,512]{1,0:T(8,128)(2,1)S(1)} %slice.153), channel_id=1, source_target_pairs={{0,64},{64,0},{128,192},{192,128},{1,65},{65,1},{129,193},{193,129... | collective-permute-start | bytes 98312 | tf_op jit(solution)/shard_map/ppermute | solution.py:26
  126.4 14.4 %collective-permute-start.10 = (bf16[1280,256]{1,0:T(8,128)(2,1)S(1)}, bf16[1280,256]{1,0:T(8,128)(2,1)S(1)}, u32[]{:S(2)}, u32[]{:S(2)}) collective-permute-start(bf16[1280,256]{1,0:T(8,128)(2,1)S(1)} %get-tuple-element.33), channel_id=1, source_target_pairs={{0,2},{2,4},{4,6},{6,0},{1,3},{3,5},{5,7},{7,1},{8,10},{10,12},{12... | collective-permute-start | bytes 1966088 | tf_op jit(solution)/shard_map/ppermute | solution.py:22
  127.1 44.9 %collective-permute-start.4 = (bf16[1280,256]{1,0:T(8,128)(2,1)S(1)}, bf16[1280,256]{1,0:T(8,128)(2,1)S(1)}, u32[]{:S(2)}, u32[]{:S(2)}) collective-permute-start(bf16[1280,256]{1,0:T(8,128)(2,1)S(1)} %get-tuple-element.27), channel_id=1, source_target_pairs={{0,192},{64,0},{128,64},{192,128},{1,193},{65,1},{129,65},{193,129... | collective-permute-start | bytes 1966088 | tf_op jit(solution)/shard_map/ppermute | solution.py:22
  128.9 15.0 %collective-permute-start.1 = (bf16[1280,256]{1,0:T(8,128)(2,1)S(1)}, bf16[1280,256]{1,0:T(8,128)(2,1)S(1)}, u32[]{:S(2)}, u32[]{:S(2)}) collective-permute-start(bf16[1280,256]{1,0:T(8,128)(2,1)S(1)} %get-tuple-element.25), channel_id=1, source_target_pairs={{0,64},{64,128},{128,192},{192,0},{1,65},{65,129},{129,193},{193,1... | collective-permute-start | bytes 1966088 | tf_op jit(solution)/shard_map/ppermute | solution.py:22
  129.1 26.6 %collective-permute-start.6 = (bf16[1280,256]{1,0:T(8,128)(2,1)S(1)}, bf16[1280,256]{1,0:T(8,128)(2,1)S(1)}, u32[]{:S(2)}, u32[]{:S(2)}) collective-permute-start(bf16[1280,256]{1,0:T(8,128)(2,1)S(1)} %get-tuple-element.30), channel_id=1, source_target_pairs={{0,192},{64,0},{128,64},{192,128},{1,193},{65,1},{129,65},{193,129... | collective-permute-start | bytes 1966088 | tf_op jit(solution)/shard_map/ppermute | solution.py:22
  132.5 27.3 %collective-permute-start.13 = (bf16[2560,256]{1,0:T(8,128)(2,1)S(1)}, bf16[2560,256]{1,0:T(8,128)(2,1)S(1)}, u32[]{:S(2)}, u32[]{:S(2)}) collective-permute-start(bf16[2560,256]{1,0:T(8,128)(2,1)S(1)} %pad_maximum_fusion.5), channel_id=1, source_target_pairs={{0,6},{2,0},{4,2},{6,4},{1,7},{3,1},{5,3},{7,5},{8,14},{10,8},{12,... | collective-permute-start | bytes 3932168 | tf_op jit(solution)/shard_map/ppermute | solution.py:22
  141.1 28.1 %collective-permute-start.11 = (bf16[2560,256]{1,0:T(8,128)(2,1)S(1)}, bf16[2560,256]{1,0:T(8,128)(2,1)S(1)}, u32[]{:S(2)}, u32[]{:S(2)}) collective-permute-start(bf16[2560,256]{1,0:T(8,128)(2,1)S(1)} %pad_maximum_fusion.4), channel_id=1, source_target_pairs={{0,2},{2,4},{4,6},{6,0},{1,3},{3,5},{5,7},{7,1},{8,10},{10,12},{12... | collective-permute-start | bytes 3932168 | tf_op jit(solution)/shard_map/ppermute | solution.py:22
  144.2 29.8 %collective-permute-start.3 = (bf16[2,1280,256]{2,1,0:T(8,128)(2,1)S(1)}, bf16[2,1280,256]{2,1,0:T(8,128)(2,1)S(1)}, u32[]{:S(2)}, u32[]{:S(2)}) collective-permute-start(bf16[2,1280,256]{2,1,0:T(8,128)(2,1)S(1)} %pad_maximum_fusion.3), channel_id=1, source_target_pairs={{0,64},{64,128},{128,192},{192,0},{1,65},{65,129},{129,193},{193,1... | collective-permute-start | bytes 3932168 | tf_op jit(solution)/shard_map/ppermute | solution.py:22
  156.0 18.0 %collective-permute-start.7 = (bf16[1280,256]{1,0:T(8,128)(2,1)S(1)}, bf16[1280,256]{1,0:T(8,128)(2,1)S(1)}, u32[]{:S(2)}, u32[]{:S(2)}) collective-permute-start(bf16[1280,256]{1,0:T(8,128)(2,1)S(1)} %add_convert_fusion.3), channel_id=1, source_target_pairs={{0,192},{64,0},{128,64},{192,128},{1,193},{65,1},{129,65},{193,129... | collective-permute-start | bytes 1966088 | tf_op jit(solution)/shard_map/ppermute | solution.py:22
  169.9 13.3 %collective-permute-start.16 = (bf16[8,80,256]{2,1,0:T(8,128)(2,1)S(1)}, bf16[8,80,256]{2,1,0:T(8,128)(2,1)S(1)}, u32[]{:S(2)}, u32[]{:S(2)}) collective-permute-start(bf16[8,80,256]{2,1,0:T(8,128)(2,1)S(1)} %bitcast.86), channel_id=1, source_target_pairs={{0,192},{64,0},{128,64},{192,128},{1,193},{65,1},{129,65},{193,129... | collective-permute-start | bytes 983048 | tf_op jit(solution)/shard_map/ppermute | solution.py:22
  171.8 14.7 %collective-permute-start.15 = (bf16[8,80,256]{2,1,0:T(8,128)(2,1)S(1)}, bf16[8,80,256]{2,1,0:T(8,128)(2,1)S(1)}, u32[]{:S(2)}, u32[]{:S(2)}) collective-permute-start(bf16[8,80,256]{2,1,0:T(8,128)(2,1)S(1)} %bitcast.85), channel_id=1, source_target_pairs={{0,64},{64,128},{128,192},{192,0},{1,65},{65,129},{129,193},{193,1... | collective-permute-start | bytes 983048 | tf_op jit(solution)/shard_map/ppermute | solution.py:22
  172.0 14.4 %collective-permute-start.14 = (bf16[8,80,256]{2,1,0:T(8,128)(2,1)S(1)}, bf16[8,80,256]{2,1,0:T(8,128)(2,1)S(1)}, u32[]{:S(2)}, u32[]{:S(2)}) collective-permute-start(bf16[8,80,256]{2,1,0:T(8,128)(2,1)S(1)} %bitcast.84), channel_id=1, source_target_pairs={{0,128},{64,192},{128,0},{192,64},{1,129},{65,193},{129,1},{193,65... | collective-permute-start | bytes 983048 | tf_op jit(solution)/shard_map/ppermute | solution.py:22
  174.6 12.0 %collective-permute-start.9 = (bf16[8,80,256]{2,1,0:T(8,128)(2,1)S(1)}, bf16[8,80,256]{2,1,0:T(8,128)(2,1)S(1)}, u32[]{:S(2)}, u32[]{:S(2)}) collective-permute-start(bf16[8,80,256]{2,1,0:T(8,128)(2,1)S(1)} %get-tuple-element.59), channel_id=1, source_target_pairs={{0,6},{2,0},{4,2},{6,4},{1,7},{3,1},{5,3},{7,5},{8,14},{10,8},{12,... | collective-permute-start | bytes 983048 | tf_op jit(solution)/shard_map/ppermute | solution.py:22
  177.6 9.0 %collective-permute-start.8 = (bf16[8,80,256]{2,1,0:T(8,128)(2,1)S(1)}, bf16[8,80,256]{2,1,0:T(8,128)(2,1)S(1)}, u32[]{:S(2)}, u32[]{:S(2)}) collective-permute-start(bf16[8,80,256]{2,1,0:T(8,128)(2,1)S(1)} %get-tuple-element.58), channel_id=1, source_target_pairs={{0,2},{2,4},{4,6},{6,0},{1,3},{3,5},{5,7},{7,1},{8,10},{10,12},{12... | collective-permute-start | bytes 983048 | tf_op jit(solution)/shard_map/ppermute | solution.py:22
  183.2 8.6 %collective-permute-start.5 = (bf16[8,80,256]{2,1,0:T(8,128)(2,1)S(1)}, bf16[8,80,256]{2,1,0:T(8,128)(2,1)S(1)}, u32[]{:S(2)}, u32[]{:S(2)}) collective-permute-start(bf16[8,80,256]{2,1,0:T(8,128)(2,1)S(1)} %dynamic-slice_bitcast_fusion.7), channel_id=1, source_target_pairs={{0,4},{2,6},{4,0},{6,2},{1,5},{3,7},{5,1},{7,3},{8,12},{10,14},{12... | collective-permute-start | bytes 983048 | tf_op jit(solution)/shard_map/ppermute | solution.py:22
  192.0 11.1 %collective-permute-start.28 = (bf16[84,512]{1,0:T(8,128)(2,1)S(1)}, bf16[84,512]{1,0:T(8,128)(2,1)S(1)}, u32[]{:S(2)}, u32[]{:S(2)}) collective-permute-start(bf16[84,512]{1,0:T(8,128)(2,1)S(1)} %pad_maximum_fusion.12), channel_id=1, source_target_pairs={{0,8},{8,0},{16,24},{24,16},{32,40},{40,32},{48,56},{56,48},{1,9},... | collective-permute-start | bytes 258056 | tf_op jit(solution)/shard_map/ppermute | solution.py:26
  193.4 14.0 %collective-permute-start.29 = (bf16[84,512]{1,0:T(8,128)(2,1)S(1)}, bf16[84,512]{1,0:T(8,128)(2,1)S(1)}, u32[]{:S(2)}, u32[]{:S(2)}) collective-permute-start(bf16[84,512]{1,0:T(8,128)(2,1)S(1)} %pad_maximum_fusion.13), channel_id=1, source_target_pairs={{0,16},{8,24},{16,0},{24,8},{32,48},{40,56},{48,32},{56,40},{1,17}... | collective-permute-start | bytes 258056 | tf_op jit(solution)/shard_map/ppermute | solution.py:26
  196.4 12.4 %collective-permute-start.30 = (bf16[84,512]{1,0:T(8,128)(2,1)S(1)}, bf16[84,512]{1,0:T(8,128)(2,1)S(1)}, u32[]{:S(2)}, u32[]{:S(2)}) collective-permute-start(bf16[84,512]{1,0:T(8,128)(2,1)S(1)} %pad_maximum_fusion.14), channel_id=1, source_target_pairs={{0,24},{8,16},{16,8},{24,0},{32,56},{40,48},{48,40},{56,32},{1,25}... | collective-permute-start | bytes 258056 | tf_op jit(solution)/shard_map/ppermute | solution.py:26
  196.7 12.1 %collective-permute-start.31 = (bf16[84,512]{1,0:T(8,128)(2,1)S(1)}, bf16[84,512]{1,0:T(8,128)(2,1)S(1)}, u32[]{:S(2)}, u32[]{:S(2)}) collective-permute-start(bf16[84,512]{1,0:T(8,128)(2,1)S(1)} %pad_maximum_fusion.15), channel_id=1, source_target_pairs={{0,32},{8,40},{16,48},{24,56},{32,0},{40,8},{48,16},{56,24},{1,33}... | collective-permute-start | bytes 258056 | tf_op jit(solution)/shard_map/ppermute | solution.py:26
  203.0 8.0 %collective-permute-start.32 = (bf16[84,512]{1,0:T(8,128)(2,1)S(1)}, bf16[84,512]{1,0:T(8,128)(2,1)S(1)}, u32[]{:S(2)}, u32[]{:S(2)}) collective-permute-start(bf16[84,512]{1,0:T(8,128)(2,1)S(1)} %pad_maximum_fusion.16), channel_id=1, source_target_pairs={{0,40},{8,32},{16,56},{24,48},{32,8},{40,0},{48,24},{56,16},{1,41}... | collective-permute-start | bytes 258056 | tf_op jit(solution)/shard_map/ppermute | solution.py:26
  203.1 11.7 %copy-start.13 = (bf16[84,512]{1,0:T(8,128)(2,1)}, bf16[84,512]{1,0:T(8,128)(2,1)S(1)}, u32[]{:S(2)}) copy-start(bf16[84,512]{1,0:T(8,128)(2,1)S(1)} %collective-permute-done.28.refs_1_) | copy-start | bytes 258052
  203.2 8.8 %collective-permute-start.33 = (bf16[84,512]{1,0:T(8,128)(2,1)S(1)}, bf16[84,512]{1,0:T(8,128)(2,1)S(1)}, u32[]{:S(2)}, u32[]{:S(2)}) collective-permute-start(bf16[84,512]{1,0:T(8,128)(2,1)S(1)} %pad_maximum_fusion.17), channel_id=1, source_target_pairs={{0,48},{8,56},{16,32},{24,40},{32,16},{40,24},{48,0},{56,8},{1,49}... | collective-permute-start | bytes 258056 | tf_op jit(solution)/shard_map/ppermute | solution.py:26
  207.4 7.4 %copy-start.14 = (bf16[84,512]{1,0:T(8,128)(2,1)}, bf16[84,512]{1,0:T(8,128)(2,1)S(1)}, u32[]{:S(2)}) copy-start(bf16[84,512]{1,0:T(8,128)(2,1)S(1)} %collective-permute-done.29.refs_2_) | copy-start | bytes 258052
  207.4 7.4 %collective-permute-start.34 = (bf16[84,512]{1,0:T(8,128)(2,1)S(1)}, bf16[84,512]{1,0:T(8,128)(2,1)S(1)}, u32[]{:S(2)}, u32[]{:S(2)}) collective-permute-start(bf16[84,512]{1,0:T(8,128)(2,1)S(1)} %pad_maximum_fusion.18), channel_id=1, source_target_pairs={{0,56},{8,48},{16,40},{24,32},{32,24},{40,16},{48,8},{56,0},{1,57}... | collective-permute-start | bytes 258056 | tf_op jit(solution)/shard_map/ppermute | solution.py:26
  208.9 6.0 %copy-start.15 = (bf16[84,512]{1,0:T(8,128)(2,1)}, bf16[84,512]{1,0:T(8,128)(2,1)S(1)}, u32[]{:S(2)}) copy-start(bf16[84,512]{1,0:T(8,128)(2,1)S(1)} %collective-permute-done.30.refs_3_) | copy-start | bytes 258052
  208.9 6.0 %copy-start.16 = (bf16[84,512]{1,0:T(8,128)(2,1)}, bf16[84,512]{1,0:T(8,128)(2,1)S(1)}, u32[]{:S(2)}) copy-start(bf16[84,512]{1,0:T(8,128)(2,1)S(1)} %collective-permute-done.31.refs_4_) | copy-start | bytes 258052
  211.0 3.8 %copy-start.17 = (bf16[84,512]{1,0:T(8,128)(2,1)}, bf16[84,512]{1,0:T(8,128)(2,1)S(1)}, u32[]{:S(2)}) copy-start(bf16[84,512]{1,0:T(8,128)(2,1)S(1)} %collective-permute-done.32.refs_5_) | copy-start | bytes 258052
  211.9 2.9 %copy-start.18 = (bf16[84,512]{1,0:T(8,128)(2,1)}, bf16[84,512]{1,0:T(8,128)(2,1)S(1)}, u32[]{:S(2)}) copy-start(bf16[84,512]{1,0:T(8,128)(2,1)S(1)} %collective-permute-done.33.refs_6_) | copy-start | bytes 258052
  214.8 0.6 copy-start.19

commit v2 on v1

v2 whole, which is shorter than its diff:
```python
import functools
import math

import jax
import jax.numpy as jnp
import numpy as np
from jax import lax
from jax.experimental import pallas as pl
from jax.experimental.pallas import tpu as pltpu
from jax.sharding import Mesh
from jax.sharding import PartitionSpec as P

KVH = 8
HD = 128
F32 = jnp.float32
BF16 = jnp.bfloat16
X = ("xh", "xl")
VMEM = pl.BlockSpec(memory_space=pltpu.VMEM)


def shift(value, axis, size, by):
    return lax.ppermute(value, axis, [(i, (i + by) % size) for i in range(size)])


def swap(value, axis, size, bits):
    return lax.ppermute(value, axis, [(i, i ^ bits) for i in range(size)])


def pick(array, index, axis=0):
    return lax.dynamic_index_in_dim(array, index, axis, keepdims=False)


def add(a, b):
    return (a.astype(F32) + b.astype(F32)).astype(BF16)


def product_kernel(rows, place, a_ref, b_ref, ca_ref, cb_ref, *outs):
    by_y, near, far = outs[:4], outs[4:6], outs[6:]
    turn, step = pl.program_id(0), pl.program_id(1)
    values = jnp.concatenate([a_ref[...], b_ref[...]], axis=0)
    cots = jnp.concatenate([ca_ref[...], cb_ref[...]], axis=0)
    total = lax.dot_general(
        values, cots, (((0,), (0,)), ((), ())), preferred_element_type=F32
    ).astype(BF16)
    part = total.shape[1] // 2
    pieces = total.shape[0] // (2 * rows)
    for k in range(4):

        @pl.when(turn == k)
        def _(k=k):
            for i in range(2 * pieces):
                here = slice(i // 2 * rows, (i // 2 + 1) * rows)
                by_y[k][i % 2, here, :] = total[i * rows : (i + 1) * rows, :part]

    for flip in (0, 1):
        for half in (0, 1):

            @pl.when((place[1] == flip) & (step == half))
            def _(flip=flip, half=half):
                for i in range(2 * pieces):
                    out = (near if i % 2 == flip else far)[half]
                    here = slice(i // 2 * rows, (i // 2 + 1) * rows)
                    out[0, here, :] = total[i * rows : (i + 1) * rows, part:]


def product(rows, place, own, other, own_cot, other_cot):
    tokens, width = own.shape
    columns = own_cot.shape[1]
    part = columns // 2
    steps = 2
    tall = width // (4 * steps)

    def of_turn(k):
        return lambda t, s, place: (0, jnp.clip((t - k) * steps + s, 0, steps - 1), 0)

    token_spec = pl.BlockSpec((tokens, tall), lambda t, s, place: (0, ((place[0] + t) % 4) * steps + s))
    whole = pl.BlockSpec((tokens, columns), lambda t, s, place: (0, 0))
    y_specs = [pl.BlockSpec((2, tall // 2, part), of_turn(k)) for k in range(4)]
    y_shapes = [jax.ShapeDtypeStruct((2, width // 8, part), BF16)] * 4
    x_spec = pl.BlockSpec((1, tall // 2, part), lambda t, s, place: ((place[0] + t) % 4, 0, 0))
    x_shape = jax.ShapeDtypeStruct((4, tall // 2, part), BF16)
    return pl.pallas_call(
        functools.partial(product_kernel, rows),
        grid_spec=pltpu.PrefetchScalarGridSpec(
            num_scalar_prefetch=1,
            grid=(4, steps),
            in_specs=[token_spec, token_spec, whole, whole],
            out_specs=y_specs + [x_spec] * 4,
        ),
        out_shape=y_shapes + [x_shape] * 4,
        compiler_params=pltpu.CompilerParams(vmem_limit_bytes=24 << 20),
        cost_estimate=pl.CostEstimate(
            flops=4 * tokens * width * columns, bytes_accessed=6 * tokens * width, transcendentals=0
        ),
        name="product",
    )(place, own, other, own_cot, other_cot)


def past_kernel(heads, lengths, query_ref, cache_ref, sum_ref, top_ref, mass_ref):
    span = cache_ref.shape[1]
    live = lax.broadcasted_iota(jnp.int32, (8, span), 1) < lengths[pl.program_id(0)]
    for j in range(heads):
        keys = cache_ref[0, :, 2 * j * HD : (2 * j + 1) * HD]
        values = cache_ref[0, :, (2 * j + 1) * HD : (2 * j + 2) * HD]
        scores = lax.dot_general(
            query_ref[0, j], keys, (((1,), (1,)), ((), ())), preferred_element_type=F32
        ) / math.sqrt(HD)
        scores = jnp.where(live, scores, jnp.float32(-1e30))
        top = jnp.max(scores, axis=1, keepdims=True)
        weights = jnp.exp(scores - top)
        mass = jnp.sum(weights, axis=1, keepdims=True)
        sum_ref[0, j] = jnp.dot(weights.astype(BF16), values, preferred_element_type=F32)
        top_ref[0, j] = jnp.broadcast_to(top, (8, HD))
        mass_ref[0, j] = jnp.broadcast_to(mass, (8, HD))


def attend_past(query, cache, lengths):
    rows, heads = query.shape[:2]
    span, columns = cache.shape[1:]
    small = pl.BlockSpec((1, heads, 8, HD), lambda r, lengths: (r, 0, 0, 0))
    shape = jax.ShapeDtypeStruct((rows, heads, 8, HD), F32)
    return pl.pallas_call(
        functools.partial(past_kernel, heads),
        grid_spec=pltpu.PrefetchScalarGridSpec(
            num_scalar_prefetch=1,
            grid=(rows,),
            in_specs=[small, pl.BlockSpec((1, span, columns), lambda r, lengths: (r, 0, 0))],
            out_specs=[small] * 3,
        ),
        out_shape=[shape] * 3,
        compiler_params=pltpu.CompilerParams(vmem_limit_bytes=24 << 20),
        cost_estimate=pl.CostEstimate(
            flops=32 * rows * span * columns,
            bytes_accessed=2 * rows * span * columns,
            transcendentals=8 * rows * heads * span,
        ),
        name="past",
    )(lengths, query, cache)


def finish_kernel(
    factor, weight_ref, query_ref, sum_ref, top_ref, mass_ref, parts_ref, weight_out, attention_out
):
    rows = weight_ref.shape[0]
    total = parts_ref[0].astype(F32)
    for k in range(1, parts_ref.shape[0]):
        total += parts_ref[k].astype(F32)
    weight_out[...] = (weight_ref[...].astype(F32) - factor * total[:rows]).astype(BF16)
    fresh = total[rows:].astype(BF16).astype(F32)
    for r in range(query_ref.shape[0]):
        for j in range(query_ref.shape[1]):
            key = fresh[r : r + 1, 2 * j * HD : (2 * j + 1) * HD]
            value = fresh[r : r + 1, (2 * j + 1) * HD : (2 * j + 2) * HD]
            newest = jnp.sum(query_ref[r, j].astype(F32) * key, axis=1, keepdims=True) / math.sqrt(HD)
            old = top_ref[r, j]
            top = jnp.maximum(old, newest)
            past = jnp.exp(old - top)
            new = jnp.exp(newest - top)
            mixed = (sum_ref[r, j] * past + new * value) / (mass_ref[r, j] * past + new)
            attention_out[r, j] = mixed.astype(BF16)


def local(tokens_in, cotangent, weight, hidden_rows, queries, cache, lengths):
    y, z, xh, xl, c = (lax.axis_index(name) for name in ("y", "z", "xh", "xl", "c"))
    ny, nz, nh, nl, nc = (lax.axis_size(name) for name in ("y", "z", "xh", "xl", "c"))
    x = xh * nl + xl
    nx = nh * nl
    tokens, width = tokens_in.shape
    columns = cotangent.shape[1]
    part = columns // 2
    rows = weight.shape[0]
    factor = 0.01 / math.sqrt(tokens * nc * nl * nh * ny * nz)

    heads = KVH // (nl * nc)
    count = queries.shape[0]
    query = queries.reshape(count, heads, -1, HD)
    group = query.shape[2]
    query = jnp.pad(query, ((0, 0), (0, 0), (0, 8 - group), (0, 0)))

    other_tokens = swap(tokens_in, "c", nc, 1)
    blocks = cotangent.reshape(nl, nc, tokens, columns)
    mine = pick(blocks, xl)
    got = swap(pick(blocks, 1 - xl), "xl", nl, 1)
    past = attend_past(query, cache, lengths)
    other_tokens, past = lax.optimization_barrier((other_tokens, past))

    place = jnp.stack([y, xh]).astype(jnp.int32)
    own = product(rows, place, tokens_in, other_tokens, pick(mine, c), pick(mine, 1 - c))
    own_y, (own_x0a, own_x0b, own_x2a, own_x2b) = own[:4], own[4:]
    up = shift(own_y[2], "y", ny, 1)
    down = shift(own_y[3], "y", ny, -1)
    up_x = shift(own_x2a, X, nx, 1)
    down_x = shift(own_x2b, X, nx, -1)

    got, up, down, up_x, down_x = lax.optimization_barrier((got, up, down, up_x, down_x))
    place = jnp.stack([y, jnp.where(xl == 0, xh, 1 - xh)]).astype(jnp.int32)
    oth = product(rows, place, tokens_in, other_tokens, pick(got, c), pick(got, 1 - c))
    oth_y, (oth_x1a, oth_x1b, oth_x3a, oth_x3b) = oth[:4], oth[4:]
    far = shift(oth_y[2], "y", ny, -1)

    far, hidden_rows = lax.optimization_barrier((far, hidden_rows))
    held = hidden_rows.reshape(count, ny, nz, nh, rows).transpose(1, 3, 0, 2, 4)
    held = jnp.broadcast_to(
        held.reshape(ny, 1, nh, count, nz * rows), (ny, nz, nh, count, nz * rows)
    )
    held = lax.all_to_all(
        held.reshape(-1, count, nz * rows), ("y", "z", "xh"), 0, 0, tiled=True
    )
    held = held.reshape(ny, nz, nh, count, nz * rows).transpose(0, 2, 1, 3, 4).reshape(-1, nz * rows)

    ups = shift(jnp.stack([add(own_y[1], up), oth_y[1]]), "y", ny, 1)
    downs = shift(add(oth_y[3], far), "y", ny, -1)
    own_sum = (own_y[0].astype(F32) + ups[0].astype(F32) + down.astype(F32)).astype(BF16)
    oth_sum = (oth_y[0].astype(F32) + ups[1].astype(F32) + downs.astype(F32)).astype(BF16)
    by_x = jnp.stack(
        [jnp.where(xl == 0, own_sum, oth_sum), jnp.where(xl == 0, oth_sum, own_sum)], axis=1
    ).reshape(nx, nz * rows, part)
    first = lax.all_to_all(by_x, X, 0, 0, tiled=True)

    ups = shift(jnp.stack([add(oth_x1a, up_x), oth_x1b], axis=1), X, nx, 1)
    downs = shift(jnp.stack([oth_x3a, add(oth_x3b, down_x)], axis=1), X, nx, -1)
    by_y = (
        jnp.stack([own_x0a, own_x0b], axis=1).astype(F32) + ups.astype(F32) + downs.astype(F32)
    ).astype(BF16)
    by_y = by_y.reshape(ny, nz * rows, part)
    second = pick(by_y, y).astype(F32)
    for k in (2, 1, 3):
        second += shift(pick(by_y, (y + k) % ny), "y", ny, k).astype(F32)
    first = jnp.sum(first.astype(F32), axis=0)
    both = jnp.concatenate([first.astype(BF16), second.astype(BF16)], axis=1)
    both = both.reshape(nz, rows, columns)

    here = (lax.broadcasted_iota(jnp.int32, (nz, 1, 1), 0) == z).astype(F32)
    update = here * weight.astype(F32) - factor * both.astype(F32)
    update = update.astype(BF16).reshape(nz * rows, columns)
    fresh = jnp.dot(held, update, preferred_element_type=F32).astype(BF16)
    fresh = lax.all_to_all(
        fresh.reshape(ny * nh, nz * count, columns), ("y", "xh"), 0, 0, tiled=True
    )
    fresh = jnp.sum(fresh.astype(F32), axis=0).astype(BF16).reshape(nz, count, columns)
    parts = lax.all_to_all(jnp.concatenate([both, fresh], axis=1), "z", 0, 0, tiled=True)

    new_weight, attention = pl.pallas_call(
        functools.partial(finish_kernel, factor),
        in_specs=[VMEM] * 6,
        out_specs=[VMEM] * 2,
        out_shape=[
            jax.ShapeDtypeStruct(weight.shape, BF16),
            jax.ShapeDtypeStruct(query.shape, BF16),
        ],
        name="finish",
    )(weight, query, *past, parts)
    return (new_weight, attention[:, :, :group].reshape(count, -1))


def solution(mesh):
    names = ("y", "z", "xh", "xl", "c")
    fine = Mesh(np.asarray(mesh.devices).reshape(4, 8, 2, 2, 2), names)
    fsdp, tp = names[:3], names[3:]
    in_specs = (
        P(names, None),
        P(fsdp, tp),
        P(fsdp, tp),
        P(fsdp, None),
        P(fsdp, tp),
        P(fsdp, None, tp),
        P(fsdp),
    )
    out_specs = (P(fsdp, tp), P(fsdp, tp))
    return jax.shard_map(local, mesh=fine, in_specs=in_specs, out_specs=out_specs, check_vma=False)
```

time: 221 us -> 164 us (0.74)
  waiting for transfers between devices: 101 us -> 49.1 us
  starting transfers between devices: 64.5 us -> 39.7 us
  blocking collectives: 0 us -> 24.6 us
  other arithmetic: 5.21 us -> 11.8 us
  matrix products: 6.65 us -> 1.06 us
  local copies, waits for them, and re-layouts: 14.5 us -> 11.2 us
    ppermute x20 -> x2, waiting for transfers between devices: 59 us -> 0.01 us  [swap(): return lax.ppermute(value, axis, [(i, i ^ bits) for i in range(size)])]
    ppermute x20 -> x2, starting transfers between devices: 42.5 us -> 2.45 us  [swap(): return lax.ppermute(value, axis, [(i, i ^ bits) for i in range(size)])]
    all_to_all x0 -> x1, blocking collectives: none -> 24.6 us  [local(): lax.all_to_all(jnp.concatenate([both, fresh], axis=1), 'z', 0, 0, tiled=T...]
    all_to_all x0 -> x3, starting transfers between devices: none -> 20.7 us  [the longest x1 11.3 us: local(): lax.all_to_all(held.reshape(-1, count, nz * rows), ('y', 'z', 'xh'), 0, 0...]
    all_to_all x0 -> x3, waiting for transfers between devices: none -> 14 us  [the longest x1 8.74 us: local(): lax.all_to_all(fresh.reshape(ny * nh, nz * count, columns), ('y', 'xh'),...]
    ppermute x15 -> x12, waiting for transfers between devices: 42.3 us -> 35.1 us  [shift(): lax.ppermute(value, axis, [(i, (i + by) % size) for i in range(size)])]
    dot_general x7 -> x1, matrix products: 6.65 us -> 1.06 us  [local(): fresh = jnp.dot(held, update, preferred_element_type=F32).astype(BF16)]
    ppermute x15 -> x12, starting transfers between devices: 22 us -> 16.5 us  [shift(): lax.ppermute(value, axis, [(i, (i + by) % size) for i in range(size)])]
  transfers between devices with their start and end apart: 35 -> 17, of which waited for: 19 -> 11; matrix products, arithmetic and copies ran while one was open for 7% -> 10% of each run, Pallas kernels for 11% -> 8%
where the time goes in v2:
time: 164 us; the launch traced here: 163 us
  waiting for transfers between devices  49.1 us (30%)
  starting transfers between devices  39.7 us (24%)
  Pallas kernels  24.8 us (15%)
  blocking collectives  24.6 us (15%)
  other arithmetic  11.8 us (7%)
  local copies, waits for them, and re-layouts  11.2 us (7%)
    ppermute x12, waiting for transfers between devices, shift(): lax.ppermute(value, axis, [(i, (i + by) % size) for i in range(size)])  35.1 us
    all_to_all x1, blocking collectives, local(): lax.all_to_all(jnp.concatenate([both, fresh], axis=1), 'z', 0, 0, tiled=T...  24.6 us
    pallas_call x2, Pallas kernels, product(): pl.pallas_call(functools.partial(product_kernel, rows), grid_spec=pltpu.P...  19.5 us
    ppermute x12, starting transfers between devices, shift(): lax.ppermute(value, axis, [(i, (i + by) % size) for i in range(size)])  16.5 us
    all_to_all x1, starting transfers between devices, local(): lax.all_to_all(held.reshape(-1, count, nz * rows), ('y', 'z', 'xh'), 0, 0...  11.3 us
    all_to_all x1, waiting for transfers between devices, local(): lax.all_to_all(fresh.reshape(ny * nh, nz * count, columns), ('y', 'xh'),...  8.74 us
    all_to_all x1, waiting for transfers between devices, local(): lax.all_to_all(held.reshape(-1, count, nz * rows), ('y', 'z', 'xh'), 0, 0...  5.25 us
    all_to_all x1, starting transfers between devices, local(): lax.all_to_all(fresh.reshape(ny * nh, nz * count, columns), ('y', 'xh'),...  5.15 us
  transfers between devices with their start and end apart: 17, of which 11 were waited for; matrix products, arithmetic and copies ran while one was open for 10% of the time, Pallas kernels for 8%

profile of v2, /device:TPU:2, one launch (start us, length us, event | category | flops | bytes accessed | tf_op | source)
XLA Modules:
  0.0 163.2 jit_solution(13483353371425552776)
XLA Ops:
  0.7 0.1 collective-permute-start
  0.8 1.3 dynamic-slice_bitcast_fusion
  2.1 2.4 %collective-permute-start.1 = (bf16[2,384,512]{2,1,0:T(8,128)(2,1)S(1)}, bf16[2,384,512]{2,1,0:T(8,128)(2,1)}, u32[]{:S(2)}, u32[]{:S(2)}) collective-permute-start(bf16[2,384,512]{2,1,0:T(8,128)(2,1)S(1)} %dynamic-slice_bitcast_fusion), channel_id=1, source_target_pairs={{0,2},{2,0},{1,3},{3,1},{4,6},{6,4},{5,7},{7,5},{8,10},{10,8},{9,1... | collective-permute-start | bytes 2359304 | tf_op jit(solution)/shard_map/ppermute | solution.py:26
  4.5 2.2 %copy-done = bf16[4,1024,512]{2,1,0:T(8,128)(2,1)S(1)} copy-done((bf16[4,1024,512]{2,1,0:T(8,128)(2,1)S(1)}, bf16[4,1024,512]{2,1,0:T(8,128)(2,1)}, u32[]{:S(2)}) %copy-start) | copy-done | bytes 4194328
  6.7 3.3 %past.1 = (f32[4,2,8,128]{3,2,1,0:T(8,128)S(1)}, f32[4,2,8,128]{3,2,1,0:T(8,128)S(1)}, f32[4,2,8,128]{3,2,1,0:T(8,128)S(1)}) custom-call(s32[4]{0:T(128)S(1)} %copy-done.5, bf16[4,2,8,128]{3,2,1,0:T(8,128)(2,1)S(1)} %pad.4.query_ref, bf16[4,1024,512]{2,1,0:T(8,128)(2,1)S(1)} %copy-done), custom_call_target="tpu_custom_call" | custom-call | flops 67108864 | bytes 4194304 | tf_op jit(solution)/shard_map/past/pallas_call | solution.py:122
  10.0 0.1 pad_add_fusion
  10.1 0.1 dynamic-slice_bitcast_fusion.3
  10.2 0.4 copy-done.2
  10.7 9.7 %product.2 = (bf16[2,640,256]{2,1,0:T(8,128)(2,1)S(1)}, bf16[2,640,256]{2,1,0:T(8,128)(2,1)S(1)}, bf16[2,640,256]{2,1,0:T(8,128)(2,1)S(1)}, bf16[2,640,256]{2,1,...) custom-call(s32[2]{0:T(128)S(1)} %get-tuple-element.75.place, ...), custom_call_target="tpu_custom_call" | custom-call | flops 4026531840 | bytes 11796480 | tf_op jit(solution)/shard_map/product/pallas_call | solution.py:82
  20.4 0.1 collective-permute-start.2
  20.5 3.2 %collective-permute-start.3 = (bf16[2,640,256]{2,1,0:T(8,128)(2,1)S(1)}, bf16[2,640,256]{2,1,0:T(8,128)(2,1)S(1)}, u32[]{:S(2)}, u32[]{:S(2)}) collective-permute-start(bf16[2,640,256]{2,1,0:T(8,128)(2,1)S(1)} %get-tuple-element.44), channel_id=1, source_target_pairs={{0,192},{64,0},{128,64},{192,128},{1,193},{65,1},{129,65},{193,129... | collective-permute-start | bytes 1966088 | tf_op jit(solution)/shard_map/ppermute | solution.py:22
  23.7 0.4 collective-permute-start.4
  24.1 1.6 collective-permute-start.5
  25.8 12.8 %collective-permute-done.2 = bf16[2,640,256]{2,1,0:T(8,128)(2,1)S(1)} collective-permute-done((bf16[2,640,256]{2,1,0:T(8,128)(2,1)S(1)}, bf16[2,640,256]{2,1,0:T(8,128)(2,1)S(1)}, u32[]{:S(2)}, u32[]{:S(2)}) %collective-permute-start.2) | collective-permute-done | bytes 655392 | tf_op jit(solution)/shard_map/ppermute | solution.py:22
  38.5 1.5 collective-permute-done.4
  40.0 0.3 collective-permute-done.5
  40.3 1.2 dynamic-slice_bitcast_fusion.1
  41.5 9.7 %product.3 = (bf16[2,640,256]{2,1,0:T(8,128)(2,1)S(1)}, bf16[2,640,256]{2,1,0:T(8,128)(2,1)S(1)}, bf16[2,640,256]{2,1,0:T(8,128)(2,1)S(1)}, bf16[2,640,256]{2,1,...) custom-call(s32[2]{0:T(128)S(1)} %get-tuple-element.76.place, ...), custom_call_target="tpu_custom_call" | custom-call | flops 4026531840 | bytes 11796480 | tf_op jit(solution)/shard_map/product/pallas_call | solution.py:82
  51.2 1.7 %collective-permute-start.7 = (bf16[2,640,256]{2,1,0:T(8,128)(2,1)S(1)}, bf16[2,640,256]{2,1,0:T(8,128)(2,1)S(1)}, u32[]{:S(2)}, u32[]{:S(2)}) collective-permute-start(bf16[2,640,256]{2,1,0:T(8,128)(2,1)S(1)} %get-tuple-element.53), channel_id=1, source_target_pairs={{0,192},{64,0},{128,64},{192,128},{1,193},{65,1},{129,65},{193,129... | collective-permute-start | bytes 1966088 | tf_op jit(solution)/shard_map/ppermute | solution.py:22
  53.0 0.2 fusion.6
  53.1 1.2 pad_maximum_fusion.3
  54.3 0.8 collective-permute-start.10
  55.2 0.2 fusion.4
  55.3 1.2 pad_maximum_fusion
  56.5 1.0 collective-permute-start.6
  57.5 0.2 fusion.5
  57.7 1.2 pad_maximum_fusion.2
  58.9 0.6 collective-permute-start.9
  59.4 7.1 %collective-permute-done.7 = bf16[2,640,256]{2,1,0:T(8,128)(2,1)S(1)} collective-permute-done((bf16[2,640,256]{2,1,0:T(8,128)(2,1)S(1)}, bf16[2,640,256]{2,1,0:T(8,128)(2,1)S(1)}, u32[]{:S(2)}, u32[]{:S(2)}) %collective-permute-start.7) | collective-permute-done | bytes 655392 | tf_op jit(solution)/shard_map/ppermute | solution.py:22
  66.5 1.0 add_convert_fusion.3
  67.6 3.1 %collective-permute-start.8 = (bf16[2,640,256]{2,1,0:T(8,128)(2,1)}, bf16[2,640,256]{2,1,0:T(8,128)(2,1)}, u32[]{:S(2)}, u32[]{:S(2)}) collective-permute-start(bf16[2,640,256]{2,1,0:T(8,128)(2,1)} %add_convert_fusion.3), channel_id=1, source_target_pairs={{0,192},{64,0},{128,64},{192,128},{1,193},{65,1},{129,65},{193,129... | collective-permute-start | bytes 1966088 | tf_op jit(solution)/shard_map/ppermute | solution.py:22
  70.7 0.1 reshape.124
  70.8 0.1 broadcast_in_dim.8
  71.0 0.8 broadcast_in_dim.9
  71.8 11.3 %all-to-all-start.1 = ((bf16[64,4,640]{2,1,0:T(4,128)(2,1)}), bf16[64,4,640]{2,1,0:T(4,128)(2,1)S(1)}, u32[]{:S(2)}, u32[]{:S(2)}) async-start(bf16[64,4,640]{2,1,0:T(4,128)(2,1)} %bitcast.29), calls=%async_computation.1 | async-start | bytes 655360 | tf_op jit(solution)/shard_map/all_to_all | solution.py:206
  83.1 0.3 collective-permute-done.8
  83.4 4.2 %collective-permute-done.6 = bf16[2,2,640,256]{3,2,1,0:T(8,128)(2,1)} collective-permute-done((bf16[2,2,640,256]{3,2,1,0:T(8,128)(2,1)}, bf16[2,2,640,256]{3,2,1,0:T(8,128)(2,1)}, u32[]{:S(2)}, u32[]{:S(2)}) %collective-permute-start.6) | collective-permute-done | bytes 1310752 | tf_op jit(solution)/shard_map/ppermute | solution.py:22
  87.6 2.2 %select_bitcast_fusion.1 = (bf16[2,1,640,256]{3,2,0,1:T(8,128)(2,1)S(1)}, bf16[2,1,640,256]{3,2,0,1:T(8,128)(2,1)S(1)}) fusion(pred[]{:T(512)S(6)} %eq.20, bf16[2,640,256]{2,1,0:T(8,128)(2,1)} %copy-done.9, bf16[2,2,640,256]{3,2,1,0:T(8,128)(2,1)} %collective-permute-done.6, bf16[2,640,256]{2,1,0:T(8,128)(2,1)S(1)} %get-tuple-element.41, ...), kind=kLoop, calls=%fused_computation.30 | loop fusion | flops 4587520 | bytes 5242881 | tf_op jit(solution)/shard_map/stack | solution.py:215
  89.8 0.1 pad_maximum_fusion.1
  89.9 1.2 copy.12
  91.1 5.2 %all-to-all-done.1 = bf16[64,4,640]{2,1,0:T(4,128)(2,1)S(1)} async-done(((bf16[64,4,640]{2,1,0:T(4,128)(2,1)}), bf16[64,4,640]{2,1,0:T(4,128)(2,1)S(1)}, u32[]{:S(2)}, u32[]{:S(2)}) %all-to-all-start.1) | async-done | bytes 327712 | tf_op jit(solution)/shard_map/all_to_all | solution.py:206
  96.3 4.3 %all-to-all-start = ((bf16[4,640,256]{2,1,0:T(8,128)(2,1)}), bf16[4,640,256]{2,1,0:T(8,128)(2,1)S(1)}, u32[]{:S(2)}, u32[]{:S(2)}) async-start(bf16[4,640,256]{2,1,0:T(8,128)(2,1)} %bitcast.15), calls=%async_computation | async-start | bytes 2621440 | tf_op jit(solution)/shard_map/all_to_all | solution.py:218
  100.6 2.2 %add_convert_fusion = bf16[4,2,320,256]{3,2,0,1:T(8,128)(2,1)S(1)} fusion(bf16[4,2,320,256]{3,2,0,1:T(8,128)(2,1)} %collective-permute-done.10, bf16[4,2,320,256]{3,2,0,1:T(8,128)(2,1)} %collective-permute-done.9, bf16[4,1,320,256]{3,2,0,1:T(8,128)(2,1)S(1)} %bitcast.76, bf16[4,1,320,256]{3,2,0,1:T(8,128)(2,1)S(1)} %bitcast.75), kind=kLoop, calls=%fused_computation | loop fusion | flops 4587520 | bytes 5242880 | tf_op jit(solution)/shard_map/convert_element_type | solution.py:224
  102.8 0.1 copy.13
  102.9 1.0 dynamic-slice_bitcast_fusion.7
  103.9 1.9 %collective-permute-start.11 = (bf16[640,256]{1,0:T(8,128)(2,1)}, bf16[640,256]{1,0:T(8,128)(2,1)}, u32[]{:S(2)}, u32[]{:S(2)}) collective-permute-start(bf16[640,256]{1,0:T(8,128)(2,1)} %get-tuple-element.70), channel_id=1, source_target_pairs={{0,128},{64,192},{128,0},{192,64},{1,129},{65,193},{129,1},{193,65... | collective-permute-start | bytes 983048 | tf_op jit(solution)/shard_map/ppermute | solution.py:22
  105.8 1.2 collective-permute-start.13
  107.0 0.8 collective-permute-start.12
  107.9 0.1 copy.15
  108.0 0.8 reshape.127
  108.8 5.6 %collective-permute-done.11 = bf16[640,256]{1,0:T(8,128)(2,1)} collective-permute-done((bf16[640,256]{1,0:T(8,128)(2,1)}, bf16[640,256]{1,0:T(8,128)(2,1)}, u32[]{:S(2)}, u32[]{:S(2)}) %collective-permute-start.11) | collective-permute-done | bytes 327712 | tf_op jit(solution)/shard_map/ppermute | solution.py:22
  114.5 3.0 %collective-permute-done.13 = bf16[640,256]{1,0:T(8,128)(2,1)} collective-permute-done((bf16[640,256]{1,0:T(8,128)(2,1)}, bf16[640,256]{1,0:T(8,128)(2,1)}, u32[]{:S(2)}, u32[]{:S(2)}) %collective-permute-start.13) | collective-permute-done | bytes 327712 | tf_op jit(solution)/shard_map/ppermute | solution.py:22
  117.4 0.4 collective-permute-done.12
  117.9 1.3 fusion.9
  119.2 0.4 reduce_sum.24
  119.6 0.2 subtract_convert_fusion
  119.8 0.3 copy-done.8
  120.2 1.1 convolution_convert_fusion
  121.2 5.1 %all-to-all-start.2 = ((bf16[8,32,512]{2,1,0:T(8,128)(2,1)}), bf16[8,32,512]{2,1,0:T(8,128)(2,1)S(1)}, u32[]{:S(2)}, u32[]{:S(2)}) async-start(bf16[8,32,512]{2,1,0:T(8,128)(2,1)} %bitcast.35), calls=%async_computation.2 | async-start | bytes 524288 | tf_op jit(solution)/shard_map/all_to_all | solution.py:237
  126.4 8.7 %all-to-all-done.2 = bf16[8,32,512]{2,1,0:T(8,128)(2,1)S(1)} async-done(((bf16[8,32,512]{2,1,0:T(8,128)(2,1)}), bf16[8,32,512]{2,1,0:T(8,128)(2,1)S(1)}, u32[]{:S(2)}, u32[]{:S(2)}) %all-to-all-start.2) | async-done | bytes 262176 | tf_op jit(solution)/shard_map/all_to_all | solution.py:237
  135.2 0.1 pad_maximum_fusion.4
  135.3 24.6 %all_to_all.20.parts_ref = bf16[8,84,512]{2,1,0:T(8,128)(2,1)} all-to-all(bf16[8,84,512]{2,1,0:T(8,128)(2,1)S(1)} %pad_maximum_fusion.4), channel_id=1, replica_groups=mesh['y'=4,'z'=8,'xh'=2,'xl'=2,'c'=2] {'z'}, dimensions={0} | all-to-all | bytes 1376256 | tf_op jit(solution)/shard_map/all_to_all | solution.py:241
  159.9 2.0 %finish.1 = (bf16[80,512]{1,0:T(8,128)(2,1)}, bf16[4,2,8,128]{3,2,1,0:T(8,128)(2,1)}) custom-call(bf16[80,512]{1,0:T(8,128)(2,1)} %weight_ref.1, bf16[4,2,8,128]{3,2,1,0:T(8,128)(2,1)} %copy-done.1, f32[4,2,8,128]{3,2,1,0:T(8,128)} %copy-done.2, f32[4,2,8,128]{3,2,1,0:T(8,128)} %copy-done.3, f32[4,2,8,128]{3,2,1,0:T(8,128)} %copy-done.4, ...), custom_call_target="tpu_custom_call" | custom-call | tf_op jit(solution)/shard_map/finish/pallas_call | solution.py:243
  161.9 1.3 reshape.130
  (37 shorter events, 0.2 us)
Async XLA Ops:
  0.6 3.8 %copy-start.12 = (bf16[4,1280]{1,0:T(4,128)(2,1)S(1)}, bf16[4,1280]{1,0:T(4,128)(2,1)}, u32[]{:S(2)}) copy-start(bf16[4,1280]{1,0:T(4,128)(2,1)} %param.11) | copy-start | bytes 30724
  0.6 3.8 %copy-start.5 = (s32[4]{0:T(128)S(1)}, s32[4]{0:T(128)}, u32[]{:S(2)}) copy-start(s32[4]{0:T(128)} %lengths.1) | copy-start | bytes 52
  0.7 9.5 %collective-permute-start = (bf16[384,5120]{1,0:T(8,128)(2,1)}, bf16[384,5120]{1,0:T(8,128)(2,1)}, u32[]{:S(2)}, u32[]{:S(2)}) collective-permute-start(bf16[384,5120]{1,0:T(8,128)(2,1)} %a_ref.3), channel_id=1, source_target_pairs={{0,1},{1,0},{2,3},{3,2},{4,5},{5,4},{6,7},{7,6},{8,9},{9,8},{10,11... | collective-permute-start | bytes 11796488 | tf_op jit(solution)/shard_map/ppermute | solution.py:26
  0.8 9.4 %copy-start.7 = (bf16[1536,512]{1,0:T(8,128)(2,1)S(1)}, bf16[1536,512]{1,0:T(8,128)(2,1)}, u32[]{:S(2)}) copy-start(bf16[1536,512]{1,0:T(8,128)(2,1)} %param.8) | copy-start | bytes 4718596
  2.1 23.7 %collective-permute-start.1 = (bf16[2,384,512]{2,1,0:T(8,128)(2,1)S(1)}, bf16[2,384,512]{2,1,0:T(8,128)(2,1)}, u32[]{:S(2)}, u32[]{:S(2)}) collective-permute-start(bf16[2,384,512]{2,1,0:T(8,128)(2,1)S(1)} %dynamic-slice_bitcast_fusion), channel_id=1, source_target_pairs={{0,2},{2,0},{1,3},{3,1},{4,6},{6,4},{5,7},{7,5},{8,10},{10,8},{9,1... | collective-permute-start | bytes 2359304 | tf_op jit(solution)/shard_map/ppermute | solution.py:26
  4.5 2.2 %copy-start = (bf16[4,1024,512]{2,1,0:T(8,128)(2,1)S(1)}, bf16[4,1024,512]{2,1,0:T(8,128)(2,1)}, u32[]{:S(2)}) copy-start(bf16[4,1024,512]{2,1,0:T(8,128)(2,1)} %cache_ref.1) | copy-start | bytes 12582916
  6.7 3.3 %copy-start.1 = (bf16[4,2,8,128]{3,2,1,0:T(8,128)(2,1)}, bf16[4,2,8,128]{3,2,1,0:T(8,128)(2,1)S(1)}, u32[]{:S(2)}) copy-start(bf16[4,2,8,128]{3,2,1,0:T(8,128)(2,1)S(1)} %pad.4.query_ref) | copy-start | bytes 49156
  6.7 4.0 %copy-start.6 = (bf16[384,5120]{1,0:T(8,128)(2,1)S(1)}, bf16[384,5120]{1,0:T(8,128)(2,1)}, u32[]{:S(2)}) copy-start(bf16[384,5120]{1,0:T(8,128)(2,1)} %a_ref.3) | copy-start | bytes 11796484
  10.0 0.6 copy-start.2
  10.0 0.6 copy-start.3
  10.0 0.6 copy-start.4
  20.4 18.1 %collective-permute-start.2 = (bf16[2,640,256]{2,1,0:T(8,128)(2,1)S(1)}, bf16[2,640,256]{2,1,0:T(8,128)(2,1)S(1)}, u32[]{:S(2)}, u32[]{:S(2)}) collective-permute-start(bf16[2,640,256]{2,1,0:T(8,128)(2,1)S(1)} %get-tuple-element.43), channel_id=1, source_target_pairs={{0,64},{64,128},{128,192},{192,0},{1,65},{65,129},{129,193},{193,1... | collective-permute-start | bytes 1966088 | tf_op jit(solution)/shard_map/ppermute | solution.py:22
  20.5 18.0 %collective-permute-start.3 = (bf16[2,640,256]{2,1,0:T(8,128)(2,1)S(1)}, bf16[2,640,256]{2,1,0:T(8,128)(2,1)S(1)}, u32[]{:S(2)}, u32[]{:S(2)}) collective-permute-start(bf16[2,640,256]{2,1,0:T(8,128)(2,1)S(1)} %get-tuple-element.44), channel_id=1, source_target_pairs={{0,192},{64,0},{128,64},{192,128},{1,193},{65,1},{129,65},{193,129... | collective-permute-start | bytes 1966088 | tf_op jit(solution)/shard_map/ppermute | solution.py:22
  23.7 16.3 %collective-permute-start.4 = (bf16[4,320,256]{2,1,0:T(8,128)(2,1)S(1)}, bf16[4,320,256]{2,1,0:T(8,128)(2,1)S(1)}, u32[]{:S(2)}, u32[]{:S(2)}) collective-permute-start(bf16[4,320,256]{2,1,0:T(8,128)(2,1)S(1)} %get-tuple-element.45), channel_id=1, source_target_pairs={{0,2},{2,4},{4,6},{6,0},{1,3},{3,5},{5,7},{7,1},{8,10},{10,12},{12... | collective-permute-start | bytes 1966088 | tf_op jit(solution)/shard_map/ppermute | solution.py:22
  24.1 16.1 %collective-permute-start.5 = (bf16[4,320,256]{2,1,0:T(8,128)(2,1)S(1)}, bf16[4,320,256]{2,1,0:T(8,128)(2,1)S(1)}, u32[]{:S(2)}, u32[]{:S(2)}) collective-permute-start(bf16[4,320,256]{2,1,0:T(8,128)(2,1)S(1)} %get-tuple-element.46), channel_id=1, source_target_pairs={{0,6},{2,0},{4,2},{6,4},{1,7},{3,1},{5,3},{7,5},{8,14},{10,8},{12,... | collective-permute-start | bytes 1966088 | tf_op jit(solution)/shard_map/ppermute | solution.py:22
  38.5 2.9 %copy-start.9 = (bf16[2,640,256]{2,1,0:T(8,128)(2,1)}, bf16[2,640,256]{2,1,0:T(8,128)(2,1)S(1)}, u32[]{:S(2)}) copy-start(bf16[2,640,256]{2,1,0:T(8,128)(2,1)S(1)} %collective-permute-done.3) | copy-start | bytes 1966084
  51.2 15.3 %collective-permute-start.7 = (bf16[2,640,256]{2,1,0:T(8,128)(2,1)S(1)}, bf16[2,640,256]{2,1,0:T(8,128)(2,1)S(1)}, u32[]{:S(2)}, u32[]{:S(2)}) collective-permute-start(bf16[2,640,256]{2,1,0:T(8,128)(2,1)S(1)} %get-tuple-element.53), channel_id=1, source_target_pairs={{0,192},{64,0},{128,64},{192,128},{1,193},{65,1},{129,65},{193,129... | collective-permute-start | bytes 1966088 | tf_op jit(solution)/shard_map/ppermute | solution.py:22
  54.3 46.3 %collective-permute-start.10 = (bf16[4,2,320,256]{3,2,0,1:T(8,128)(2,1)}, bf16[4,2,320,256]{3,2,0,1:T(8,128)(2,1)}, u32[]{:S(2)}, u32[]{:S(2)}) collective-permute-start(bf16[4,2,320,256]{3,2,0,1:T(8,128)(2,1)} %pad_maximum_fusion.3), channel_id=1, source_target_pairs={{0,6},{2,0},{4,2},{6,4},{1,7},{3,1},{5,3},{7,5},{8,14},{10,8},{12,... | collective-permute-start | bytes 3932168 | tf_op jit(solution)/shard_map/ppermute | solution.py:22
  56.5 31.0 %collective-permute-start.6 = (bf16[2,2,640,256]{3,2,1,0:T(8,128)(2,1)}, bf16[2,2,640,256]{3,2,1,0:T(8,128)(2,1)}, u32[]{:S(2)}, u32[]{:S(2)}) collective-permute-start(bf16[2,2,640,256]{3,2,1,0:T(8,128)(2,1)} %pad_maximum_fusion), channel_id=1, source_target_pairs={{0,64},{64,128},{128,192},{192,0},{1,65},{65,129},{129,193},{193,1... | collective-permute-start | bytes 3932168 | tf_op jit(solution)/shard_map/ppermute | solution.py:22
  58.9 11.8 %copy-start.11 = (bf16[4,5120]{1,0:T(4,128)(2,1)S(1)}, bf16[4,5120]{1,0:T(4,128)(2,1)}, u32[]{:S(2)}) copy-start(bf16[4,5120]{1,0:T(4,128)(2,1)} %param.10) | copy-start | bytes 122884
  58.9 41.7 %collective-permute-start.9 = (bf16[4,2,320,256]{3,2,0,1:T(8,128)(2,1)}, bf16[4,2,320,256]{3,2,0,1:T(8,128)(2,1)}, u32[]{:S(2)}, u32[]{:S(2)}) collective-permute-start(bf16[4,2,320,256]{3,2,0,1:T(8,128)(2,1)} %pad_maximum_fusion.2), channel_id=1, source_target_pairs={{0,2},{2,4},{4,6},{6,0},{1,3},{3,5},{5,7},{7,1},{8,10},{10,12},{12... | collective-permute-start | bytes 3932168 | tf_op jit(solution)/shard_map/ppermute | solution.py:22
  67.6 15.8 %collective-permute-start.8 = (bf16[2,640,256]{2,1,0:T(8,128)(2,1)}, bf16[2,640,256]{2,1,0:T(8,128)(2,1)}, u32[]{:S(2)}, u32[]{:S(2)}) collective-permute-start(bf16[2,640,256]{2,1,0:T(8,128)(2,1)} %add_convert_fusion.3), channel_id=1, source_target_pairs={{0,192},{64,0},{128,64},{192,128},{1,193},{65,1},{129,65},{193,129... | collective-permute-start | bytes 1966088 | tf_op jit(solution)/shard_map/ppermute | solution.py:22
  71.8 24.5 %all-to-all-start.1 = ((bf16[64,4,640]{2,1,0:T(4,128)(2,1)}), bf16[64,4,640]{2,1,0:T(4,128)(2,1)S(1)}, u32[]{:S(2)}, u32[]{:S(2)}) async-start(bf16[64,4,640]{2,1,0:T(4,128)(2,1)} %bitcast.29), calls=%async_computation.1 | async-start | bytes 655360 | tf_op jit(solution)/shard_map/all_to_all | solution.py:206
  96.3 22.9 %all-to-all-start = ((bf16[4,640,256]{2,1,0:T(8,128)(2,1)}), bf16[4,640,256]{2,1,0:T(8,128)(2,1)S(1)}, u32[]{:S(2)}, u32[]{:S(2)}) async-start(bf16[4,640,256]{2,1,0:T(8,128)(2,1)} %bitcast.15), calls=%async_computation | async-start | bytes 2621440 | tf_op jit(solution)/shard_map/all_to_all | solution.py:218
  102.9 4.9 %copy-start.10 = (bf16[80,512]{1,0:T(8,128)(2,1)S(1)}, bf16[80,512]{1,0:T(8,128)(2,1)}, u32[]{:S(2)}) copy-start(bf16[80,512]{1,0:T(8,128)(2,1)} %weight_ref.1) | copy-start | bytes 245764
  103.9 10.5 %collective-permute-start.11 = (bf16[640,256]{1,0:T(8,128)(2,1)}, bf16[640,256]{1,0:T(8,128)(2,1)}, u32[]{:S(2)}, u32[]{:S(2)}) collective-permute-start(bf16[640,256]{1,0:T(8,128)(2,1)} %get-tuple-element.70), channel_id=1, source_target_pairs={{0,128},{64,192},{128,0},{192,64},{1,129},{65,193},{129,1},{193,65... | collective-permute-start | bytes 983048 | tf_op jit(solution)/shard_map/ppermute | solution.py:22
  105.8 11.6 %collective-permute-start.13 = (bf16[640,256]{1,0:T(8,128)(2,1)}, bf16[640,256]{1,0:T(8,128)(2,1)}, u32[]{:S(2)}, u32[]{:S(2)}) collective-permute-start(bf16[640,256]{1,0:T(8,128)(2,1)} %get-tuple-element.71), channel_id=1, source_target_pairs={{0,192},{64,0},{128,64},{192,128},{1,193},{65,1},{129,65},{193,129... | collective-permute-start | bytes 983048 | tf_op jit(solution)/shard_map/ppermute | solution.py:22
  107.0 10.8 %collective-permute-start.12 = (bf16[640,256]{1,0:T(8,128)(2,1)}, bf16[640,256]{1,0:T(8,128)(2,1)}, u32[]{:S(2)}, u32[]{:S(2)}) collective-permute-start(bf16[640,256]{1,0:T(8,128)(2,1)} %get-tuple-element.72), channel_id=1, source_target_pairs={{0,64},{64,128},{128,192},{192,0},{1,65},{65,129},{129,193},{193,1... | collective-permute-start | bytes 983048 | tf_op jit(solution)/shard_map/ppermute | solution.py:22
  119.2 1.0 copy-start.8
  121.2 13.9 %all-to-all-start.2 = ((bf16[8,32,512]{2,1,0:T(8,128)(2,1)}), bf16[8,32,512]{2,1,0:T(8,128)(2,1)S(1)}, u32[]{:S(2)}, u32[]{:S(2)}) async-start(bf16[8,32,512]{2,1,0:T(8,128)(2,1)} %bitcast.35), calls=%async_computation.2 | async-start | bytes 524288 | tf_op jit(solution)/shard_map/all_to_all | solution.py:237

commit v3 on v2

--- a/solution.py
+++ b/solution.py
@@ -36,64 +36,59 @@
 
 def product_kernel(rows, place, a_ref, b_ref, ca_ref, cb_ref, *outs):
     by_y, near, far = outs[:4], outs[4:6], outs[6:]
-    turn, step = pl.program_id(0), pl.program_id(1)
+    turn = pl.program_id(0)
     values = jnp.concatenate([a_ref[...], b_ref[...]], axis=0)
     cots = jnp.concatenate([ca_ref[...], cb_ref[...]], axis=0)
     total = lax.dot_general(
         values, cots, (((0,), (0,)), ((), ())), preferred_element_type=F32
     ).astype(BF16)
     part = total.shape[1] // 2
-    pieces = total.shape[0] // (2 * rows)
+    pieces = total.shape[0] // rows
     for k in range(4):
 
         @pl.when(turn == k)
         def _(k=k):
-            for i in range(2 * pieces):
+            for i in range(pieces):
                 here = slice(i // 2 * rows, (i // 2 + 1) * rows)
                 by_y[k][i % 2, here, :] = total[i * rows : (i + 1) * rows, :part]
 
     for flip in (0, 1):
-        for half in (0, 1):
-
-            @pl.when((place[1] == flip) & (step == half))
-            def _(flip=flip, half=half):
-                for i in range(2 * pieces):
-                    out = (near if i % 2 == flip else far)[half]
-                    here = slice(i // 2 * rows, (i // 2 + 1) * rows)
-                    out[0, here, :] = total[i * rows : (i + 1) * rows, part:]
-
-
-def product(rows, place, own, other, own_cot, other_cot):
+
+        @pl.when(place[1] == flip)
+        def _(flip=flip):
+            for i in range(pieces):
+                half, j = divmod(i // 2, pieces // 4)
+                out = (near if i % 2 == flip else far)[half]
+                out[0, j * rows : (j + 1) * rows, :] = total[i * rows : (i + 1) * rows, part:]
+
+
+def product(rows, place, own, other, cots):
     tokens, width = own.shape
-    columns = own_cot.shape[1]
+    columns = cots.shape[2]
     part = columns // 2
-    steps = 2
-    tall = width // (4 * steps)
-
-    def of_turn(k):
-        return lambda t, s, place: (0, jnp.clip((t - k) * steps + s, 0, steps - 1), 0)
-
-    token_spec = pl.BlockSpec((tokens, tall), lambda t, s, place: (0, ((place[0] + t) % 4) * steps + s))
-    whole = pl.BlockSpec((tokens, columns), lambda t, s, place: (0, 0))
-    y_specs = [pl.BlockSpec((2, tall // 2, part), of_turn(k)) for k in range(4)]
-    y_shapes = [jax.ShapeDtypeStruct((2, width // 8, part), BF16)] * 4
-    x_spec = pl.BlockSpec((1, tall // 2, part), lambda t, s, place: ((place[0] + t) % 4, 0, 0))
-    x_shape = jax.ShapeDtypeStruct((4, tall // 2, part), BF16)
+    tall = width // 4
+    token_spec = pl.BlockSpec((tokens, tall), lambda t, place: (0, (place[0] + t) % 4))
+    first_cot = pl.BlockSpec((None, tokens, columns), lambda t, place: (place[2], 0, 0))
+    second_cot = pl.BlockSpec((None, tokens, columns), lambda t, place: (place[2] ^ 1, 0, 0))
+    y_spec = pl.BlockSpec((2, tall // 2, part), lambda t, place: (0, 0, 0))
+    y_shape = jax.ShapeDtypeStruct((2, tall // 2, part), BF16)
+    x_spec = pl.BlockSpec((1, tall // 4, part), lambda t, place: ((place[0] + t) % 4, 0, 0))
+    x_shape = jax.ShapeDtypeStruct((4, tall // 4, part), BF16)
     return pl.pallas_call(
         functools.partial(product_kernel, rows),
         grid_spec=pltpu.PrefetchScalarGridSpec(
             num_scalar_prefetch=1,
-            grid=(4, steps),
-            in_specs=[token_spec, token_spec, whole, whole],
-            out_specs=y_specs + [x_spec] * 4,
-        ),
-        out_shape=y_shapes + [x_shape] * 4,
-        compiler_params=pltpu.CompilerParams(vmem_limit_bytes=24 << 20),
+            grid=(4,),
+            in_specs=[token_spec, token_spec, first_cot, second_cot],
+            out_specs=[y_spec] * 4 + [x_spec] * 4,
+        ),
+        out_shape=[y_shape] * 4 + [x_shape] * 4,
+        compiler_params=pltpu.CompilerParams(vmem_limit_bytes=32 << 20),
         cost_estimate=pl.CostEstimate(
             flops=4 * tokens * width * columns, bytes_accessed=6 * tokens * width, transcendentals=0
         ),
         name="product",
-    )(place, own, other, own_cot, other_cot)
+    )(place, own, other, cots, cots)
 
 
 def past_kernel(heads, lengths, query_ref, cache_ref, sum_ref, top_ref, mass_ref):
@@ -147,17 +142,20 @@
         total += parts_ref[k].astype(F32)
     weight_out[...] = (weight_ref[...].astype(F32) - factor * total[:rows]).astype(BF16)
     fresh = total[rows:].astype(BF16).astype(F32)
-    for r in range(query_ref.shape[0]):
-        for j in range(query_ref.shape[1]):
-            key = fresh[r : r + 1, 2 * j * HD : (2 * j + 1) * HD]
-            value = fresh[r : r + 1, (2 * j + 1) * HD : (2 * j + 2) * HD]
-            newest = jnp.sum(query_ref[r, j].astype(F32) * key, axis=1, keepdims=True) / math.sqrt(HD)
-            old = top_ref[r, j]
+    heads, group = sum_ref.shape[:2]
+    for j in range(heads):
+        key = fresh[:, 2 * j * HD : (2 * j + 1) * HD]
+        value = fresh[:, (2 * j + 1) * HD : (2 * j + 2) * HD]
+        for g in range(group):
+            here = slice((j * group + g) * HD, (j * group + g + 1) * HD)
+            query = query_ref[:, here].astype(F32)
+            newest = jnp.sum(query * key, axis=1, keepdims=True) / math.sqrt(HD)
+            old = top_ref[j, g]
             top = jnp.maximum(old, newest)
             past = jnp.exp(old - top)
             new = jnp.exp(newest - top)
-            mixed = (sum_ref[r, j] * past + new * value) / (mass_ref[r, j] * past + new)
-            attention_out[r, j] = mixed.astype(BF16)
+            mixed = (sum_ref[j, g] * past + new * value) / (mass_ref[j, g] * past + new)
+            attention_out[:, here] = mixed.astype(BF16)
 
 
 def local(tokens_in, cotangent, weight, hidden_rows, queries, cache, lengths):
@@ -179,24 +177,26 @@
 
     other_tokens = swap(tokens_in, "c", nc, 1)
     blocks = cotangent.reshape(nl, nc, tokens, columns)
-    mine = pick(blocks, xl)
     got = swap(pick(blocks, 1 - xl), "xl", nl, 1)
-    past = attend_past(query, cache, lengths)
-    other_tokens, past = lax.optimization_barrier((other_tokens, past))
-
-    place = jnp.stack([y, xh]).astype(jnp.int32)
-    own = product(rows, place, tokens_in, other_tokens, pick(mine, c), pick(mine, 1 - c))
+
+    place = jnp.stack([y, xh, xl * nc + c]).astype(jnp.int32)
+    own = product(
+        rows, place, tokens_in, other_tokens, cotangent.reshape(nl * nc, tokens, columns)
+    )
     own_y, (own_x0a, own_x0b, own_x2a, own_x2b) = own[:4], own[4:]
     up = shift(own_y[2], "y", ny, 1)
     down = shift(own_y[3], "y", ny, -1)
     up_x = shift(own_x2a, X, nx, 1)
     down_x = shift(own_x2b, X, nx, -1)
 
-    got, up, down, up_x, down_x = lax.optimization_barrier((got, up, down, up_x, down_x))
-    place = jnp.stack([y, jnp.where(xl == 0, xh, 1 - xh)]).astype(jnp.int32)
-    oth = product(rows, place, tokens_in, other_tokens, pick(got, c), pick(got, 1 - c))
+    place = jnp.stack([y, jnp.where(xl == 0, xh, 1 - xh), c]).astype(jnp.int32)
+    oth = product(rows, place, tokens_in, other_tokens, got)
     oth_y, (oth_x1a, oth_x1b, oth_x3a, oth_x3b) = oth[:4], oth[4:]
-    far = shift(oth_y[2], "y", ny, -1)
+    oth_y2, up, down, up_x, down_x, query = lax.optimization_barrier(
+        (oth_y[2], up, down, up_x, down_x, query)
+    )
+    far = shift(oth_y2, "y", ny, -1)
+    past = attend_past(query, cache, lengths)
 
     far, hidden_rows = lax.optimization_barrier((far, hidden_rows))
     held = hidden_rows.reshape(count, ny, nz, nh, rows).transpose(1, 3, 0, 2, 4)
@@ -208,25 +208,29 @@
     )
     held = held.reshape(ny, nz, nh, count, nz * rows).transpose(0, 2, 1, 3, 4).reshape(-1, nz * rows)
 
-    ups = shift(jnp.stack([add(own_y[1], up), oth_y[1]]), "y", ny, 1)
-    downs = shift(add(oth_y[3], far), "y", ny, -1)
-    own_sum = (own_y[0].astype(F32) + ups[0].astype(F32) + down.astype(F32)).astype(BF16)
-    oth_sum = (oth_y[0].astype(F32) + ups[1].astype(F32) + downs.astype(F32)).astype(BF16)
-    by_x = jnp.stack(
-        [jnp.where(xl == 0, own_sum, oth_sum), jnp.where(xl == 0, oth_sum, own_sum)], axis=1
-    ).reshape(nx, nz * rows, part)
-    first = lax.all_to_all(by_x, X, 0, 0, tiled=True)
-
-    ups = shift(jnp.stack([add(oth_x1a, up_x), oth_x1b], axis=1), X, nx, 1)
-    downs = shift(jnp.stack([oth_x3a, add(oth_x3b, down_x)], axis=1), X, nx, -1)
+    oth_up = shift(oth_y[1], "y", ny, 1)
+    own_up = shift(add(own_y[1], up), "y", ny, 1)
+    oth_down = shift(add(oth_y[3], far), "y", ny, -1)
+    up_b = shift(oth_x1b, X, nx, 1)
+    down_a = shift(oth_x3a, X, nx, -1)
+    up_a = shift(add(oth_x1a, up_x), X, nx, 1)
+    down_b = shift(add(oth_x3b, down_x), X, nx, -1)
+
+    def after_y(k):
+        index = ((x + k) % nx) // nl
+        terms = (oth_y[0], oth_up, oth_down) if k % 2 else (own_y[0], own_up, down)
+        return sum(pick(term, index).astype(F32) for term in terms)
+
     by_y = (
-        jnp.stack([own_x0a, own_x0b], axis=1).astype(F32) + ups.astype(F32) + downs.astype(F32)
+        jnp.stack([own_x0a, own_x0b], axis=1).astype(F32)
+        + jnp.stack([up_a, up_b], axis=1).astype(F32)
+        + jnp.stack([down_a, down_b], axis=1).astype(F32)
     ).astype(BF16)
     by_y = by_y.reshape(ny, nz * rows, part)
-    second = pick(by_y, y).astype(F32)
+    first, second = after_y(0), pick(by_y, y).astype(F32)
     for k in (2, 1, 3):
+        first += shift(after_y(k).astype(BF16), X, nx, k).astype(F32)
         second += shift(pick(by_y, (y + k) % ny), "y", ny, k).astype(F32)
-    first = jnp.sum(first.astype(F32), axis=0)
     both = jnp.concatenate([first.astype(BF16), second.astype(BF16)], axis=1)
     both = both.reshape(nz, rows, columns)
 
@@ -240,17 +244,17 @@
     fresh = jnp.sum(fresh.astype(F32), axis=0).astype(BF16).reshape(nz, count, columns)
     parts = lax.all_to_all(jnp.concatenate([both, fresh], axis=1), "z", 0, 0, tiled=True)
 
-    new_weight, attention = pl.pallas_call(
+    past = [values[:, :, :group].transpose(1, 2, 0, 3) for values in past]
+    return pl.pallas_call(
         functools.partial(finish_kernel, factor),
         in_specs=[VMEM] * 6,
         out_specs=[VMEM] * 2,
         out_shape=[
             jax.ShapeDtypeStruct(weight.shape, BF16),
-            jax.ShapeDtypeStruct(query.shape, BF16),
+            jax.ShapeDtypeStruct(queries.shape, BF16),
         ],
         name="finish",
-    )(weight, query, *past, parts)
-    return (new_weight, attention[:, :, :group].reshape(count, -1))
+    )(weight, queries, *past, parts)
 
 
 def solution(mesh):

time: 164 us -> 157 us (0.957)
  blocking collectives: 24.6 us -> 0 us
  starting transfers between devices: 39.7 us -> 54.2 us
  other arithmetic: 11.8 us -> 17.8 us
  waiting for transfers between devices: 49.1 us -> 43.9 us
  local copies, waits for them, and re-layouts: 11.2 us -> 15.4 us
  Pallas kernels: 24.8 us -> 23 us
    all_to_all x1 -> x0, blocking collectives: 24.6 us -> none  [local(): lax.all_to_all(jnp.concatenate([both, fresh], axis=1), 'z', 0, 0, tiled=T...]
    ppermute x12 -> x18, waiting for transfers between devices: 35.1 us -> 20.9 us  [shift(): lax.ppermute(value, axis, [(i, (i + by) % size) for i in range(size)])]
    all_to_all x1, waiting for transfers between devices: 0.01 us -> 11.6 us  [local(): lax.all_to_all(jnp.concatenate([both, fresh], axis=1), 'z', 0, 0, tiled=T...]
    ppermute x12 -> x18, starting transfers between devices: 16.5 us -> 27.8 us  [shift(): lax.ppermute(value, axis, [(i, (i + by) % size) for i in range(size)])]
    unnamed x26 -> x22, local copies, waits for them, and re-layouts: 3.05 us -> 9.64 us
    another operation x9 -> x2, other arithmetic: 6.51 us -> 0.15 us  [the longest x1 0.08 us: local(): place = jnp.stack([y, jnp.where(xl == 0, xh, 1 - xh), c]).astype(jnp.int32)]
    convert_element_type x1 -> x4, other arithmetic: 1.03 us -> 7.29 us  [add(): return (a.astype(F32) + b.astype(F32)).astype(BF16)]
    all_to_all x1, waiting for transfers between devices: 5.25 us -> 0.01 us  [local(): lax.all_to_all(held.reshape(-1, count, nz * rows), ('y', 'z', 'xh'), 0, 0...]
  transfers between devices with their start and end apart: 17 -> 23, of which waited for: 11 -> 12; matrix products, arithmetic and copies ran while one was open for 10% -> 13% of each run, Pallas kernels for 8% -> 13%
where the time goes in v3:
time: 157 us; the launch traced here: 156 us
  starting transfers between devices  54.2 us (35%)
  waiting for transfers between devices  43.9 us (28%)
  Pallas kernels  23 us (15%)
  other arithmetic  17.8 us (11%)
  local copies, waits for them, and re-layouts  15.4 us (10%)
    ppermute x18, starting transfers between devices, shift(): lax.ppermute(value, axis, [(i, (i + by) % size) for i in range(size)])  27.8 us
    ppermute x18, waiting for transfers between devices, shift(): lax.ppermute(value, axis, [(i, (i + by) % size) for i in range(size)])  20.9 us
    pallas_call x2, Pallas kernels, product(): pl.pallas_call(functools.partial(product_kernel, rows), grid_spec=pltpu.P...  17.7 us
    all_to_all x1, starting transfers between devices, local(): lax.all_to_all(held.reshape(-1, count, nz * rows), ('y', 'z', 'xh'), 0, 0...  12.6 us
    all_to_all x1, waiting for transfers between devices, local(): lax.all_to_all(jnp.concatenate([both, fresh], axis=1), 'z', 0, 0, tiled=T...  11.6 us
    unnamed x22, local copies, waits for them, and re-layouts  9.64 us
    all_to_all x1, waiting for transfers between devices, local(): lax.all_to_all(fresh.reshape(ny * nh, nz * count, columns), ('y', 'xh'),...  8.74 us
    convert_element_type x4, other arithmetic, add(): return (a.astype(F32) + b.astype(F32)).astype(BF16)  7.29 us
  transfers between devices with their start and end apart: 23, of which 12 were waited for; matrix products, arithmetic and copies ran while one was open for 13% of the time, Pallas kernels for 13%

profile of v3, /device:TPU:2, one launch (start us, length us, event | category | flops | bytes accessed | tf_op | source)
XLA Modules:
  0.0 156.4 jit_solution(7663790732682937835)
XLA Ops:
  0.6 0.1 collective-permute-start
  0.7 2.1 %dynamic-slice_bitcast_fusion = bf16[2,384,512]{2,1,0:T(8,128)(2,1)} fusion(bf16[2,2,384,512]{3,2,1,0:T(8,128)(2,1)} %bitcast.63, s32[]{:T(128)S(6)} %select_n.86), kind=kLoop, calls=%fused_computation.7 | loop fusion | bytes 1572868 | tf_op jit(solution)/shard_map/jit(dynamic_index_in_dim)/squeeze | solution.py:30
  2.8 2.3 %collective-permute-start.1 = (bf16[2,384,512]{2,1,0:T(8,128)(2,1)}, bf16[2,384,512]{2,1,0:T(8,128)(2,1)}, u32[]{:S(2)}, u32[]{:S(2)}) collective-permute-start(bf16[2,384,512]{2,1,0:T(8,128)(2,1)} %dynamic-slice_bitcast_fusion), channel_id=1, source_target_pairs={{0,2},{2,0},{1,3},{3,1},{4,6},{6,4},{5,7},{7,5},{8,10},{10,8},{9,1... | collective-permute-start | bytes 2359304 | tf_op jit(solution)/shard_map/ppermute | solution.py:26
  5.2 2.6 %collective-permute-done.b_ref = bf16[384,5120]{1,0:T(8,128)(2,1)} collective-permute-done((bf16[384,5120]{1,0:T(8,128)(2,1)}, bf16[384,5120]{1,0:T(8,128)(2,1)}, u32[]{:S(2)}, u32[]{:S(2)}) %collective-permute-start) | collective-permute-done | bytes 3932192 | tf_op jit(solution)/shard_map/ppermute | solution.py:26
  7.8 1.4 copy-done.1
  9.3 2.1 %copy-done.3 = bf16[384,5120]{1,0:T(8,128)(2,1)S(1)} copy-done((bf16[384,5120]{1,0:T(8,128)(2,1)S(1)}, bf16[384,5120]{1,0:T(8,128)(2,1)}, u32[]{:S(2)}) %copy-start.3) | copy-done | bytes 3932184
  11.4 8.9 %product.3 = (bf16[2,640,256]{2,1,0:T(8,128)(2,1)S(1)}, bf16[2,640,256]{2,1,0:T(8,128)(2,1)S(1)}, bf16[2,640,256]{2,1,0:T(8,128)(2,1)}, bf16[2,640,256]{2,1,0:T(...) custom-call(s32[3]{0:T(128)S(1)} %pad_add_fusion.1.place, ...), custom_call_target="tpu_custom_call" | custom-call | flops 4026531840 | bytes 11796480 | tf_op jit(solution)/shard_map/product/pallas_call | solution.py:77
  20.3 1.6 %collective-permute-start.2 = (bf16[2,640,256]{2,1,0:T(8,128)(2,1)}, bf16[2,640,256]{2,1,0:T(8,128)(2,1)}, u32[]{:S(2)}, u32[]{:S(2)}) collective-permute-start(bf16[2,640,256]{2,1,0:T(8,128)(2,1)} %get-tuple-element.30), channel_id=1, source_target_pairs={{0,64},{64,128},{128,192},{192,0},{1,65},{65,129},{129,193},{193,1... | collective-permute-start | bytes 1966088 | tf_op jit(solution)/shard_map/ppermute | solution.py:22
  21.9 1.6 %collective-permute-start.3 = (bf16[2,640,256]{2,1,0:T(8,128)(2,1)}, bf16[2,640,256]{2,1,0:T(8,128)(2,1)}, u32[]{:S(2)}, u32[]{:S(2)}) collective-permute-start(bf16[2,640,256]{2,1,0:T(8,128)(2,1)} %get-tuple-element.31), channel_id=1, source_target_pairs={{0,192},{64,0},{128,64},{192,128},{1,193},{65,1},{129,65},{193,129... | collective-permute-start | bytes 1966088 | tf_op jit(solution)/shard_map/ppermute | solution.py:22
  23.6 1.5 collective-permute-start.4
  25.0 0.8 collective-permute-start.5
  26.0 2.1 %copy-done.4 = bf16[384,5120]{1,0:T(8,128)(2,1)S(1)} copy-done((bf16[384,5120]{1,0:T(8,128)(2,1)S(1)}, bf16[384,5120]{1,0:T(8,128)(2,1)}, u32[]{:S(2)}) %copy-start.4) | copy-done | bytes 3932184
  28.1 8.7 %product.2 = (bf16[2,640,256]{2,1,0:T(8,128)(2,1)S(1)}, bf16[2,640,256]{2,1,0:T(8,128)(2,1)}, bf16[2,640,256]{2,1,0:T(8,128)(2,1)S(1)}, bf16[2,640,256]{2,1,0:T(...) custom-call(s32[3]{0:T(128)S(1)} %pad_add_fusion.place, ...), custom_call_target="tpu_custom_call" | custom-call | flops 4026531840 | bytes 11796480 | tf_op jit(solution)/shard_map/product/pallas_call | solution.py:77
  36.8 1.2 collective-permute-start.14
  38.0 0.6 collective-permute-done.2
  38.7 2.2 %collective-permute-start.15 = (bf16[4,320,256]{2,1,0:T(8,128)(2,1)S(1)}, bf16[4,320,256]{2,1,0:T(8,128)(2,1)S(1)}, u32[]{:S(2)}, u32[]{:S(2)}) collective-permute-start(bf16[4,320,256]{2,1,0:T(8,128)(2,1)S(1)} %get-tuple-element.52), channel_id=1, source_target_pairs={{0,6},{2,0},{4,2},{6,4},{1,7},{3,1},{5,3},{7,5},{8,14},{10,8},{12,... | collective-permute-start | bytes 1966088 | tf_op jit(solution)/shard_map/ppermute | solution.py:22
  40.9 0.3 collective-permute-done.4
  41.2 0.9 collective-permute-done.5
  42.1 1.6 %collective-permute-start.9 = (bf16[2,640,256]{2,1,0:T(8,128)(2,1)S(1)}, bf16[2,640,256]{2,1,0:T(8,128)(2,1)S(1)}, u32[]{:S(2)}, u32[]{:S(2)}) collective-permute-start(bf16[2,640,256]{2,1,0:T(8,128)(2,1)S(1)} %get-tuple-element.45), channel_id=1, source_target_pairs={{0,192},{64,0},{128,64},{192,128},{1,193},{65,1},{129,65},{193,129... | collective-permute-start | bytes 1966088 | tf_op jit(solution)/shard_map/ppermute | solution.py:22
  43.7 2.1 %add_convert_fusion.1 = bf16[4,320,256]{2,1,0:T(8,128)(2,1)} fusion(bf16[4,320,256]{2,1,0:T(8,128)(2,1)} %collective-permute-done.5, bf16[4,320,256]{2,1,0:T(8,128)(2,1)S(1)} %get-tuple-element.53), kind=kLoop, calls=%fused_computation.2 | loop fusion | flops 1310720 | bytes 1966080 | tf_op jit(solution)/shard_map/convert_element_type | solution.py:34
  45.8 0.7 collective-permute-start.16
  46.5 2.1 %add_convert_fusion.2 = bf16[4,320,256]{2,1,0:T(8,128)(2,1)} fusion(bf16[4,320,256]{2,1,0:T(8,128)(2,1)} %collective-permute-done.4, bf16[4,320,256]{2,1,0:T(8,128)(2,1)S(1)} %get-tuple-element.49), kind=kLoop, calls=%fused_computation.3 | loop fusion | flops 1310720 | bytes 1966080 | tf_op jit(solution)/shard_map/convert_element_type | solution.py:34
  48.6 1.3 collective-permute-start.13
  49.9 2.1 %add_convert_fusion.4 = bf16[2,640,256]{2,1,0:T(8,128)(2,1)} fusion(bf16[2,640,256]{2,1,0:T(8,128)(2,1)} %collective-permute-done.2, bf16[2,640,256]{2,1,0:T(8,128)(2,1)S(1)} %get-tuple-element.39), kind=kLoop, calls=%fused_computation.5 | loop fusion | flops 1310720 | bytes 1966080 | tf_op jit(solution)/shard_map/convert_element_type | solution.py:34
  52.0 4.7 %collective-permute-done.9 = bf16[2,640,256]{2,1,0:T(8,128)(2,1)S(1)} collective-permute-done((bf16[2,640,256]{2,1,0:T(8,128)(2,1)S(1)}, bf16[2,640,256]{2,1,0:T(8,128)(2,1)S(1)}, u32[]{:S(2)}, u32[]{:S(2)}) %collective-permute-start.9) | collective-permute-done | bytes 655392 | tf_op jit(solution)/shard_map/ppermute | solution.py:22
  56.7 1.0 add_convert_fusion.3
  57.7 1.6 collective-permute-start.8
  59.3 0.9 copy-done.7
  60.2 2.5 %collective-permute-start.10 = (bf16[2,640,256]{2,1,0:T(8,128)(2,1)}, bf16[2,640,256]{2,1,0:T(8,128)(2,1)}, u32[]{:S(2)}, u32[]{:S(2)}) collective-permute-start(bf16[2,640,256]{2,1,0:T(8,128)(2,1)} %add_convert_fusion.3), channel_id=1, source_target_pairs={{0,192},{64,0},{128,64},{192,128},{1,193},{65,1},{129,65},{193,129... | collective-permute-start | bytes 1966088 | tf_op jit(solution)/shard_map/ppermute | solution.py:22
  62.7 6.8 %collective-permute-done.16 = bf16[4,320,256]{2,1,0:T(8,128)(2,1)} collective-permute-done((bf16[4,320,256]{2,1,0:T(8,128)(2,1)}, bf16[4,320,256]{2,1,0:T(8,128)(2,1)}, u32[]{:S(2)}, u32[]{:S(2)}) %collective-permute-start.16) | collective-permute-done | bytes 655392 | tf_op jit(solution)/shard_map/ppermute | solution.py:22
  69.5 2.1 %add_convert_fusion = bf16[4,2,320,256]{3,2,0,1:T(8,128)(2,1)S(1)} fusion(bf16[4,1,320,256]{3,2,0,1:T(8,128)(2,1)S(1)} %bitcast.62, bf16[4,1,320,256]{3,2,0,1:T(8,128)(2,1)S(1)} %bitcast.61, bf16[4,1,320,256]{3,2,0,1:T(8,128)(2,1)} %bitcast.73, bf16[4,1,320,256]{3,2,0,1:T(8,128)(2,1)} %bitcast.17, bf16[4,1,320,256]{3,2,0,1:T(8,128)(2,1)} %bitcast.20, ...), kind=kLoop, calls=%fused_computation | loop fusion | flops 5898240 | bytes 5242880 | tf_op jit(solution)/shard_map/convert_element_type | solution.py:228
  71.7 0.1 copy.20
  71.8 1.0 dynamic-slice_bitcast_fusion.3
  72.8 1.9 %collective-permute-start.17 = (bf16[640,256]{1,0:T(8,128)(2,1)}, bf16[640,256]{1,0:T(8,128)(2,1)}, u32[]{:S(2)}, u32[]{:S(2)}) collective-permute-start(bf16[640,256]{1,0:T(8,128)(2,1)} %get-tuple-element.58), channel_id=1, source_target_pairs={{0,128},{64,192},{128,0},{192,64},{1,129},{65,193},{129,1},{193,65... | collective-permute-start | bytes 983048 | tf_op jit(solution)/shard_map/ppermute | solution.py:22
  74.6 0.1 reshape.142
  74.8 0.1 broadcast_in_dim.8
  74.9 0.8 broadcast_in_dim.9
  75.7 12.6 %all-to-all-start = ((bf16[64,4,640]{2,1,0:T(4,128)(2,1)}), bf16[64,4,640]{2,1,0:T(4,128)(2,1)S(1)}, u32[]{:S(2)}, u32[]{:S(2)}) async-start(bf16[64,4,640]{2,1,0:T(4,128)(2,1)} %bitcast.28), calls=%async_computation | async-start | bytes 655360 | tf_op jit(solution)/shard_map/all_to_all | solution.py:206
  88.5 1.7 %collective-permute-start.18 = (bf16[640,256]{1,0:T(8,128)(2,1)}, bf16[640,256]{1,0:T(8,128)(2,1)S(1)}, u32[]{:S(2)}, u32[]{:S(2)}) collective-permute-start(bf16[640,256]{1,0:T(8,128)(2,1)} %get-tuple-element.60), channel_id=1, source_target_pairs={{0,64},{64,128},{128,192},{192,0},{1,65},{65,129},{129,193},{193,1... | collective-permute-start | bytes 983048 | tf_op jit(solution)/shard_map/ppermute | solution.py:22
  90.2 1.7 %collective-permute-start.19 = (bf16[640,256]{1,0:T(8,128)(2,1)}, bf16[640,256]{1,0:T(8,128)(2,1)S(1)}, u32[]{:S(2)}, u32[]{:S(2)}) collective-permute-start(bf16[640,256]{1,0:T(8,128)(2,1)} %get-tuple-element.59), channel_id=1, source_target_pairs={{0,192},{64,0},{128,64},{192,128},{1,193},{65,1},{129,65},{193,129... | collective-permute-start | bytes 983048 | tf_op jit(solution)/shard_map/ppermute | solution.py:22
  91.9 1.9 %fusion.6 = bf16[640,256]{1,0:T(8,128)(2,1)} fusion(bf16[2,640,256]{2,1,0:T(8,128)(2,1)} %collective-permute-done.3, s32[]{:T(128)S(6)} %select_n.92, bf16[2,640,256]{2,1,0:T(8,128)(2,1)} %collective-permute-done.6, bf16[2,640,256]{2,1,0:T(8,128)(2,1)S(1)} %get-tuple-element.38), kind=kLoop, calls=%fused_computation.21 | loop fusion | flops 983040 | bytes 1310724 | tf_op jit(solution)/shard_map/convert_element_type | solution.py:232
  93.8 3.1 %collective-permute-start.7 = (bf16[640,256]{1,0:T(8,128)(2,1)}, bf16[640,256]{1,0:T(8,128)(2,1)S(1)}, u32[]{:S(2)}, u32[]{:S(2)}) collective-permute-start(bf16[640,256]{1,0:T(8,128)(2,1)} %fusion.6), channel_id=1, source_target_pairs={{0,4},{2,6},{4,0},{6,2},{1,5},{3,7},{5,1},{7,3},{8,12},{10,14},{12... | collective-permute-start | bytes 983048 | tf_op jit(solution)/shard_map/ppermute | solution.py:22
  96.9 2.4 %fusion.7 = (bf16[640,256]{1,0:T(8,128)(2,1)}, bf16[640,256]{1,0:T(8,128)(2,1)}) fusion(bf16[2,640,256]{2,1,0:T(8,128)(2,1)} %collective-permute-done.10, s32[]{:T(128)S(6)} %select_n.95, bf16[2,640,256]{2,1,0:T(8,128)(2,1)} %collective-permute-done.8, bf16[2,640,256]{2,1,0:T(8,128)(2,1)S(1)} %get-tuple-element.42, s32[]{:T(128)S(6)} %select_n.98), kind=kLoop, calls=%fused_computation.22 | loop fusion | flops 1966080 | bytes 2621448 | tf_op jit(solution)/shard_map/convert_element_type | solution.py:232
  99.2 2.8 %collective-permute-start.12 = (bf16[640,256]{1,0:T(8,128)(2,1)}, bf16[640,256]{1,0:T(8,128)(2,1)}, u32[]{:S(2)}, u32[]{:S(2)}) collective-permute-start(bf16[640,256]{1,0:T(8,128)(2,1)} %get-tuple-element.57), channel_id=1, source_target_pairs={{0,6},{2,0},{4,2},{6,4},{1,7},{3,1},{5,3},{7,5},{8,14},{10,8},{12,... | collective-permute-start | bytes 983048 | tf_op jit(solution)/shard_map/ppermute | solution.py:22
  102.1 2.0 %collective-permute-done.18 = bf16[640,256]{1,0:T(8,128)(2,1)S(1)} collective-permute-done((bf16[640,256]{1,0:T(8,128)(2,1)}, bf16[640,256]{1,0:T(8,128)(2,1)S(1)}, u32[]{:S(2)}, u32[]{:S(2)}) %collective-permute-start.18) | collective-permute-done | bytes 327712 | tf_op jit(solution)/shard_map/ppermute | solution.py:22
  104.0 1.1 fusion.2
  105.2 0.1 copy.22
  105.4 1.0 collective-permute-done.7
  106.4 4.2 %collective-permute-done.11 = bf16[640,256]{1,0:T(8,128)(2,1)} collective-permute-done((bf16[640,256]{1,0:T(8,128)(2,1)}, bf16[640,256]{1,0:T(8,128)(2,1)}, u32[]{:S(2)}, u32[]{:S(2)}) %collective-permute-start.11) | collective-permute-done | bytes 327712 | tf_op jit(solution)/shard_map/ppermute | solution.py:22
  110.5 0.5 collective-permute-done.12
  111.0 1.5 fusion.5
  112.5 0.2 subtract_convert_fusion
  112.8 1.1 convolution_convert_fusion
  113.9 5.0 %all-to-all-start.1 = ((bf16[8,32,512]{2,1,0:T(8,128)(2,1)}), bf16[8,32,512]{2,1,0:T(8,128)(2,1)S(1)}, u32[]{:S(2)}, u32[]{:S(2)}) async-start(bf16[8,32,512]{2,1,0:T(8,128)(2,1)} %bitcast.34), calls=%async_computation.1 | async-start | bytes 524288 | tf_op jit(solution)/shard_map/all_to_all | solution.py:241
  118.9 8.7 %all-to-all-done.1 = bf16[8,32,512]{2,1,0:T(8,128)(2,1)S(1)} async-done(((bf16[8,32,512]{2,1,0:T(8,128)(2,1)}), bf16[8,32,512]{2,1,0:T(8,128)(2,1)S(1)}, u32[]{:S(2)}, u32[]{:S(2)}) %all-to-all-start.1) | async-done | bytes 262176 | tf_op jit(solution)/shard_map/all_to_all | solution.py:241
  127.7 0.9 pad_maximum_fusion
  128.7 6.4 %all-to-all-start.2 = ((bf16[8,84,512]{2,1,0:T(8,128)(2,1)}), bf16[8,84,512]{2,1,0:T(8,128)(2,1)S(1)}, u32[]{:S(2)}, u32[]{:S(2)}) async-start(bf16[8,84,512]{2,1,0:T(8,128)(2,1)} %pad_maximum_fusion), calls=%async_computation.2 | async-start | bytes 1441792 | tf_op jit(solution)/shard_map/all_to_all | solution.py:245
  135.1 2.2 %copy-done = bf16[4,1024,512]{2,1,0:T(8,128)(2,1)S(1)} copy-done((bf16[4,1024,512]{2,1,0:T(8,128)(2,1)S(1)}, bf16[4,1024,512]{2,1,0:T(8,128)(2,1)}, u32[]{:S(2)}) %copy-start) | copy-done | bytes 4194328
  137.2 3.3 %past.1 = (f32[4,2,8,128]{3,2,1,0:T(8,128)S(1)}, f32[4,2,8,128]{3,2,1,0:T(8,128)S(1)}, f32[4,2,8,128]{3,2,1,0:T(8,128)S(1)}) custom-call(s32[4]{0:T(128)S(1)} %copy-done.2, bf16[4,2,8,128]{3,2,1,0:T(8,128)(2,1)S(1)} %pad.4.query_ref, bf16[4,1024,512]{2,1,0:T(8,128)(2,1)S(1)} %copy-done), custom_call_target="tpu_custom_call" | custom-call | flops 67108864 | bytes 4194304 | tf_op jit(solution)/shard_map/past/pallas_call | solution.py:117
  140.6 0.6 slice_bitcast_fusion.2.sum_ref
  141.3 0.6 slice_bitcast_fusion
  141.9 11.6 %all-to-all-done.2.parts_ref = bf16[8,84,512]{2,1,0:T(8,128)(2,1)S(1)} async-done(((bf16[8,84,512]{2,1,0:T(8,128)(2,1)}), bf16[8,84,512]{2,1,0:T(8,128)(2,1)S(1)}, u32[]{:S(2)}, u32[]{:S(2)}) %all-to-all-start.2) | async-done | bytes 688160 | tf_op jit(solution)/shard_map/all_to_all | solution.py:245
  153.5 0.9 copy-done.5
  154.3 2.0 %finish.1 = (bf16[80,512]{1,0:T(8,128)(2,1)}, bf16[4,1280]{1,0:T(4,128)(2,1)}) custom-call(bf16[80,512]{1,0:T(8,128)(2,1)} %weight_ref.1, bf16[4,1280]{1,0:T(4,128)(2,1)} %query_ref.1, f32[2,5,4,128]{3,2,1,0:T(4,128)} %slice_bitcast_fusion.2.sum_ref, f32[2,5,4,128]{3,2,1,0:T(4,128)} %get-tuple-element.62.top_ref, ...), custom_call_target="tpu_custom_call" | custom-call | tf_op jit(solution)/shard_map/finish/pallas_call | solution.py:248
  (43 shorter events, 0.5 us)
Async XLA Ops:
  0.6 7.2 %collective-permute-start = (bf16[384,5120]{1,0:T(8,128)(2,1)}, bf16[384,5120]{1,0:T(8,128)(2,1)}, u32[]{:S(2)}, u32[]{:S(2)}) collective-permute-start(bf16[384,5120]{1,0:T(8,128)(2,1)} %a_ref.3), channel_id=1, source_target_pairs={{0,1},{1,0},{2,3},{3,2},{4,5},{5,4},{6,7},{7,6},{8,9},{9,8},{10,11... | collective-permute-start | bytes 11796488 | tf_op jit(solution)/shard_map/ppermute | solution.py:26
  2.8 23.1 %collective-permute-start.1 = (bf16[2,384,512]{2,1,0:T(8,128)(2,1)}, bf16[2,384,512]{2,1,0:T(8,128)(2,1)}, u32[]{:S(2)}, u32[]{:S(2)}) collective-permute-start(bf16[2,384,512]{2,1,0:T(8,128)(2,1)} %dynamic-slice_bitcast_fusion), channel_id=1, source_target_pairs={{0,2},{2,0},{1,3},{3,1},{4,6},{6,4},{5,7},{7,5},{8,10},{10,8},{9,1... | collective-permute-start | bytes 2359304 | tf_op jit(solution)/shard_map/ppermute | solution.py:26
  7.8 1.4 copy-start.1
  9.3 2.1 %copy-start.3 = (bf16[384,5120]{1,0:T(8,128)(2,1)S(1)}, bf16[384,5120]{1,0:T(8,128)(2,1)}, u32[]{:S(2)}) copy-start(bf16[384,5120]{1,0:T(8,128)(2,1)} %a_ref.3) | copy-start | bytes 11796484
  11.4 14.5 %copy-start.10 = (bf16[4,1280]{1,0:T(4,128)(2,1)S(1)}, bf16[4,1280]{1,0:T(4,128)(2,1)}, u32[]{:S(2)}) copy-start(bf16[4,1280]{1,0:T(4,128)(2,1)} %query_ref.1) | copy-start | bytes 30724
  20.3 18.3 %collective-permute-start.2 = (bf16[2,640,256]{2,1,0:T(8,128)(2,1)}, bf16[2,640,256]{2,1,0:T(8,128)(2,1)}, u32[]{:S(2)}, u32[]{:S(2)}) collective-permute-start(bf16[2,640,256]{2,1,0:T(8,128)(2,1)} %get-tuple-element.30), channel_id=1, source_target_pairs={{0,64},{64,128},{128,192},{192,0},{1,65},{65,129},{129,193},{193,1... | collective-permute-start | bytes 1966088 | tf_op jit(solution)/shard_map/ppermute | solution.py:22
  21.9 19.0 %collective-permute-start.3 = (bf16[2,640,256]{2,1,0:T(8,128)(2,1)}, bf16[2,640,256]{2,1,0:T(8,128)(2,1)}, u32[]{:S(2)}, u32[]{:S(2)}) collective-permute-start(bf16[2,640,256]{2,1,0:T(8,128)(2,1)} %get-tuple-element.31), channel_id=1, source_target_pairs={{0,192},{64,0},{128,64},{192,128},{1,193},{65,1},{129,65},{193,129... | collective-permute-start | bytes 1966088 | tf_op jit(solution)/shard_map/ppermute | solution.py:22
  23.6 17.6 %collective-permute-start.4 = (bf16[4,320,256]{2,1,0:T(8,128)(2,1)}, bf16[4,320,256]{2,1,0:T(8,128)(2,1)}, u32[]{:S(2)}, u32[]{:S(2)}) collective-permute-start(bf16[4,320,256]{2,1,0:T(8,128)(2,1)} %get-tuple-element.32), channel_id=1, source_target_pairs={{0,2},{2,4},{4,6},{6,0},{1,3},{3,5},{5,7},{7,1},{8,10},{10,12},{12... | collective-permute-start | bytes 1966088 | tf_op jit(solution)/shard_map/ppermute | solution.py:22
  25.0 17.0 %collective-permute-start.5 = (bf16[4,320,256]{2,1,0:T(8,128)(2,1)}, bf16[4,320,256]{2,1,0:T(8,128)(2,1)}, u32[]{:S(2)}, u32[]{:S(2)}) collective-permute-start(bf16[4,320,256]{2,1,0:T(8,128)(2,1)} %get-tuple-element.33), channel_id=1, source_target_pairs={{0,6},{2,0},{4,2},{6,4},{1,7},{3,1},{5,3},{7,5},{8,14},{10,8},{12,... | collective-permute-start | bytes 1966088 | tf_op jit(solution)/shard_map/ppermute | solution.py:22
  26.0 2.1 %copy-start.4 = (bf16[384,5120]{1,0:T(8,128)(2,1)S(1)}, bf16[384,5120]{1,0:T(8,128)(2,1)}, u32[]{:S(2)}) copy-start(bf16[384,5120]{1,0:T(8,128)(2,1)} %a_ref.3) | copy-start | bytes 11796484
  36.8 20.9 %collective-permute-start.14 = (bf16[4,320,256]{2,1,0:T(8,128)(2,1)S(1)}, bf16[4,320,256]{2,1,0:T(8,128)(2,1)S(1)}, u32[]{:S(2)}, u32[]{:S(2)}) collective-permute-start(bf16[4,320,256]{2,1,0:T(8,128)(2,1)S(1)} %get-tuple-element.51), channel_id=1, source_target_pairs={{0,2},{2,4},{4,6},{6,0},{1,3},{3,5},{5,7},{7,1},{8,10},{10,12},{12... | collective-permute-start | bytes 1966088 | tf_op jit(solution)/shard_map/ppermute | solution.py:22
  38.7 20.6 %collective-permute-start.15 = (bf16[4,320,256]{2,1,0:T(8,128)(2,1)S(1)}, bf16[4,320,256]{2,1,0:T(8,128)(2,1)S(1)}, u32[]{:S(2)}, u32[]{:S(2)}) collective-permute-start(bf16[4,320,256]{2,1,0:T(8,128)(2,1)S(1)} %get-tuple-element.52), channel_id=1, source_target_pairs={{0,6},{2,0},{4,2},{6,4},{1,7},{3,1},{5,3},{7,5},{8,14},{10,8},{12,... | collective-permute-start | bytes 1966088 | tf_op jit(solution)/shard_map/ppermute | solution.py:22
  42.1 14.6 %collective-permute-start.9 = (bf16[2,640,256]{2,1,0:T(8,128)(2,1)S(1)}, bf16[2,640,256]{2,1,0:T(8,128)(2,1)S(1)}, u32[]{:S(2)}, u32[]{:S(2)}) collective-permute-start(bf16[2,640,256]{2,1,0:T(8,128)(2,1)S(1)} %get-tuple-element.45), channel_id=1, source_target_pairs={{0,192},{64,0},{128,64},{192,128},{1,193},{65,1},{129,65},{193,129... | collective-permute-start | bytes 1966088 | tf_op jit(solution)/shard_map/ppermute | solution.py:22
  45.8 23.8 %collective-permute-start.16 = (bf16[4,320,256]{2,1,0:T(8,128)(2,1)}, bf16[4,320,256]{2,1,0:T(8,128)(2,1)}, u32[]{:S(2)}, u32[]{:S(2)}) collective-permute-start(bf16[4,320,256]{2,1,0:T(8,128)(2,1)} %add_convert_fusion.1), channel_id=1, source_target_pairs={{0,6},{2,0},{4,2},{6,4},{1,7},{3,1},{5,3},{7,5},{8,14},{10,8},{12,... | collective-permute-start | bytes 1966088 | tf_op jit(solution)/shard_map/ppermute | solution.py:22
  48.6 20.9 %collective-permute-start.13 = (bf16[4,320,256]{2,1,0:T(8,128)(2,1)}, bf16[4,320,256]{2,1,0:T(8,128)(2,1)}, u32[]{:S(2)}, u32[]{:S(2)}) collective-permute-start(bf16[4,320,256]{2,1,0:T(8,128)(2,1)} %add_convert_fusion.2), channel_id=1, source_target_pairs={{0,2},{2,4},{4,6},{6,0},{1,3},{3,5},{5,7},{7,1},{8,10},{10,12},{12... | collective-permute-start | bytes 1966088 | tf_op jit(solution)/shard_map/ppermute | solution.py:22
  56.7 33.5 %collective-permute-start.6 = (bf16[2,640,256]{2,1,0:T(8,128)(2,1)}, bf16[2,640,256]{2,1,0:T(8,128)(2,1)}, u32[]{:S(2)}, u32[]{:S(2)}) collective-permute-start(bf16[2,640,256]{2,1,0:T(8,128)(2,1)} %add_convert_fusion.4), channel_id=1, source_target_pairs={{0,64},{64,128},{128,192},{192,0},{1,65},{65,129},{129,193},{193,1... | collective-permute-start | bytes 1966088 | tf_op jit(solution)/shard_map/ppermute | solution.py:22
  57.7 1.6 %copy-start.6 = (bf16[4,320,256]{2,1,0:T(8,128)(2,1)}, bf16[4,320,256]{2,1,0:T(8,128)(2,1)S(1)}, u32[]{:S(2)}) copy-start(bf16[4,320,256]{2,1,0:T(8,128)(2,1)S(1)} %collective-permute-done.14) | copy-start | bytes 1966084
  57.7 36.1 %collective-permute-start.8 = (bf16[2,640,256]{2,1,0:T(8,128)(2,1)}, bf16[2,640,256]{2,1,0:T(8,128)(2,1)}, u32[]{:S(2)}, u32[]{:S(2)}) collective-permute-start(bf16[2,640,256]{2,1,0:T(8,128)(2,1)} %get-tuple-element.43), channel_id=1, source_target_pairs={{0,64},{64,128},{128,192},{192,0},{1,65},{65,129},{129,193},{193,1... | collective-permute-start | bytes 1966088 | tf_op jit(solution)/shard_map/ppermute | solution.py:22
  59.3 0.9 copy-start.7
  60.2 36.7 %collective-permute-start.10 = (bf16[2,640,256]{2,1,0:T(8,128)(2,1)}, bf16[2,640,256]{2,1,0:T(8,128)(2,1)}, u32[]{:S(2)}, u32[]{:S(2)}) collective-permute-start(bf16[2,640,256]{2,1,0:T(8,128)(2,1)} %add_convert_fusion.3), channel_id=1, source_target_pairs={{0,192},{64,0},{128,64},{192,128},{1,193},{65,1},{129,65},{193,129... | collective-permute-start | bytes 1966088 | tf_op jit(solution)/shard_map/ppermute | solution.py:22
  71.8 2.9 %copy-start.9 = (bf16[4,5120]{1,0:T(4,128)(2,1)S(1)}, bf16[4,5120]{1,0:T(4,128)(2,1)}, u32[]{:S(2)}) copy-start(bf16[4,5120]{1,0:T(4,128)(2,1)} %param.10) | copy-start | bytes 122884
  71.8 16.7 %copy-start.8 = (bf16[80,512]{1,0:T(8,128)(2,1)S(1)}, bf16[80,512]{1,0:T(8,128)(2,1)}, u32[]{:S(2)}) copy-start(bf16[80,512]{1,0:T(8,128)(2,1)} %weight_ref.1) | copy-start | bytes 245764
  72.8 26.5 %collective-permute-start.17 = (bf16[640,256]{1,0:T(8,128)(2,1)}, bf16[640,256]{1,0:T(8,128)(2,1)}, u32[]{:S(2)}, u32[]{:S(2)}) collective-permute-start(bf16[640,256]{1,0:T(8,128)(2,1)} %get-tuple-element.58), channel_id=1, source_target_pairs={{0,128},{64,192},{128,0},{192,64},{1,129},{65,193},{129,1},{193,65... | collective-permute-start | bytes 983048 | tf_op jit(solution)/shard_map/ppermute | solution.py:22
  75.7 29.5 %all-to-all-start = ((bf16[64,4,640]{2,1,0:T(4,128)(2,1)}), bf16[64,4,640]{2,1,0:T(4,128)(2,1)S(1)}, u32[]{:S(2)}, u32[]{:S(2)}) async-start(bf16[64,4,640]{2,1,0:T(4,128)(2,1)} %bitcast.28), calls=%async_computation | async-start | bytes 655360 | tf_op jit(solution)/shard_map/all_to_all | solution.py:206
  88.5 15.5 %collective-permute-start.18 = (bf16[640,256]{1,0:T(8,128)(2,1)}, bf16[640,256]{1,0:T(8,128)(2,1)S(1)}, u32[]{:S(2)}, u32[]{:S(2)}) collective-permute-start(bf16[640,256]{1,0:T(8,128)(2,1)} %get-tuple-element.60), channel_id=1, source_target_pairs={{0,64},{64,128},{128,192},{192,0},{1,65},{65,129},{129,193},{193,1... | collective-permute-start | bytes 983048 | tf_op jit(solution)/shard_map/ppermute | solution.py:22
  90.2 13.8 %collective-permute-start.19 = (bf16[640,256]{1,0:T(8,128)(2,1)}, bf16[640,256]{1,0:T(8,128)(2,1)S(1)}, u32[]{:S(2)}, u32[]{:S(2)}) collective-permute-start(bf16[640,256]{1,0:T(8,128)(2,1)} %get-tuple-element.59), channel_id=1, source_target_pairs={{0,192},{64,0},{128,64},{192,128},{1,193},{65,1},{129,65},{193,129... | collective-permute-start | bytes 983048 | tf_op jit(solution)/shard_map/ppermute | solution.py:22
  93.8 12.6 %collective-permute-start.7 = (bf16[640,256]{1,0:T(8,128)(2,1)}, bf16[640,256]{1,0:T(8,128)(2,1)S(1)}, u32[]{:S(2)}, u32[]{:S(2)}) collective-permute-start(bf16[640,256]{1,0:T(8,128)(2,1)} %fusion.6), channel_id=1, source_target_pairs={{0,4},{2,6},{4,0},{6,2},{1,5},{3,7},{5,1},{7,3},{8,12},{10,14},{12... | collective-permute-start | bytes 983048 | tf_op jit(solution)/shard_map/ppermute | solution.py:22
  99.2 11.3 %collective-permute-start.11 = (bf16[640,256]{1,0:T(8,128)(2,1)}, bf16[640,256]{1,0:T(8,128)(2,1)}, u32[]{:S(2)}, u32[]{:S(2)}) collective-permute-start(bf16[640,256]{1,0:T(8,128)(2,1)} %get-tuple-element.56), channel_id=1, source_target_pairs={{0,2},{2,4},{4,6},{6,0},{1,3},{3,5},{5,7},{7,1},{8,10},{10,12},{12... | collective-permute-start | bytes 983048 | tf_op jit(solution)/shard_map/ppermute | solution.py:22
  99.2 11.8 %collective-permute-start.12 = (bf16[640,256]{1,0:T(8,128)(2,1)}, bf16[640,256]{1,0:T(8,128)(2,1)}, u32[]{:S(2)}, u32[]{:S(2)}) collective-permute-start(bf16[640,256]{1,0:T(8,128)(2,1)} %get-tuple-element.57), channel_id=1, source_target_pairs={{0,6},{2,0},{4,2},{6,4},{1,7},{3,1},{5,3},{7,5},{8,14},{10,8},{12,... | collective-permute-start | bytes 983048 | tf_op jit(solution)/shard_map/ppermute | solution.py:22
  113.9 13.8 %all-to-all-start.1 = ((bf16[8,32,512]{2,1,0:T(8,128)(2,1)}), bf16[8,32,512]{2,1,0:T(8,128)(2,1)S(1)}, u32[]{:S(2)}, u32[]{:S(2)}) async-start(bf16[8,32,512]{2,1,0:T(8,128)(2,1)} %bitcast.34), calls=%async_computation.1 | async-start | bytes 524288 | tf_op jit(solution)/shard_map/all_to_all | solution.py:241
  127.7 7.3 %copy-start.2 = (s32[4]{0:T(128)S(1)}, s32[4]{0:T(128)}, u32[]{:S(2)}) copy-start(s32[4]{0:T(128)} %lengths.1) | copy-start | bytes 52
  128.7 24.8 %all-to-all-start.2 = ((bf16[8,84,512]{2,1,0:T(8,128)(2,1)}), bf16[8,84,512]{2,1,0:T(8,128)(2,1)S(1)}, u32[]{:S(2)}, u32[]{:S(2)}) async-start(bf16[8,84,512]{2,1,0:T(8,128)(2,1)} %pad_maximum_fusion), calls=%async_computation.2 | async-start | bytes 1441792 | tf_op jit(solution)/shard_map/all_to_all | solution.py:245
  135.1 2.2 %copy-start = (bf16[4,1024,512]{2,1,0:T(8,128)(2,1)S(1)}, bf16[4,1024,512]{2,1,0:T(8,128)(2,1)}, u32[]{:S(2)}) copy-start(bf16[4,1024,512]{2,1,0:T(8,128)(2,1)} %cache_ref.1) | copy-start | bytes 12582916
  153.5 0.9 copy-start.5

commit v4 on v3

--- a/solution.py
+++ b/solution.py
@@ -179,6 +179,13 @@
     blocks = cotangent.reshape(nl, nc, tokens, columns)
     got = swap(pick(blocks, 1 - xl), "xl", nl, 1)
 
+    held = hidden_rows.reshape(count, ny, nz, nh, rows).transpose(3, 1, 0, 2, 4)
+    held = held.reshape(nh, ny, count, nz * rows)
+    ours, theirs = pick(held, xh), swap(pick(held, 1 - xh), "xh", nh, 1)
+    held = jnp.concatenate(
+        [jnp.where(xh == 0, ours, theirs), jnp.where(xh == 0, theirs, ours)], axis=1
+    )
+
     place = jnp.stack([y, xh, xl * nc + c]).astype(jnp.int32)
     own = product(
         rows, place, tokens_in, other_tokens, cotangent.reshape(nl * nc, tokens, columns)
@@ -198,23 +205,24 @@
     far = shift(oth_y2, "y", ny, -1)
     past = attend_past(query, cache, lengths)
 
-    far, hidden_rows = lax.optimization_barrier((far, hidden_rows))
-    held = hidden_rows.reshape(count, ny, nz, nh, rows).transpose(1, 3, 0, 2, 4)
-    held = jnp.broadcast_to(
-        held.reshape(ny, 1, nh, count, nz * rows), (ny, nz, nh, count, nz * rows)
-    )
+    far, held = lax.optimization_barrier((far, held))
+    held = jnp.broadcast_to(held[:, None], (ny, nz, *held.shape[1:]))
     held = lax.all_to_all(
-        held.reshape(-1, count, nz * rows), ("y", "z", "xh"), 0, 0, tiled=True
-    )
-    held = held.reshape(ny, nz, nh, count, nz * rows).transpose(0, 2, 1, 3, 4).reshape(-1, nz * rows)
+        held.reshape(ny * nz, nh * count, nz * rows), ("y", "z"), 0, 0, tiled=True
+    ).reshape(-1, nz * rows)
 
     oth_up = shift(oth_y[1], "y", ny, 1)
     own_up = shift(add(own_y[1], up), "y", ny, 1)
+    far, oth_up = lax.optimization_barrier((far, oth_up))
     oth_down = shift(add(oth_y[3], far), "y", ny, -1)
     up_b = shift(oth_x1b, X, nx, 1)
     down_a = shift(oth_x3a, X, nx, -1)
     up_a = shift(add(oth_x1a, up_x), X, nx, 1)
     down_b = shift(add(oth_x3b, down_x), X, nx, -1)
+
+    up_a, up_b, down_a, down_b, own_up = lax.optimization_barrier(
+        (up_a, up_b, down_a, down_b, own_up)
+    )
 
     def after_y(k):
         index = ((x + k) % nx) // nl
@@ -238,6 +246,7 @@
     update = here * weight.astype(F32) - factor * both.astype(F32)
     update = update.astype(BF16).reshape(nz * rows, columns)
     fresh = jnp.dot(held, update, preferred_element_type=F32).astype(BF16)
+    fresh = fresh.reshape(ny, nz, nh, count, columns).transpose(0, 2, 1, 3, 4)
     fresh = lax.all_to_all(
         fresh.reshape(ny * nh, nz * count, columns), ("y", "xh"), 0, 0, tiled=True
     )

time: 157 us -> 150 us (0.955)
  starting transfers between devices: 54.2 us -> 48.6 us
  waiting for transfers between devices: 43.9 us -> 41.6 us
    all_to_all x1, waiting for transfers between devices: 0.01 us -> 7.9 us  [local(): lax.all_to_all(held.reshape(ny * nz, nh * count, nz * rows), ('y', 'z'),...]
    ppermute x18, waiting for transfers between devices: 20.9 us -> 13.8 us  [shift(): lax.ppermute(value, axis, [(i, (i + by) % size) for i in range(size)])]
    all_to_all x1, starting transfers between devices: 12.6 us -> 8.51 us  [local(): lax.all_to_all(held.reshape(ny * nz, nh * count, nz * rows), ('y', 'z'),...]
    all_to_all x1, waiting for transfers between devices: 11.6 us -> 8.57 us  [local(): lax.all_to_all(jnp.concatenate([both, fresh], axis=1), 'z', 0, 0, tiled=T...]
    all_to_all x1, starting transfers between devices: 6.39 us -> 3.59 us  [local(): lax.all_to_all(jnp.concatenate([both, fresh], axis=1), 'z', 0, 0, tiled=T...]
    ppermute x2 -> x3, starting transfers between devices: 2.37 us -> 4.52 us  [swap(): return lax.ppermute(value, axis, [(i, i ^ bits) for i in range(size)])]
    squeeze x2 -> x3, local copies, waits for them, and re-layouts: 3.08 us -> 3.14 us  [pick(): return lax.dynamic_index_in_dim(array, index, axis, keepdims=False)]
    unnamed x22 -> x26, local copies, waits for them, and re-layouts: 9.64 us -> 9.63 us
  transfers between devices with their start and end apart: 23 -> 24, of which waited for: 12 -> 8; matrix products, arithmetic and copies ran while one was open for 13% -> 15% of each run, Pallas kernels for 13% -> 14%
where the time goes in v4:
time: 150 us; the launch traced here: 149 us
  starting transfers between devices  48.6 us (32%)
  waiting for transfers between devices  41.6 us (28%)
  Pallas kernels  22.8 us (15%)
  other arithmetic  18.3 us (12%)
  local copies, waits for them, and re-layouts  16.1 us (11%)
    ppermute x18, starting transfers between devices, shift(): lax.ppermute(value, axis, [(i, (i + by) % size) for i in range(size)])  28.3 us
    pallas_call x2, Pallas kernels, product(): pl.pallas_call(functools.partial(product_kernel, rows), grid_spec=pltpu.P...  17.4 us
    ppermute x18, waiting for transfers between devices, shift(): lax.ppermute(value, axis, [(i, (i + by) % size) for i in range(size)])  13.8 us
    unnamed x26, local copies, waits for them, and re-layouts  9.63 us
    all_to_all x1, waiting for transfers between devices, local(): lax.all_to_all(fresh.reshape(ny * nh, nz * count, columns), ('y', 'xh'),...  8.74 us
    all_to_all x1, waiting for transfers between devices, local(): lax.all_to_all(jnp.concatenate([both, fresh], axis=1), 'z', 0, 0, tiled=T...  8.57 us
    all_to_all x1, starting transfers between devices, local(): lax.all_to_all(held.reshape(ny * nz, nh * count, nz * rows), ('y', 'z'),...  8.51 us
    all_to_all x1, waiting for transfers between devices, local(): lax.all_to_all(held.reshape(ny * nz, nh * count, nz * rows), ('y', 'z'),...  7.9 us
  transfers between devices with their start and end apart: 24, of which 8 were waited for; matrix products, arithmetic and copies ran while one was open for 15% of the time, Pallas kernels for 14%

profile of v4, /device:TPU:2, one launch (start us, length us, event | category | flops | bytes accessed | tf_op | source)
XLA Modules:
  0.0 148.8 jit_solution(8461893924755189429)
XLA Ops:
  0.6 0.1 collective-permute-start
  0.7 2.1 %dynamic-slice_bitcast_fusion = bf16[2,384,512]{2,1,0:T(8,128)(2,1)} fusion(bf16[2,2,384,512]{3,2,1,0:T(8,128)(2,1)} %bitcast.69, s32[]{:T(128)S(6)} %select_n.105), kind=kLoop, calls=%fused_computation.7 | loop fusion | bytes 1572868 | tf_op jit(solution)/shard_map/jit(dynamic_index_in_dim)/squeeze | solution.py:30
  2.9 2.3 %collective-permute-start.1 = (bf16[2,384,512]{2,1,0:T(8,128)(2,1)}, bf16[2,384,512]{2,1,0:T(8,128)(2,1)}, u32[]{:S(2)}, u32[]{:S(2)}) collective-permute-start(bf16[2,384,512]{2,1,0:T(8,128)(2,1)} %dynamic-slice_bitcast_fusion), channel_id=1, source_target_pairs={{0,2},{2,0},{1,3},{3,1},{4,6},{6,4},{5,7},{7,5},{8,10},{10,8},{9,1... | collective-permute-start | bytes 2359304 | tf_op jit(solution)/shard_map/ppermute | solution.py:26
  5.1 0.1 pad_add_fusion.1.place
  5.2 2.6 %collective-permute-done.b_ref = bf16[384,5120]{1,0:T(8,128)(2,1)} collective-permute-done((bf16[384,5120]{1,0:T(8,128)(2,1)}, bf16[384,5120]{1,0:T(8,128)(2,1)}, u32[]{:S(2)}, u32[]{:S(2)}) %collective-permute-start) | collective-permute-done | bytes 3932192 | tf_op jit(solution)/shard_map/ppermute | solution.py:26
  7.8 1.4 copy-done.1
  9.3 2.1 %copy-done.3 = bf16[384,5120]{1,0:T(8,128)(2,1)S(1)} copy-done((bf16[384,5120]{1,0:T(8,128)(2,1)S(1)}, bf16[384,5120]{1,0:T(8,128)(2,1)}, u32[]{:S(2)}) %copy-start.3) | copy-done | bytes 3932184
  11.4 8.8 %product.3 = (bf16[2,640,256]{2,1,0:T(8,128)(2,1)S(1)}, bf16[2,640,256]{2,1,0:T(8,128)(2,1)S(1)}, bf16[2,640,256]{2,1,0:T(8,128)(2,1)}, bf16[2,640,256]{2,1,0:T(...) custom-call(s32[3]{0:T(128)S(1)} %pad_add_fusion.1.place, ...), custom_call_target="tpu_custom_call" | custom-call | flops 4026531840 | bytes 11796480 | tf_op jit(solution)/shard_map/product/pallas_call | solution.py:77
  20.2 1.6 %collective-permute-start.2 = (bf16[2,640,256]{2,1,0:T(8,128)(2,1)}, bf16[2,640,256]{2,1,0:T(8,128)(2,1)}, u32[]{:S(2)}, u32[]{:S(2)}) collective-permute-start(bf16[2,640,256]{2,1,0:T(8,128)(2,1)} %get-tuple-element.37), channel_id=1, source_target_pairs={{0,64},{64,128},{128,192},{192,0},{1,65},{65,129},{129,193},{193,1... | collective-permute-start | bytes 1966088 | tf_op jit(solution)/shard_map/ppermute | solution.py:22
  21.8 1.6 %collective-permute-start.3 = (bf16[2,640,256]{2,1,0:T(8,128)(2,1)}, bf16[2,640,256]{2,1,0:T(8,128)(2,1)}, u32[]{:S(2)}, u32[]{:S(2)}) collective-permute-start(bf16[2,640,256]{2,1,0:T(8,128)(2,1)} %get-tuple-element.38), channel_id=1, source_target_pairs={{0,192},{64,0},{128,64},{192,128},{1,193},{65,1},{129,65},{193,129... | collective-permute-start | bytes 1966088 | tf_op jit(solution)/shard_map/ppermute | solution.py:22
  23.5 1.5 %collective-permute-start.4 = (bf16[4,320,256]{2,1,0:T(8,128)(2,1)}, bf16[4,320,256]{2,1,0:T(8,128)(2,1)}, u32[]{:S(2)}, u32[]{:S(2)}) collective-permute-start(bf16[4,320,256]{2,1,0:T(8,128)(2,1)} %get-tuple-element.39), channel_id=1, source_target_pairs={{0,2},{2,4},{4,6},{6,0},{1,3},{3,5},{5,7},{7,1},{8,10},{10,12},{12... | collective-permute-start | bytes 1966088 | tf_op jit(solution)/shard_map/ppermute | solution.py:22
  25.0 0.8 collective-permute-start.5
  25.8 0.1 reshape.143
  25.9 0.1 reshape.144
  26.0 0.1 pad_add_fusion.place
  26.1 2.2 %collective-permute-start.13 = (bf16[4,4,640]{2,1,0:T(4,128)(2,1)S(1)}, bf16[4,4,640]{2,1,0:T(4,128)(2,1)S(1)}, u32[]{:S(2)}, u32[]{:S(2)}) collective-permute-start(bf16[4,4,640]{2,1,0:T(4,128)(2,1)S(1)} %dynamic-slice_bitcast_fusion.4), channel_id=1, source_target_pairs={{0,4},{4,0},{1,5},{5,1},{2,6},{6,2},{3,7},{7,3},{8,12},{12,8},{9,1... | collective-permute-start | bytes 61448 | tf_op jit(solution)/shard_map/ppermute | solution.py:26
  28.3 2.1 %copy-done.4 = bf16[384,5120]{1,0:T(8,128)(2,1)S(1)} copy-done((bf16[384,5120]{1,0:T(8,128)(2,1)S(1)}, bf16[384,5120]{1,0:T(8,128)(2,1)}, u32[]{:S(2)}) %copy-start.4) | copy-done | bytes 3932184
  30.4 8.6 %product.2 = (bf16[2,640,256]{2,1,0:T(8,128)(2,1)S(1)}, bf16[2,640,256]{2,1,0:T(8,128)(2,1)S(1)}, bf16[2,640,256]{2,1,0:T(8,128)(2,1)S(1)}, bf16[2,640,256]{2,1,...) custom-call(s32[3]{0:T(128)S(1)} %pad_add_fusion.place, ...), custom_call_target="tpu_custom_call" | custom-call | flops 4026531840 | bytes 11796480 | tf_op jit(solution)/shard_map/product/pallas_call | solution.py:77
  39.0 2.6 %collective-permute-start.7 = (bf16[4,320,256]{2,1,0:T(8,128)(2,1)S(1)}, bf16[4,320,256]{2,1,0:T(8,128)(2,1)S(1)}, u32[]{:S(2)}, u32[]{:S(2)}) collective-permute-start(bf16[4,320,256]{2,1,0:T(8,128)(2,1)S(1)} %get-tuple-element.48), channel_id=1, source_target_pairs={{0,2},{2,4},{4,6},{6,0},{1,3},{3,5},{5,7},{7,1},{8,10},{10,12},{12... | collective-permute-start | bytes 1966088 | tf_op jit(solution)/shard_map/ppermute | solution.py:22
  41.6 0.1 collective-permute-start.14
  41.8 3.2 %collective-permute-start.12 = (bf16[2,640,256]{2,1,0:T(8,128)(2,1)S(1)}, bf16[2,640,256]{2,1,0:T(8,128)(2,1)S(1)}, u32[]{:S(2)}, u32[]{:S(2)}) collective-permute-start(bf16[2,640,256]{2,1,0:T(8,128)(2,1)S(1)} %get-tuple-element.57), channel_id=1, source_target_pairs={{0,192},{64,0},{128,64},{192,128},{1,193},{65,1},{129,65},{193,129... | collective-permute-start | bytes 1966088 | tf_op jit(solution)/shard_map/ppermute | solution.py:22
  45.0 2.1 %add_convert_fusion.3 = bf16[4,320,256]{2,1,0:T(8,128)(2,1)} fusion(bf16[4,320,256]{2,1,0:T(8,128)(2,1)} %collective-permute-done.5, bf16[4,320,256]{2,1,0:T(8,128)(2,1)S(1)} %get-tuple-element.50), kind=kLoop, calls=%fused_computation.4 | loop fusion | flops 1310720 | bytes 1966080 | tf_op jit(solution)/shard_map/convert_element_type | solution.py:34
  47.0 2.1 %add_convert_fusion.4 = bf16[4,320,256]{2,1,0:T(8,128)(2,1)} fusion(bf16[4,320,256]{2,1,0:T(8,128)(2,1)} %collective-permute-done.4, bf16[4,320,256]{2,1,0:T(8,128)(2,1)S(1)} %get-tuple-element.46), kind=kLoop, calls=%fused_computation.5 | loop fusion | flops 1310720 | bytes 1966080 | tf_op jit(solution)/shard_map/convert_element_type | solution.py:34
  49.1 2.1 %add_convert_fusion.2 = bf16[2,640,256]{2,1,0:T(8,128)(2,1)} fusion(bf16[2,640,256]{2,1,0:T(8,128)(2,1)} %collective-permute-done.2, bf16[2,640,256]{2,1,0:T(8,128)(2,1)S(1)} %get-tuple-element.52), kind=kLoop, calls=%fused_computation.3 | loop fusion | flops 1310720 | bytes 1966080 | tf_op jit(solution)/shard_map/convert_element_type | solution.py:34
  51.2 2.3 %collective-permute-start.9 = (bf16[4,320,256]{2,1,0:T(8,128)(2,1)}, bf16[4,320,256]{2,1,0:T(8,128)(2,1)S(1)}, u32[]{:S(2)}, u32[]{:S(2)}) collective-permute-start(bf16[4,320,256]{2,1,0:T(8,128)(2,1)} %add_convert_fusion.3), channel_id=1, source_target_pairs={{0,6},{2,0},{4,2},{6,4},{1,7},{3,1},{5,3},{7,5},{8,14},{10,8},{12,... | collective-permute-start | bytes 1966088 | tf_op jit(solution)/shard_map/ppermute | solution.py:22
  53.5 4.5 %collective-permute-done.14 = bf16[2,640,256]{2,1,0:T(8,128)(2,1)S(1)} collective-permute-done((bf16[2,640,256]{2,1,0:T(8,128)(2,1)S(1)}, bf16[2,640,256]{2,1,0:T(8,128)(2,1)S(1)}, u32[]{:S(2)}, u32[]{:S(2)}) %collective-permute-start.14) | collective-permute-done | bytes 655392 | tf_op jit(solution)/shard_map/ppermute | solution.py:22
  58.0 1.7 %collective-permute-start.6 = (bf16[4,320,256]{2,1,0:T(8,128)(2,1)}, bf16[4,320,256]{2,1,0:T(8,128)(2,1)}, u32[]{:S(2)}, u32[]{:S(2)}) collective-permute-start(bf16[4,320,256]{2,1,0:T(8,128)(2,1)} %add_convert_fusion.4), channel_id=1, source_target_pairs={{0,2},{2,4},{4,6},{6,0},{1,3},{3,5},{5,7},{7,1},{8,10},{10,12},{12... | collective-permute-start | bytes 1966088 | tf_op jit(solution)/shard_map/ppermute | solution.py:22
  59.7 0.6 pad_maximum_fusion.2
  60.4 1.0 add_convert_fusion.1
  61.4 0.9 copy-done.6
  62.3 3.2 %collective-permute-start.15 = (bf16[2,640,256]{2,1,0:T(8,128)(2,1)}, bf16[2,640,256]{2,1,0:T(8,128)(2,1)}, u32[]{:S(2)}, u32[]{:S(2)}) collective-permute-start(bf16[2,640,256]{2,1,0:T(8,128)(2,1)} %add_convert_fusion.1), channel_id=1, source_target_pairs={{0,192},{64,0},{128,64},{192,128},{1,193},{65,1},{129,65},{193,129... | collective-permute-start | bytes 1966088 | tf_op jit(solution)/shard_map/ppermute | solution.py:22
  65.6 5.4 %collective-permute-done.9 = bf16[4,320,256]{2,1,0:T(8,128)(2,1)S(1)} collective-permute-done((bf16[4,320,256]{2,1,0:T(8,128)(2,1)}, bf16[4,320,256]{2,1,0:T(8,128)(2,1)S(1)}, u32[]{:S(2)}, u32[]{:S(2)}) %collective-permute-start.9) | collective-permute-done | bytes 655392 | tf_op jit(solution)/shard_map/ppermute | solution.py:22
  71.0 2.7 %collective-permute-done.6 = bf16[4,320,256]{2,1,0:T(8,128)(2,1)} collective-permute-done((bf16[4,320,256]{2,1,0:T(8,128)(2,1)}, bf16[4,320,256]{2,1,0:T(8,128)(2,1)}, u32[]{:S(2)}, u32[]{:S(2)}) %collective-permute-start.6) | collective-permute-done | bytes 655392 | tf_op jit(solution)/shard_map/ppermute | solution.py:22
  73.7 1.2 collective-permute-done.10
  74.8 2.0 %add_convert_fusion = bf16[4,2,320,256]{3,2,0,1:T(8,128)(2,1)S(1)} fusion(bf16[4,1,320,256]{3,2,0,1:T(8,128)(2,1)S(1)} %bitcast.68, bf16[4,1,320,256]{3,2,0,1:T(8,128)(2,1)S(1)} %bitcast.67, bf16[4,1,320,256]{3,2,0,1:T(8,128)(2,1)} %bitcast.79, bf16[4,1,320,256]{3,2,0,1:T(8,128)(2,1)} %bitcast.20, bf16[4,1,320,256]{3,2,0,1:T(8,128)(2,1)S(1)} %bitcast.80, ...), kind=kLoop, calls=%fused_computation | loop fusion | flops 5898240 | bytes 5242880 | tf_op jit(solution)/shard_map/convert_element_type | solution.py:236
  76.8 0.1 copy.16
  76.9 1.0 dynamic-slice_bitcast_fusion.3
  78.0 1.3 collective-permute-start.19
  79.2 2.0 %collective-permute-start.20 = (bf16[640,256]{1,0:T(8,128)(2,1)}, bf16[640,256]{1,0:T(8,128)(2,1)}, u32[]{:S(2)}, u32[]{:S(2)}) collective-permute-start(bf16[640,256]{1,0:T(8,128)(2,1)} %get-tuple-element.73), channel_id=1, source_target_pairs={{0,192},{64,0},{128,64},{192,128},{1,193},{65,1},{129,65},{193,129... | collective-permute-start | bytes 983048 | tf_op jit(solution)/shard_map/ppermute | solution.py:22
  81.3 1.9 %fusion.6 = bf16[640,256]{1,0:T(8,128)(2,1)} fusion(bf16[2,640,256]{2,1,0:T(8,128)(2,1)} %collective-permute-done.3, s32[]{:T(128)S(6)} %select_n.111, bf16[2,640,256]{2,1,0:T(8,128)(2,1)} %collective-permute-done.10, bf16[2,640,256]{2,1,0:T(8,128)(2,1)S(1)} %get-tuple-element.45), kind=kLoop, calls=%fused_computation.21 | loop fusion | flops 983040 | bytes 1310724 | tf_op jit(solution)/shard_map/convert_element_type | solution.py:240
  83.2 3.6 %collective-permute-start.11 = (bf16[640,256]{1,0:T(8,128)(2,1)}, bf16[640,256]{1,0:T(8,128)(2,1)}, u32[]{:S(2)}, u32[]{:S(2)}) collective-permute-start(bf16[640,256]{1,0:T(8,128)(2,1)} %fusion.6), channel_id=1, source_target_pairs={{0,4},{2,6},{4,0},{6,2},{1,5},{3,7},{5,1},{7,3},{8,12},{10,14},{12... | collective-permute-start | bytes 983048 | tf_op jit(solution)/shard_map/ppermute | solution.py:22
  86.8 2.2 %fusion.7 = (bf16[640,256]{1,0:T(8,128)(2,1)}, bf16[640,256]{1,0:T(8,128)(2,1)}) fusion(bf16[2,640,256]{2,1,0:T(8,128)(2,1)} %collective-permute-done.15, s32[]{:T(128)S(6)} %select_n.114, bf16[2,640,256]{2,1,0:T(8,128)(2,1)S(1)} %copy-done.8, bf16[2,640,256]{2,1,0:T(8,128)(2,1)S(1)} %get-tuple-element.56, s32[]{:T(128)S(6)} %select_n.122), kind=kLoop, calls=%fused_computation.22 | loop fusion | flops 1966080 | bytes 2621448 | tf_op jit(solution)/shard_map/convert_element_type | solution.py:240
  89.0 0.1 collective-permute-start.16
  89.1 2.6 %collective-permute-start.17 = (bf16[640,256]{1,0:T(8,128)(2,1)}, bf16[640,256]{1,0:T(8,128)(2,1)}, u32[]{:S(2)}, u32[]{:S(2)}) collective-permute-start(bf16[640,256]{1,0:T(8,128)(2,1)} %get-tuple-element.71), channel_id=1, source_target_pairs={{0,6},{2,0},{4,2},{6,4},{1,7},{3,1},{5,3},{7,5},{8,14},{10,8},{12,... | collective-permute-start | bytes 983048 | tf_op jit(solution)/shard_map/ppermute | solution.py:22
  91.7 0.8 broadcast_in_dim.2
  92.5 8.5 %all-to-all-start = ((bf16[32,8,640]{2,1,0:T(8,128)(2,1)}), bf16[32,8,640]{2,1,0:T(8,128)(2,1)S(1)}, u32[]{:S(2)}, u32[]{:S(2)}) async-start(bf16[32,8,640]{2,1,0:T(8,128)(2,1)} %bitcast.30), calls=%async_computation | async-start | bytes 655360 | tf_op jit(solution)/shard_map/all_to_all | solution.py:210
  101.0 1.3 fusion.2
  102.4 1.5 %fusion.5 = bf16[640,256]{1,0:T(8,128)(2,1)S(1)} fusion(bf16[640,256]{1,0:T(8,128)(2,1)} %collective-permute-done.17, bf16[640,256]{1,0:T(8,128)(2,1)S(1)} %collective-permute-done.16, bf16[640,256]{1,0:T(8,128)(2,1)} %collective-permute-done.11, bf16[2,640,256]{2,1,0:T(8,128)(2,1)} %collective-permute-done.3, s32[]{:T(128)S(6)} %select_n.108, ...), kind=kLoop, calls=%fused_computation.17 | loop fusion | flops 1966080 | bytes 2293764 | tf_op jit(solution)/shard_map/convert_element_type | solution.py:242
  103.9 0.2 subtract_convert_fusion
  104.2 7.9 %all-to-all-done = bf16[32,8,640]{2,1,0:T(8,128)(2,1)S(1)} async-done(((bf16[32,8,640]{2,1,0:T(8,128)(2,1)}), bf16[32,8,640]{2,1,0:T(8,128)(2,1)S(1)}, u32[]{:S(2)}, u32[]{:S(2)}) %all-to-all-start) | async-done | bytes 327712 | tf_op jit(solution)/shard_map/all_to_all | solution.py:210
  112.1 0.4 convolution_convert_fusion
  112.5 0.1 copy.20
  112.6 0.8 reshape.149
  113.4 3.7 %all-to-all-start.1 = ((bf16[8,32,512]{2,1,0:T(8,128)(2,1)}), bf16[8,32,512]{2,1,0:T(8,128)(2,1)S(1)}, u32[]{:S(2)}, u32[]{:S(2)}) async-start(bf16[8,32,512]{2,1,0:T(8,128)(2,1)} %reshape.149), calls=%async_computation.1 | async-start | bytes 524288 | tf_op jit(solution)/shard_map/all_to_all | solution.py:250
  117.1 8.7 %all-to-all-done.1 = bf16[8,32,512]{2,1,0:T(8,128)(2,1)S(1)} async-done(((bf16[8,32,512]{2,1,0:T(8,128)(2,1)}), bf16[8,32,512]{2,1,0:T(8,128)(2,1)S(1)}, u32[]{:S(2)}, u32[]{:S(2)}) %all-to-all-start.1) | async-done | bytes 262176 | tf_op jit(solution)/shard_map/all_to_all | solution.py:250
  125.9 0.9 pad_maximum_fusion
  126.9 3.6 %all-to-all-start.2 = ((bf16[8,84,512]{2,1,0:T(8,128)(2,1)}), bf16[8,84,512]{2,1,0:T(8,128)(2,1)S(1)}, u32[]{:S(2)}, u32[]{:S(2)}) async-start(bf16[8,84,512]{2,1,0:T(8,128)(2,1)} %pad_maximum_fusion), calls=%async_computation.2 | async-start | bytes 1441792 | tf_op jit(solution)/shard_map/all_to_all | solution.py:254
  130.5 2.2 %copy-done = bf16[4,1024,512]{2,1,0:T(8,128)(2,1)S(1)} copy-done((bf16[4,1024,512]{2,1,0:T(8,128)(2,1)S(1)}, bf16[4,1024,512]{2,1,0:T(8,128)(2,1)}, u32[]{:S(2)}) %copy-start) | copy-done | bytes 4194328
  132.6 3.3 %past.1 = (f32[4,2,8,128]{3,2,1,0:T(8,128)S(1)}, f32[4,2,8,128]{3,2,1,0:T(8,128)S(1)}, f32[4,2,8,128]{3,2,1,0:T(8,128)S(1)}) custom-call(s32[4]{0:T(128)S(1)} %copy-done.2, bf16[4,2,8,128]{3,2,1,0:T(8,128)(2,1)S(1)} %pad.4.query_ref, bf16[4,1024,512]{2,1,0:T(8,128)(2,1)S(1)} %copy-done), custom_call_target="tpu_custom_call" | custom-call | flops 67108864 | bytes 4194304 | tf_op jit(solution)/shard_map/past/pallas_call | solution.py:117
  136.1 0.6 slice_bitcast_fusion.2.sum_ref
  136.7 0.6 slice_bitcast_fusion
  137.3 8.6 %all-to-all-done.2.parts_ref = bf16[8,84,512]{2,1,0:T(8,128)(2,1)S(1)} async-done(((bf16[8,84,512]{2,1,0:T(8,128)(2,1)}), bf16[8,84,512]{2,1,0:T(8,128)(2,1)S(1)}, u32[]{:S(2)}, u32[]{:S(2)}) %all-to-all-start.2) | async-done | bytes 688160 | tf_op jit(solution)/shard_map/all_to_all | solution.py:254
  145.9 0.9 copy-done.5
  146.7 2.0 %finish.1 = (bf16[80,512]{1,0:T(8,128)(2,1)}, bf16[4,1280]{1,0:T(4,128)(2,1)}) custom-call(bf16[80,512]{1,0:T(8,128)(2,1)} %weight_ref.1, bf16[4,1280]{1,0:T(4,128)(2,1)} %query_ref.1, f32[2,5,4,128]{3,2,1,0:T(4,128)} %slice_bitcast_fusion.2.sum_ref, f32[2,5,4,128]{3,2,1,0:T(4,128)} %get-tuple-element.78.top_ref, ...), custom_call_target="tpu_custom_call" | custom-call | tf_op jit(solution)/shard_map/finish/pallas_call | solution.py:257
  (53 shorter events, 0.4 us)
Async XLA Ops:
  0.6 7.2 %collective-permute-start = (bf16[384,5120]{1,0:T(8,128)(2,1)}, bf16[384,5120]{1,0:T(8,128)(2,1)}, u32[]{:S(2)}, u32[]{:S(2)}) collective-permute-start(bf16[384,5120]{1,0:T(8,128)(2,1)} %a_ref.3), channel_id=1, source_target_pairs={{0,1},{1,0},{2,3},{3,2},{4,5},{5,4},{6,7},{7,6},{8,9},{9,8},{10,11... | collective-permute-start | bytes 11796488 | tf_op jit(solution)/shard_map/ppermute | solution.py:26
  2.9 23.3 %collective-permute-start.1 = (bf16[2,384,512]{2,1,0:T(8,128)(2,1)}, bf16[2,384,512]{2,1,0:T(8,128)(2,1)}, u32[]{:S(2)}, u32[]{:S(2)}) collective-permute-start(bf16[2,384,512]{2,1,0:T(8,128)(2,1)} %dynamic-slice_bitcast_fusion), channel_id=1, source_target_pairs={{0,2},{2,0},{1,3},{3,1},{4,6},{6,4},{5,7},{7,5},{8,10},{10,8},{9,1... | collective-permute-start | bytes 2359304 | tf_op jit(solution)/shard_map/ppermute | solution.py:26
  7.8 1.4 copy-start.1
  9.3 2.1 %copy-start.3 = (bf16[384,5120]{1,0:T(8,128)(2,1)S(1)}, bf16[384,5120]{1,0:T(8,128)(2,1)}, u32[]{:S(2)}) copy-start(bf16[384,5120]{1,0:T(8,128)(2,1)} %a_ref.3) | copy-start | bytes 11796484
  11.4 14.4 %copy-start.12 = (bf16[4,1280]{1,0:T(4,128)(2,1)S(1)}, bf16[4,1280]{1,0:T(4,128)(2,1)}, u32[]{:S(2)}) copy-start(bf16[4,1280]{1,0:T(4,128)(2,1)} %query_ref.1) | copy-start | bytes 30724
  11.4 14.4 %copy-start.11 = (bf16[4,5120]{1,0:T(4,128)(2,1)S(1)}, bf16[4,5120]{1,0:T(4,128)(2,1)}, u32[]{:S(2)}) copy-start(bf16[4,5120]{1,0:T(4,128)(2,1)} %param.10) | copy-start | bytes 122884
  20.2 18.8 %collective-permute-start.2 = (bf16[2,640,256]{2,1,0:T(8,128)(2,1)}, bf16[2,640,256]{2,1,0:T(8,128)(2,1)}, u32[]{:S(2)}, u32[]{:S(2)}) collective-permute-start(bf16[2,640,256]{2,1,0:T(8,128)(2,1)} %get-tuple-element.37), channel_id=1, source_target_pairs={{0,64},{64,128},{128,192},{192,0},{1,65},{65,129},{129,193},{193,1... | collective-permute-start | bytes 1966088 | tf_op jit(solution)/shard_map/ppermute | solution.py:22
  21.8 19.8 %collective-permute-start.3 = (bf16[2,640,256]{2,1,0:T(8,128)(2,1)}, bf16[2,640,256]{2,1,0:T(8,128)(2,1)}, u32[]{:S(2)}, u32[]{:S(2)}) collective-permute-start(bf16[2,640,256]{2,1,0:T(8,128)(2,1)} %get-tuple-element.38), channel_id=1, source_target_pairs={{0,192},{64,0},{128,64},{192,128},{1,193},{65,1},{129,65},{193,129... | collective-permute-start | bytes 1966088 | tf_op jit(solution)/shard_map/ppermute | solution.py:22
  23.5 18.2 %collective-permute-start.4 = (bf16[4,320,256]{2,1,0:T(8,128)(2,1)}, bf16[4,320,256]{2,1,0:T(8,128)(2,1)}, u32[]{:S(2)}, u32[]{:S(2)}) collective-permute-start(bf16[4,320,256]{2,1,0:T(8,128)(2,1)} %get-tuple-element.39), channel_id=1, source_target_pairs={{0,2},{2,4},{4,6},{6,0},{1,3},{3,5},{5,7},{7,1},{8,10},{10,12},{12... | collective-permute-start | bytes 1966088 | tf_op jit(solution)/shard_map/ppermute | solution.py:22
  25.0 16.8 %collective-permute-start.5 = (bf16[4,320,256]{2,1,0:T(8,128)(2,1)}, bf16[4,320,256]{2,1,0:T(8,128)(2,1)}, u32[]{:S(2)}, u32[]{:S(2)}) collective-permute-start(bf16[4,320,256]{2,1,0:T(8,128)(2,1)} %get-tuple-element.40), channel_id=1, source_target_pairs={{0,6},{2,0},{4,2},{6,4},{1,7},{3,1},{5,3},{7,5},{8,14},{10,8},{12,... | collective-permute-start | bytes 1966088 | tf_op jit(solution)/shard_map/ppermute | solution.py:22
  26.1 25.1 %collective-permute-start.13 = (bf16[4,4,640]{2,1,0:T(4,128)(2,1)S(1)}, bf16[4,4,640]{2,1,0:T(4,128)(2,1)S(1)}, u32[]{:S(2)}, u32[]{:S(2)}) collective-permute-start(bf16[4,4,640]{2,1,0:T(4,128)(2,1)S(1)} %dynamic-slice_bitcast_fusion.4), channel_id=1, source_target_pairs={{0,4},{4,0},{1,5},{5,1},{2,6},{6,2},{3,7},{7,3},{8,12},{12,8},{9,1... | collective-permute-start | bytes 61448 | tf_op jit(solution)/shard_map/ppermute | solution.py:26
  28.3 2.1 %copy-start.4 = (bf16[384,5120]{1,0:T(8,128)(2,1)S(1)}, bf16[384,5120]{1,0:T(8,128)(2,1)}, u32[]{:S(2)}) copy-start(bf16[384,5120]{1,0:T(8,128)(2,1)} %a_ref.3) | copy-start | bytes 11796484
  39.0 22.4 %collective-permute-start.7 = (bf16[4,320,256]{2,1,0:T(8,128)(2,1)S(1)}, bf16[4,320,256]{2,1,0:T(8,128)(2,1)S(1)}, u32[]{:S(2)}, u32[]{:S(2)}) collective-permute-start(bf16[4,320,256]{2,1,0:T(8,128)(2,1)S(1)} %get-tuple-element.48), channel_id=1, source_target_pairs={{0,2},{2,4},{4,6},{6,0},{1,3},{3,5},{5,7},{7,1},{8,10},{10,12},{12... | collective-permute-start | bytes 1966088 | tf_op jit(solution)/shard_map/ppermute | solution.py:22
  41.6 23.9 %collective-permute-start.8 = (bf16[4,320,256]{2,1,0:T(8,128)(2,1)}, bf16[4,320,256]{2,1,0:T(8,128)(2,1)}, u32[]{:S(2)}, u32[]{:S(2)}) collective-permute-start(bf16[4,320,256]{2,1,0:T(8,128)(2,1)} %get-tuple-element.49), channel_id=1, source_target_pairs={{0,6},{2,0},{4,2},{6,4},{1,7},{3,1},{5,3},{7,5},{8,14},{10,8},{12,... | collective-permute-start | bytes 1966088 | tf_op jit(solution)/shard_map/ppermute | solution.py:22
  41.6 16.4 %collective-permute-start.14 = (bf16[2,640,256]{2,1,0:T(8,128)(2,1)S(1)}, bf16[2,640,256]{2,1,0:T(8,128)(2,1)S(1)}, u32[]{:S(2)}, u32[]{:S(2)}) collective-permute-start(bf16[2,640,256]{2,1,0:T(8,128)(2,1)S(1)} %get-tuple-element.59), channel_id=1, source_target_pairs={{0,64},{64,128},{128,192},{192,0},{1,65},{65,129},{129,193},{193,1... | collective-permute-start | bytes 1966088 | tf_op jit(solution)/shard_map/ppermute | solution.py:22
  41.8 17.9 %collective-permute-start.12 = (bf16[2,640,256]{2,1,0:T(8,128)(2,1)S(1)}, bf16[2,640,256]{2,1,0:T(8,128)(2,1)S(1)}, u32[]{:S(2)}, u32[]{:S(2)}) collective-permute-start(bf16[2,640,256]{2,1,0:T(8,128)(2,1)S(1)} %get-tuple-element.57), channel_id=1, source_target_pairs={{0,192},{64,0},{128,64},{192,128},{1,193},{65,1},{129,65},{193,129... | collective-permute-start | bytes 1966088 | tf_op jit(solution)/shard_map/ppermute | solution.py:22
  51.2 19.7 %collective-permute-start.9 = (bf16[4,320,256]{2,1,0:T(8,128)(2,1)}, bf16[4,320,256]{2,1,0:T(8,128)(2,1)S(1)}, u32[]{:S(2)}, u32[]{:S(2)}) collective-permute-start(bf16[4,320,256]{2,1,0:T(8,128)(2,1)} %add_convert_fusion.3), channel_id=1, source_target_pairs={{0,6},{2,0},{4,2},{6,4},{1,7},{3,1},{5,3},{7,5},{8,14},{10,8},{12,... | collective-permute-start | bytes 1966088 | tf_op jit(solution)/shard_map/ppermute | solution.py:22
  58.0 3.4 %copy-start.7 = (bf16[2,640,256]{2,1,0:T(8,128)(2,1)}, bf16[2,640,256]{2,1,0:T(8,128)(2,1)S(1)}, u32[]{:S(2)}) copy-start(bf16[2,640,256]{2,1,0:T(8,128)(2,1)S(1)} %collective-permute-done.14) | copy-start | bytes 1966084
  58.0 15.6 %collective-permute-start.6 = (bf16[4,320,256]{2,1,0:T(8,128)(2,1)}, bf16[4,320,256]{2,1,0:T(8,128)(2,1)}, u32[]{:S(2)}, u32[]{:S(2)}) collective-permute-start(bf16[4,320,256]{2,1,0:T(8,128)(2,1)} %add_convert_fusion.4), channel_id=1, source_target_pairs={{0,2},{2,4},{4,6},{6,0},{1,3},{3,5},{5,7},{7,1},{8,10},{10,12},{12... | collective-permute-start | bytes 1966088 | tf_op jit(solution)/shard_map/ppermute | solution.py:22
  59.7 15.1 %collective-permute-start.10 = (bf16[2,640,256]{2,1,0:T(8,128)(2,1)}, bf16[2,640,256]{2,1,0:T(8,128)(2,1)}, u32[]{:S(2)}, u32[]{:S(2)}) collective-permute-start(bf16[2,640,256]{2,1,0:T(8,128)(2,1)} %add_convert_fusion.2), channel_id=1, source_target_pairs={{0,64},{64,128},{128,192},{192,0},{1,65},{65,129},{129,193},{193,1... | collective-permute-start | bytes 1966088 | tf_op jit(solution)/shard_map/ppermute | solution.py:22
  61.4 0.9 copy-start.6
  62.3 24.5 %collective-permute-start.15 = (bf16[2,640,256]{2,1,0:T(8,128)(2,1)}, bf16[2,640,256]{2,1,0:T(8,128)(2,1)}, u32[]{:S(2)}, u32[]{:S(2)}) collective-permute-start(bf16[2,640,256]{2,1,0:T(8,128)(2,1)} %add_convert_fusion.1), channel_id=1, source_target_pairs={{0,192},{64,0},{128,64},{192,128},{1,193},{65,1},{129,65},{193,129... | collective-permute-start | bytes 1966088 | tf_op jit(solution)/shard_map/ppermute | solution.py:22
  76.9 1.0 copy-start.9
  77.9 8.9 %copy-start.8 = (bf16[2,640,256]{2,1,0:T(8,128)(2,1)S(1)}, bf16[2,640,256]{2,1,0:T(8,128)(2,1)}, u32[]{:S(2)}) copy-start(bf16[2,640,256]{2,1,0:T(8,128)(2,1)} %copy-done.7) | copy-start | bytes 1966084
  77.9 11.2 %collective-permute-start.18 = (bf16[640,256]{1,0:T(8,128)(2,1)}, bf16[640,256]{1,0:T(8,128)(2,1)}, u32[]{:S(2)}, u32[]{:S(2)}) collective-permute-start(bf16[640,256]{1,0:T(8,128)(2,1)} %get-tuple-element.72), channel_id=1, source_target_pairs={{0,128},{64,192},{128,0},{192,64},{1,129},{65,193},{129,1},{193,65... | collective-permute-start | bytes 983048 | tf_op jit(solution)/shard_map/ppermute | solution.py:22
  78.0 23.1 %collective-permute-start.19 = (bf16[640,256]{1,0:T(8,128)(2,1)}, bf16[640,256]{1,0:T(8,128)(2,1)}, u32[]{:S(2)}, u32[]{:S(2)}) collective-permute-start(bf16[640,256]{1,0:T(8,128)(2,1)} %get-tuple-element.74), channel_id=1, source_target_pairs={{0,64},{64,128},{128,192},{192,0},{1,65},{65,129},{129,193},{193,1... | collective-permute-start | bytes 983048 | tf_op jit(solution)/shard_map/ppermute | solution.py:22
  79.2 21.8 %collective-permute-start.20 = (bf16[640,256]{1,0:T(8,128)(2,1)}, bf16[640,256]{1,0:T(8,128)(2,1)}, u32[]{:S(2)}, u32[]{:S(2)}) collective-permute-start(bf16[640,256]{1,0:T(8,128)(2,1)} %get-tuple-element.73), channel_id=1, source_target_pairs={{0,192},{64,0},{128,64},{192,128},{1,193},{65,1},{129,65},{193,129... | collective-permute-start | bytes 983048 | tf_op jit(solution)/shard_map/ppermute | solution.py:22
  83.2 19.2 %collective-permute-start.11 = (bf16[640,256]{1,0:T(8,128)(2,1)}, bf16[640,256]{1,0:T(8,128)(2,1)}, u32[]{:S(2)}, u32[]{:S(2)}) collective-permute-start(bf16[640,256]{1,0:T(8,128)(2,1)} %fusion.6), channel_id=1, source_target_pairs={{0,4},{2,6},{4,0},{6,2},{1,5},{3,7},{5,1},{7,3},{8,12},{10,14},{12... | collective-permute-start | bytes 983048 | tf_op jit(solution)/shard_map/ppermute | solution.py:22
  86.8 4.9 %copy-start.10 = (bf16[4,8,640]{2,1,0:T(8,128)(2,1)S(1)}, bf16[4,8,640]{2,1,0:T(8,128)(2,1)}, u32[]{:S(2)}) copy-start(bf16[4,8,640]{2,1,0:T(8,128)(2,1)} %pad_maximum_fusion.2) | copy-start | bytes 122884
  89.0 13.4 %collective-permute-start.16 = (bf16[640,256]{1,0:T(8,128)(2,1)}, bf16[640,256]{1,0:T(8,128)(2,1)S(1)}, u32[]{:S(2)}, u32[]{:S(2)}) collective-permute-start(bf16[640,256]{1,0:T(8,128)(2,1)} %get-tuple-element.70), channel_id=1, source_target_pairs={{0,2},{2,4},{4,6},{6,0},{1,3},{3,5},{5,7},{7,1},{8,10},{10,12},{12... | collective-permute-start | bytes 983048 | tf_op jit(solution)/shard_map/ppermute | solution.py:22
  89.1 13.3 %collective-permute-start.17 = (bf16[640,256]{1,0:T(8,128)(2,1)}, bf16[640,256]{1,0:T(8,128)(2,1)}, u32[]{:S(2)}, u32[]{:S(2)}) collective-permute-start(bf16[640,256]{1,0:T(8,128)(2,1)} %get-tuple-element.71), channel_id=1, source_target_pairs={{0,6},{2,0},{4,2},{6,4},{1,7},{3,1},{5,3},{7,5},{8,14},{10,8},{12,... | collective-permute-start | bytes 983048 | tf_op jit(solution)/shard_map/ppermute | solution.py:22
  92.5 19.6 %all-to-all-start = ((bf16[32,8,640]{2,1,0:T(8,128)(2,1)}), bf16[32,8,640]{2,1,0:T(8,128)(2,1)S(1)}, u32[]{:S(2)}, u32[]{:S(2)}) async-start(bf16[32,8,640]{2,1,0:T(8,128)(2,1)} %bitcast.30), calls=%async_computation | async-start | bytes 655360 | tf_op jit(solution)/shard_map/all_to_all | solution.py:210
  113.4 12.5 %all-to-all-start.1 = ((bf16[8,32,512]{2,1,0:T(8,128)(2,1)}), bf16[8,32,512]{2,1,0:T(8,128)(2,1)S(1)}, u32[]{:S(2)}, u32[]{:S(2)}) async-start(bf16[8,32,512]{2,1,0:T(8,128)(2,1)} %reshape.149), calls=%async_computation.1 | async-start | bytes 524288 | tf_op jit(solution)/shard_map/all_to_all | solution.py:250
  125.9 4.5 %copy-start.2 = (s32[4]{0:T(128)S(1)}, s32[4]{0:T(128)}, u32[]{:S(2)}) copy-start(s32[4]{0:T(128)} %lengths.1) | copy-start | bytes 52
  126.9 19.0 %all-to-all-start.2 = ((bf16[8,84,512]{2,1,0:T(8,128)(2,1)}), bf16[8,84,512]{2,1,0:T(8,128)(2,1)S(1)}, u32[]{:S(2)}, u32[]{:S(2)}) async-start(bf16[8,84,512]{2,1,0:T(8,128)(2,1)} %pad_maximum_fusion), calls=%async_computation.2 | async-start | bytes 1441792 | tf_op jit(solution)/shard_map/all_to_all | solution.py:254
  130.5 2.2 %copy-start = (bf16[4,1024,512]{2,1,0:T(8,128)(2,1)S(1)}, bf16[4,1024,512]{2,1,0:T(8,128)(2,1)}, u32[]{:S(2)}) copy-start(bf16[4,1024,512]{2,1,0:T(8,128)(2,1)} %cache_ref.1) | copy-start | bytes 12582916
  145.9 0.9 copy-start.5

commit v5 on v4

--- a/solution.py
+++ b/solution.py
@@ -35,13 +35,27 @@
 
 
 def product_kernel(rows, place, a_ref, b_ref, ca_ref, cb_ref, *outs):
+    values = jnp.concatenate([a_ref[...], b_ref[...]], axis=0)
+    cots = jnp.concatenate([ca_ref[...], cb_ref[...]], axis=0)
+    store(rows, place, tokens_by(values, cots).astype(BF16), outs)
+
+
+def rest_kernel(rows, place, head_ref, b_ref, cb_ref, *outs):
+    total = tokens_by(b_ref[...], cb_ref[...]) + head_ref[...].astype(F32)
+    store(rows, place, total.astype(BF16), outs)
+
+
+def head_kernel(place, a_ref, ca_ref, out_ref):
+    out_ref[...] = tokens_by(a_ref[...], ca_ref[...]).astype(BF16)
+
+
+def tokens_by(values, cots):
+    return lax.dot_general(values, cots, (((0,), (0,)), ((), ())), preferred_element_type=F32)
+
+
+def store(rows, place, total, outs):
     by_y, near, far = outs[:4], outs[4:6], outs[6:]
     turn = pl.program_id(0)
-    values = jnp.concatenate([a_ref[...], b_ref[...]], axis=0)
-    cots = jnp.concatenate([ca_ref[...], cb_ref[...]], axis=0)
-    total = lax.dot_general(
-        values, cots, (((0,), (0,)), ((), ())), preferred_element_type=F32
-    ).astype(BF16)
     part = total.shape[1] // 2
     pieces = total.shape[0] // rows
     for k in range(4):
@@ -62,7 +76,7 @@
                 out[0, j * rows : (j + 1) * rows, :] = total[i * rows : (i + 1) * rows, part:]
 
 
-def product(rows, place, own, other, cots):
+def product(rows, place, own, other, cots, head=None):
     tokens, width = own.shape
     columns = cots.shape[2]
     part = columns // 2
@@ -70,25 +84,35 @@
     token_spec = pl.BlockSpec((tokens, tall), lambda t, place: (0, (place[0] + t) % 4))
     first_cot = pl.BlockSpec((None, tokens, columns), lambda t, place: (place[2], 0, 0))
     second_cot = pl.BlockSpec((None, tokens, columns), lambda t, place: (place[2] ^ 1, 0, 0))
+    head_spec = pl.BlockSpec((tall, columns), lambda t, place: ((place[0] + t) % 4, 0))
     y_spec = pl.BlockSpec((2, tall // 2, part), lambda t, place: (0, 0, 0))
     y_shape = jax.ShapeDtypeStruct((2, tall // 2, part), BF16)
     x_spec = pl.BlockSpec((1, tall // 4, part), lambda t, place: ((place[0] + t) % 4, 0, 0))
     x_shape = jax.ShapeDtypeStruct((4, tall // 4, part), BF16)
+    out_specs, out_shape = [y_spec] * 4 + [x_spec] * 4, [y_shape] * 4 + [x_shape] * 4
+    kernel, name, share = functools.partial(product_kernel, rows), "product", 2
+    in_specs, args = [token_spec, token_spec, first_cot, second_cot], (own, other, cots, cots)
+    if head is not None:
+        kernel, name, share = functools.partial(rest_kernel, rows), "rest", 1
+        in_specs, args = [head_spec, token_spec, second_cot], (head, other, cots)
+    elif other is None:
+        kernel, name, share = head_kernel, "head", 1
+        in_specs, args = [token_spec, first_cot], (own, cots)
+        out_specs, out_shape = head_spec, jax.ShapeDtypeStruct((width, columns), BF16)
     return pl.pallas_call(
-        functools.partial(product_kernel, rows),
+        kernel,
         grid_spec=pltpu.PrefetchScalarGridSpec(
-            num_scalar_prefetch=1,
-            grid=(4,),
-            in_specs=[token_spec, token_spec, first_cot, second_cot],
-            out_specs=[y_spec] * 4 + [x_spec] * 4,
+            num_scalar_prefetch=1, grid=(4,), in_specs=in_specs, out_specs=out_specs
         ),
-        out_shape=[y_shape] * 4 + [x_shape] * 4,
+        out_shape=out_shape,
         compiler_params=pltpu.CompilerParams(vmem_limit_bytes=32 << 20),
         cost_estimate=pl.CostEstimate(
-            flops=4 * tokens * width * columns, bytes_accessed=6 * tokens * width, transcendentals=0
+            flops=2 * share * tokens * width * columns,
+            bytes_accessed=6 * tokens * width,
+            transcendentals=0,
         ),
-        name="product",
-    )(place, own, other, cots, cots)
+        name=name,
+    )(place, *args)
 
 
 def past_kernel(heads, lengths, query_ref, cache_ref, sum_ref, top_ref, mass_ref):
@@ -187,9 +211,9 @@
     )
 
     place = jnp.stack([y, xh, xl * nc + c]).astype(jnp.int32)
-    own = product(
-        rows, place, tokens_in, other_tokens, cotangent.reshape(nl * nc, tokens, columns)
-    )
+    own_cots = cotangent.reshape(nl * nc, tokens, columns)
+    head = product(rows, place, tokens_in, None, own_cots)
+    own = product(rows, place, tokens_in, other_tokens, own_cots, head)
     own_y, (own_x0a, own_x0b, own_x2a, own_x2b) = own[:4], own[4:]
     up = shift(own_y[2], "y", ny, 1)
     down = shift(own_y[3], "y", ny, -1)

time: 150 us -> 150 us (level)
  starting transfers between devices: 48.6 us -> 43.2 us
  Pallas kernels: 22.8 us -> 25.9 us
  waiting for transfers between devices: 41.6 us -> 43.7 us
    ppermute x18, starting transfers between devices: 28.3 us -> 22.1 us  [shift(): lax.ppermute(value, axis, [(i, (i + by) % size) for i in range(size)])]
    ppermute x18, waiting for transfers between devices: 13.8 us -> 18.4 us  [shift(): lax.ppermute(value, axis, [(i, (i + by) % size) for i in range(size)])]
    pallas_call x2 -> x3, Pallas kernels: 17.4 us -> 20.6 us  [product(): pl.pallas_call(kernel, grid_spec=pltpu.PrefetchScalarGridSpec(num_scalar_...]
    ppermute x3, waiting for transfers between devices: 2.64 us -> 0.01 us  [swap(): return lax.ppermute(value, axis, [(i, i ^ bits) for i in range(size)])]
    all_to_all x1, starting transfers between devices: 8.51 us -> 10.6 us  [local(): lax.all_to_all(held.reshape(ny * nz, nh * count, nz * rows), ('y', 'z'),...]
  transfers between devices with their start and end apart: 24 -> 24, of which waited for: 8 -> 8; matrix products, arithmetic and copies ran while one was open for 15% -> 16% of each run, Pallas kernels for 14% -> 16%
where the time goes in v5:
time: 150 us; the launch traced here: 149 us
  waiting for transfers between devices  43.7 us (29%)
  starting transfers between devices  43.2 us (29%)
  Pallas kernels  25.9 us (17%)
  other arithmetic  18.3 us (12%)
  local copies, waits for them, and re-layouts  15.5 us (10%)
    ppermute x18, starting transfers between devices, shift(): lax.ppermute(value, axis, [(i, (i + by) % size) for i in range(size)])  22.1 us
    pallas_call x3, Pallas kernels, product(): pl.pallas_call(kernel, grid_spec=pltpu.PrefetchScalarGridSpec(num_scalar_...  20.6 us
    ppermute x18, waiting for transfers between devices, shift(): lax.ppermute(value, axis, [(i, (i + by) % size) for i in range(size)])  18.4 us
    all_to_all x1, starting transfers between devices, local(): lax.all_to_all(held.reshape(ny * nz, nh * count, nz * rows), ('y', 'z'),...  10.6 us
    all_to_all x1, waiting for transfers between devices, local(): lax.all_to_all(fresh.reshape(ny * nh, nz * count, columns), ('y', 'xh'),...  8.67 us
    all_to_all x1, waiting for transfers between devices, local(): lax.all_to_all(jnp.concatenate([both, fresh], axis=1), 'z', 0, 0, tiled=T...  8.62 us
    unnamed x26, local copies, waits for them, and re-layouts  8.17 us
    all_to_all x1, waiting for transfers between devices, local(): lax.all_to_all(held.reshape(ny * nz, nh * count, nz * rows), ('y', 'z'),...  7.99 us
  transfers between devices with their start and end apart: 24, of which 8 were waited for; matrix products, arithmetic and copies ran while one was open for 16% of the time, Pallas kernels for 16%

profile of v5, /device:TPU:2, one launch (start us, length us, event | category | flops | bytes accessed | tf_op | source)
XLA Modules:
  0.0 149.0 jit_solution(10848259001106957460)
XLA Ops:
  0.6 0.1 collective-permute-start
  0.7 2.2 %dynamic-slice_bitcast_fusion = bf16[2,384,512]{2,1,0:T(8,128)(2,1)} fusion(bf16[2,2,384,512]{3,2,1,0:T(8,128)(2,1)} %bitcast.67, s32[]{:T(128)S(6)} %select_n.105), kind=kLoop, calls=%fused_computation.7 | loop fusion | bytes 1572868 | tf_op jit(solution)/shard_map/jit(dynamic_index_in_dim)/squeeze | solution.py:30
  3.0 2.3 %collective-permute-start.1 = (bf16[2,384,512]{2,1,0:T(8,128)(2,1)}, bf16[2,384,512]{2,1,0:T(8,128)(2,1)}, u32[]{:S(2)}, u32[]{:S(2)}) collective-permute-start(bf16[2,384,512]{2,1,0:T(8,128)(2,1)} %dynamic-slice_bitcast_fusion), channel_id=1, source_target_pairs={{0,2},{2,0},{1,3},{3,1},{4,6},{6,4},{5,7},{7,5},{8,10},{10,8},{9,1... | collective-permute-start | bytes 2359304 | tf_op jit(solution)/shard_map/ppermute | solution.py:26
  5.3 0.1 pad_add_fusion.1.place
  5.3 2.1 %copy-done.2 = bf16[384,5120]{1,0:T(8,128)(2,1)S(1)} copy-done((bf16[384,5120]{1,0:T(8,128)(2,1)S(1)}, bf16[384,5120]{1,0:T(8,128)(2,1)}, u32[]{:S(2)}) %copy-start.2) | copy-done | bytes 3932184
  7.5 4.4 %head.1.head_ref = bf16[5120,512]{1,0:T(8,128)(2,1)S(1)} custom-call(s32[3]{0:T(128)S(1)} %pad_add_fusion.1.place, bf16[384,5120]{1,0:T(8,128)(2,1)S(1)} %copy-done.2, bf16[4,384,512]{2,1,0:T(8,128)(2,1)S(1)} %bitcast.68), custom_call_target="tpu_custom_call" | custom-call | flops 2013265920 | bytes 11796480 | tf_op jit(solution)/shard_map/head/pallas_call | solution.py:102
  11.9 7.5 %rest.1 = (bf16[2,640,256]{2,1,0:T(8,128)(2,1)S(1)}, bf16[2,640,256]{2,1,0:T(8,128)(2,1)S(1)}, bf16[2,640,256]{2,1,0:T(8,128)(2,1)}, bf16[2,640,256]{2,1,0:T(8,1...) custom-call(s32[3]{0:T(128)S(1)} %pad_add_fusion.1.place, ...), custom_call_target="tpu_custom_call" | custom-call | flops 2013265920 | bytes 11796480 | tf_op jit(solution)/shard_map/rest/pallas_call | solution.py:102
  19.5 0.9 copy-done.4
  20.3 3.2 %collective-permute-start.3 = (bf16[2,640,256]{2,1,0:T(8,128)(2,1)}, bf16[2,640,256]{2,1,0:T(8,128)(2,1)}, u32[]{:S(2)}, u32[]{:S(2)}) collective-permute-start(bf16[2,640,256]{2,1,0:T(8,128)(2,1)} %get-tuple-element.38), channel_id=1, source_target_pairs={{0,192},{64,0},{128,64},{192,128},{1,193},{65,1},{129,65},{193,129... | collective-permute-start | bytes 1966088 | tf_op jit(solution)/shard_map/ppermute | solution.py:22
  23.6 0.4 collective-permute-start.4
  24.0 1.6 %collective-permute-start.5 = (bf16[4,320,256]{2,1,0:T(8,128)(2,1)}, bf16[4,320,256]{2,1,0:T(8,128)(2,1)}, u32[]{:S(2)}, u32[]{:S(2)}) collective-permute-start(bf16[4,320,256]{2,1,0:T(8,128)(2,1)} %get-tuple-element.40), channel_id=1, source_target_pairs={{0,6},{2,0},{4,2},{6,4},{1,7},{3,1},{5,3},{7,5},{8,14},{10,8},{12,... | collective-permute-start | bytes 1966088 | tf_op jit(solution)/shard_map/ppermute | solution.py:22
  25.6 0.9 reshape.143
  26.5 0.1 reshape.144
  26.7 0.1 pad_add_fusion.place
  26.8 0.8 collective-permute-start.13
  27.6 2.1 %copy-done.3 = bf16[384,5120]{1,0:T(8,128)(2,1)S(1)} copy-done((bf16[384,5120]{1,0:T(8,128)(2,1)S(1)}, bf16[384,5120]{1,0:T(8,128)(2,1)}, u32[]{:S(2)}) %copy-start.3) | copy-done | bytes 3932184
  29.7 8.6 %product.1 = (bf16[2,640,256]{2,1,0:T(8,128)(2,1)S(1)}, bf16[2,640,256]{2,1,0:T(8,128)(2,1)S(1)}, bf16[2,640,256]{2,1,0:T(8,128)(2,1)S(1)}, bf16[2,640,256]{2,1,...) custom-call(s32[3]{0:T(128)S(1)} %pad_add_fusion.place, ...), custom_call_target="tpu_custom_call" | custom-call | flops 4026531840 | bytes 11796480 | tf_op jit(solution)/shard_map/product/pallas_call | solution.py:102
  38.3 0.3 collective-permute-done.2
  38.6 1.7 %collective-permute-start.7 = (bf16[4,320,256]{2,1,0:T(8,128)(2,1)S(1)}, bf16[4,320,256]{2,1,0:T(8,128)(2,1)}, u32[]{:S(2)}, u32[]{:S(2)}) collective-permute-start(bf16[4,320,256]{2,1,0:T(8,128)(2,1)S(1)} %get-tuple-element.48), channel_id=1, source_target_pairs={{0,2},{2,4},{4,6},{6,0},{1,3},{3,5},{5,7},{7,1},{8,10},{10,12},{12... | collective-permute-start | bytes 1966088 | tf_op jit(solution)/shard_map/ppermute | solution.py:22
  40.3 0.4 collective-permute-start.8
  40.6 0.1 collective-permute-start.14
  40.7 3.2 %collective-permute-start.12 = (bf16[2,640,256]{2,1,0:T(8,128)(2,1)S(1)}, bf16[2,640,256]{2,1,0:T(8,128)(2,1)S(1)}, u32[]{:S(2)}, u32[]{:S(2)}) collective-permute-start(bf16[2,640,256]{2,1,0:T(8,128)(2,1)S(1)} %get-tuple-element.57), channel_id=1, source_target_pairs={{0,192},{64,0},{128,64},{192,128},{1,193},{65,1},{129,65},{193,129... | collective-permute-start | bytes 1966088 | tf_op jit(solution)/shard_map/ppermute | solution.py:22
  43.9 2.1 %add_convert_fusion.2 = bf16[2,640,256]{2,1,0:T(8,128)(2,1)} fusion(bf16[2,640,256]{2,1,0:T(8,128)(2,1)} %collective-permute-done.2, bf16[2,640,256]{2,1,0:T(8,128)(2,1)S(1)} %copy-done.5), kind=kLoop, calls=%fused_computation.3 | loop fusion | flops 1310720 | bytes 1966080 | tf_op jit(solution)/shard_map/convert_element_type | solution.py:34
  46.0 2.1 %add_convert_fusion.3 = bf16[4,320,256]{2,1,0:T(8,128)(2,1)} fusion(bf16[4,320,256]{2,1,0:T(8,128)(2,1)} %collective-permute-done.5, bf16[4,320,256]{2,1,0:T(8,128)(2,1)S(1)} %get-tuple-element.50), kind=kLoop, calls=%fused_computation.4 | loop fusion | flops 1310720 | bytes 1966080 | tf_op jit(solution)/shard_map/convert_element_type | solution.py:34
  48.1 2.2 %add_convert_fusion.4 = bf16[4,320,256]{2,1,0:T(8,128)(2,1)} fusion(bf16[4,320,256]{2,1,0:T(8,128)(2,1)} %collective-permute-done.4, bf16[4,320,256]{2,1,0:T(8,128)(2,1)S(1)} %get-tuple-element.46), kind=kLoop, calls=%fused_computation.5 | loop fusion | flops 1310720 | bytes 1966080 | tf_op jit(solution)/shard_map/convert_element_type | solution.py:34
  50.3 9.2 %collective-permute-done.14 = bf16[2,640,256]{2,1,0:T(8,128)(2,1)S(1)} collective-permute-done((bf16[2,640,256]{2,1,0:T(8,128)(2,1)S(1)}, bf16[2,640,256]{2,1,0:T(8,128)(2,1)S(1)}, u32[]{:S(2)}, u32[]{:S(2)}) %collective-permute-start.14) | collective-permute-done | bytes 655392 | tf_op jit(solution)/shard_map/ppermute | solution.py:22
  59.5 2.7 %collective-permute-start.9 = (bf16[4,320,256]{2,1,0:T(8,128)(2,1)}, bf16[4,320,256]{2,1,0:T(8,128)(2,1)S(1)}, u32[]{:S(2)}, u32[]{:S(2)}) collective-permute-start(bf16[4,320,256]{2,1,0:T(8,128)(2,1)} %add_convert_fusion.3), channel_id=1, source_target_pairs={{0,6},{2,0},{4,2},{6,4},{1,7},{3,1},{5,3},{7,5},{8,14},{10,8},{12,... | collective-permute-start | bytes 1966088 | tf_op jit(solution)/shard_map/ppermute | solution.py:22
  62.2 0.6 pad_maximum_fusion.2
  62.9 1.0 add_convert_fusion.1
  63.9 0.6 collective-permute-start.15
  64.5 6.8 %collective-permute-done.10 = bf16[2,640,256]{2,1,0:T(8,128)(2,1)} collective-permute-done((bf16[2,640,256]{2,1,0:T(8,128)(2,1)}, bf16[2,640,256]{2,1,0:T(8,128)(2,1)}, u32[]{:S(2)}, u32[]{:S(2)}) %collective-permute-start.10) | collective-permute-done | bytes 655392 | tf_op jit(solution)/shard_map/ppermute | solution.py:22
  71.3 0.5 collective-permute-done.9
  71.8 1.6 %collective-permute-done.6 = bf16[4,320,256]{2,1,0:T(8,128)(2,1)} collective-permute-done((bf16[4,320,256]{2,1,0:T(8,128)(2,1)}, bf16[4,320,256]{2,1,0:T(8,128)(2,1)}, u32[]{:S(2)}, u32[]{:S(2)}) %collective-permute-start.6) | collective-permute-done | bytes 655392 | tf_op jit(solution)/shard_map/ppermute | solution.py:22
  73.4 2.0 %add_convert_fusion = bf16[4,2,320,256]{3,2,0,1:T(8,128)(2,1)S(1)} fusion(bf16[4,1,320,256]{3,2,0,1:T(8,128)(2,1)S(1)} %bitcast.71, bf16[4,1,320,256]{3,2,0,1:T(8,128)(2,1)S(1)} %bitcast.70, bf16[4,1,320,256]{3,2,0,1:T(8,128)(2,1)} %bitcast.21, bf16[4,1,320,256]{3,2,0,1:T(8,128)(2,1)} %bitcast.20, bf16[4,1,320,256]{3,2,0,1:T(8,128)(2,1)S(1)} %bitcast.79, ...), kind=kLoop, calls=%fused_computation | loop fusion | flops 5898240 | bytes 5242880 | tf_op jit(solution)/shard_map/convert_element_type | solution.py:260
  75.3 0.1 copy.16
  75.4 1.0 dynamic-slice_bitcast_fusion.3
  76.4 0.7 collective-permute-start.18
  77.2 1.4 collective-permute-start.19
  78.6 1.9 %collective-permute-start.20 = (bf16[640,256]{1,0:T(8,128)(2,1)}, bf16[640,256]{1,0:T(8,128)(2,1)}, u32[]{:S(2)}, u32[]{:S(2)}) collective-permute-start(bf16[640,256]{1,0:T(8,128)(2,1)} %get-tuple-element.73), channel_id=1, source_target_pairs={{0,192},{64,0},{128,64},{192,128},{1,193},{65,1},{129,65},{193,129... | collective-permute-start | bytes 983048 | tf_op jit(solution)/shard_map/ppermute | solution.py:22
  80.5 1.9 %fusion.6 = bf16[640,256]{1,0:T(8,128)(2,1)} fusion(bf16[2,640,256]{2,1,0:T(8,128)(2,1)} %collective-permute-done.3, s32[]{:T(128)S(6)} %select_n.111, bf16[2,640,256]{2,1,0:T(8,128)(2,1)} %collective-permute-done.10, bf16[2,640,256]{2,1,0:T(8,128)(2,1)S(1)} %get-tuple-element.45), kind=kLoop, calls=%fused_computation.21 | loop fusion | flops 983040 | bytes 1310724 | tf_op jit(solution)/shard_map/convert_element_type | solution.py:264
  82.4 0.9 collective-permute-start.11
  83.3 2.2 %fusion.7 = (bf16[640,256]{1,0:T(8,128)(2,1)}, bf16[640,256]{1,0:T(8,128)(2,1)}) fusion(bf16[2,640,256]{2,1,0:T(8,128)(2,1)} %collective-permute-done.15, s32[]{:T(128)S(6)} %select_n.114, bf16[2,640,256]{2,1,0:T(8,128)(2,1)S(1)} %copy-done.9, bf16[2,640,256]{2,1,0:T(8,128)(2,1)S(1)} %get-tuple-element.56, s32[]{:T(128)S(6)} %select_n.122), kind=kLoop, calls=%fused_computation.22 | loop fusion | flops 1966080 | bytes 2621448 | tf_op jit(solution)/shard_map/convert_element_type | solution.py:264
  85.5 2.8 %collective-permute-start.16 = (bf16[640,256]{1,0:T(8,128)(2,1)}, bf16[640,256]{1,0:T(8,128)(2,1)S(1)}, u32[]{:S(2)}, u32[]{:S(2)}) collective-permute-start(bf16[640,256]{1,0:T(8,128)(2,1)} %get-tuple-element.70), channel_id=1, source_target_pairs={{0,2},{2,4},{4,6},{6,0},{1,3},{3,5},{5,7},{7,1},{8,10},{10,12},{12... | collective-permute-start | bytes 983048 | tf_op jit(solution)/shard_map/ppermute | solution.py:22
  88.3 0.6 collective-permute-start.17
  88.9 0.7 broadcast_in_dim.2
  89.7 10.6 %all-to-all-start = ((bf16[32,8,640]{2,1,0:T(8,128)(2,1)}), bf16[32,8,640]{2,1,0:T(8,128)(2,1)}, u32[]{:S(2)}, u32[]{:S(2)}) async-start(bf16[32,8,640]{2,1,0:T(8,128)(2,1)} %bitcast.30), calls=%async_computation | async-start | bytes 655360 | tf_op jit(solution)/shard_map/all_to_all | solution.py:234
  100.3 1.3 fusion.2
  101.6 1.4 fusion.5
  103.1 0.2 subtract_convert_fusion
  103.3 8.0 %all-to-all-done = bf16[32,8,640]{2,1,0:T(8,128)(2,1)} async-done(((bf16[32,8,640]{2,1,0:T(8,128)(2,1)}), bf16[32,8,640]{2,1,0:T(8,128)(2,1)}, u32[]{:S(2)}, u32[]{:S(2)}) %all-to-all-start) | async-done | bytes 327712 | tf_op jit(solution)/shard_map/all_to_all | solution.py:234
  111.3 1.3 convolution_convert_fusion
  112.7 0.1 copy.20
  112.8 0.8 reshape.149
  113.6 3.4 %all-to-all-start.1 = ((bf16[8,32,512]{2,1,0:T(8,128)(2,1)}), bf16[8,32,512]{2,1,0:T(8,128)(2,1)S(1)}, u32[]{:S(2)}, u32[]{:S(2)}) async-start(bf16[8,32,512]{2,1,0:T(8,128)(2,1)} %reshape.149), calls=%async_computation.1 | async-start | bytes 524288 | tf_op jit(solution)/shard_map/all_to_all | solution.py:274
  117.1 8.7 %all-to-all-done.1 = bf16[8,32,512]{2,1,0:T(8,128)(2,1)S(1)} async-done(((bf16[8,32,512]{2,1,0:T(8,128)(2,1)}), bf16[8,32,512]{2,1,0:T(8,128)(2,1)S(1)}, u32[]{:S(2)}, u32[]{:S(2)}) %all-to-all-start.1) | async-done | bytes 262176 | tf_op jit(solution)/shard_map/all_to_all | solution.py:274
  125.8 0.9 pad_maximum_fusion
  126.7 3.9 %all-to-all-start.2 = ((bf16[8,84,512]{2,1,0:T(8,128)(2,1)}), bf16[8,84,512]{2,1,0:T(8,128)(2,1)S(1)}, u32[]{:S(2)}, u32[]{:S(2)}) async-start(bf16[8,84,512]{2,1,0:T(8,128)(2,1)} %pad_maximum_fusion), calls=%async_computation.2 | async-start | bytes 1441792 | tf_op jit(solution)/shard_map/all_to_all | solution.py:278
  130.7 2.2 %copy-done.1 = bf16[4,1024,512]{2,1,0:T(8,128)(2,1)S(1)} copy-done((bf16[4,1024,512]{2,1,0:T(8,128)(2,1)S(1)}, bf16[4,1024,512]{2,1,0:T(8,128)(2,1)}, u32[]{:S(2)}) %copy-start.1) | copy-done | bytes 4194328
  132.8 3.3 %past.1 = (f32[4,2,8,128]{3,2,1,0:T(8,128)S(1)}, f32[4,2,8,128]{3,2,1,0:T(8,128)S(1)}, f32[4,2,8,128]{3,2,1,0:T(8,128)S(1)}) custom-call(s32[4]{0:T(128)S(1)} %copy-done.6, bf16[4,2,8,128]{3,2,1,0:T(8,128)(2,1)S(1)} %pad.4.query_ref, bf16[4,1024,512]{2,1,0:T(8,128)(2,1)S(1)} %copy-done.1), custom_call_target="tpu_custom_call" | custom-call | flops 67108864 | bytes 4194304 | tf_op jit(solution)/shard_map/past/pallas_call | solution.py:141
  136.3 0.6 slice_bitcast_fusion.2.sum_ref
  136.9 0.6 slice_bitcast_fusion
  137.5 8.6 %all-to-all-done.2.parts_ref = bf16[8,84,512]{2,1,0:T(8,128)(2,1)S(1)} async-done(((bf16[8,84,512]{2,1,0:T(8,128)(2,1)}), bf16[8,84,512]{2,1,0:T(8,128)(2,1)S(1)}, u32[]{:S(2)}, u32[]{:S(2)}) %all-to-all-start.2) | async-done | bytes 688160 | tf_op jit(solution)/shard_map/all_to_all | solution.py:278
  146.1 0.9 copy-done.7
  147.0 2.0 %finish.1 = (bf16[80,512]{1,0:T(8,128)(2,1)}, bf16[4,1280]{1,0:T(4,128)(2,1)}) custom-call(bf16[80,512]{1,0:T(8,128)(2,1)} %weight_ref.1, bf16[4,1280]{1,0:T(4,128)(2,1)} %query_ref.1, f32[2,5,4,128]{3,2,1,0:T(4,128)} %slice_bitcast_fusion.2.sum_ref, f32[2,5,4,128]{3,2,1,0:T(4,128)} %get-tuple-element.78.top_ref, ...), custom_call_target="tpu_custom_call" | custom-call | tf_op jit(solution)/shard_map/finish/pallas_call | solution.py:281
  (54 shorter events, 0.4 us)
Async XLA Ops:
  0.6 4.7 %copy-start = (bf16[1536,512]{1,0:T(8,128)(2,1)S(1)}, bf16[1536,512]{1,0:T(8,128)(2,1)}, u32[]{:S(2)}) copy-start(bf16[1536,512]{1,0:T(8,128)(2,1)} %param.8) | copy-start | bytes 4718596
  0.6 11.3 %collective-permute-start = (bf16[384,5120]{1,0:T(8,128)(2,1)}, bf16[384,5120]{1,0:T(8,128)(2,1)}, u32[]{:S(2)}, u32[]{:S(2)}) collective-permute-start(bf16[384,5120]{1,0:T(8,128)(2,1)} %a_ref.3), channel_id=1, source_target_pairs={{0,1},{1,0},{2,3},{3,2},{4,5},{5,4},{6,7},{7,6},{8,9},{9,8},{10,11... | collective-permute-start | bytes 11796488 | tf_op jit(solution)/shard_map/ppermute | solution.py:26
  3.0 23.8 %collective-permute-start.1 = (bf16[2,384,512]{2,1,0:T(8,128)(2,1)}, bf16[2,384,512]{2,1,0:T(8,128)(2,1)}, u32[]{:S(2)}, u32[]{:S(2)}) collective-permute-start(bf16[2,384,512]{2,1,0:T(8,128)(2,1)} %dynamic-slice_bitcast_fusion), channel_id=1, source_target_pairs={{0,2},{2,0},{1,3},{3,1},{4,6},{6,4},{5,7},{7,5},{8,10},{10,8},{9,1... | collective-permute-start | bytes 2359304 | tf_op jit(solution)/shard_map/ppermute | solution.py:26
  5.3 2.1 %copy-start.2 = (bf16[384,5120]{1,0:T(8,128)(2,1)S(1)}, bf16[384,5120]{1,0:T(8,128)(2,1)}, u32[]{:S(2)}) copy-start(bf16[384,5120]{1,0:T(8,128)(2,1)} %a_ref.3) | copy-start | bytes 11796484
  11.9 13.7 %copy-start.12 = (bf16[4,1280]{1,0:T(4,128)(2,1)S(1)}, bf16[4,1280]{1,0:T(4,128)(2,1)}, u32[]{:S(2)}) copy-start(bf16[4,1280]{1,0:T(4,128)(2,1)} %query_ref.1) | copy-start | bytes 30724
  19.5 0.9 copy-start.4
  20.3 18.3 %collective-permute-start.2 = (bf16[2,640,256]{2,1,0:T(8,128)(2,1)}, bf16[2,640,256]{2,1,0:T(8,128)(2,1)}, u32[]{:S(2)}, u32[]{:S(2)}) collective-permute-start(bf16[2,640,256]{2,1,0:T(8,128)(2,1)} %get-tuple-element.37), channel_id=1, source_target_pairs={{0,64},{64,128},{128,192},{192,0},{1,65},{65,129},{129,193},{193,1... | collective-permute-start | bytes 1966088 | tf_op jit(solution)/shard_map/ppermute | solution.py:22
  20.3 19.9 %collective-permute-start.3 = (bf16[2,640,256]{2,1,0:T(8,128)(2,1)}, bf16[2,640,256]{2,1,0:T(8,128)(2,1)}, u32[]{:S(2)}, u32[]{:S(2)}) collective-permute-start(bf16[2,640,256]{2,1,0:T(8,128)(2,1)} %get-tuple-element.38), channel_id=1, source_target_pairs={{0,192},{64,0},{128,64},{192,128},{1,193},{65,1},{129,65},{193,129... | collective-permute-start | bytes 1966088 | tf_op jit(solution)/shard_map/ppermute | solution.py:22
  23.6 17.0 %collective-permute-start.4 = (bf16[4,320,256]{2,1,0:T(8,128)(2,1)}, bf16[4,320,256]{2,1,0:T(8,128)(2,1)}, u32[]{:S(2)}, u32[]{:S(2)}) collective-permute-start(bf16[4,320,256]{2,1,0:T(8,128)(2,1)} %get-tuple-element.39), channel_id=1, source_target_pairs={{0,2},{2,4},{4,6},{6,0},{1,3},{3,5},{5,7},{7,1},{8,10},{10,12},{12... | collective-permute-start | bytes 1966088 | tf_op jit(solution)/shard_map/ppermute | solution.py:22
  24.0 16.7 %collective-permute-start.5 = (bf16[4,320,256]{2,1,0:T(8,128)(2,1)}, bf16[4,320,256]{2,1,0:T(8,128)(2,1)}, u32[]{:S(2)}, u32[]{:S(2)}) collective-permute-start(bf16[4,320,256]{2,1,0:T(8,128)(2,1)} %get-tuple-element.40), channel_id=1, source_target_pairs={{0,6},{2,0},{4,2},{6,4},{1,7},{3,1},{5,3},{7,5},{8,14},{10,8},{12,... | collective-permute-start | bytes 1966088 | tf_op jit(solution)/shard_map/ppermute | solution.py:22
  26.8 23.5 %collective-permute-start.13 = (bf16[4,4,640]{2,1,0:T(4,128)(2,1)S(1)}, bf16[4,4,640]{2,1,0:T(4,128)(2,1)S(1)}, u32[]{:S(2)}, u32[]{:S(2)}) collective-permute-start(bf16[4,4,640]{2,1,0:T(4,128)(2,1)S(1)} %dynamic-slice_bitcast_fusion.4), channel_id=1, source_target_pairs={{0,4},{4,0},{1,5},{5,1},{2,6},{6,2},{3,7},{7,3},{8,12},{12,8},{9,1... | collective-permute-start | bytes 61448 | tf_op jit(solution)/shard_map/ppermute | solution.py:26
  27.5 2.1 %copy-start.3 = (bf16[384,5120]{1,0:T(8,128)(2,1)S(1)}, bf16[384,5120]{1,0:T(8,128)(2,1)}, u32[]{:S(2)}) copy-start(bf16[384,5120]{1,0:T(8,128)(2,1)} %a_ref.3) | copy-start | bytes 11796484
  29.7 14.2 %copy-start.5 = (bf16[2,640,256]{2,1,0:T(8,128)(2,1)S(1)}, bf16[2,640,256]{2,1,0:T(8,128)(2,1)}, u32[]{:S(2)}) copy-start(bf16[2,640,256]{2,1,0:T(8,128)(2,1)} %copy-done.4) | copy-start | bytes 1966084
  38.6 25.3 %collective-permute-start.7 = (bf16[4,320,256]{2,1,0:T(8,128)(2,1)S(1)}, bf16[4,320,256]{2,1,0:T(8,128)(2,1)}, u32[]{:S(2)}, u32[]{:S(2)}) collective-permute-start(bf16[4,320,256]{2,1,0:T(8,128)(2,1)S(1)} %get-tuple-element.48), channel_id=1, source_target_pairs={{0,2},{2,4},{4,6},{6,0},{1,3},{3,5},{5,7},{7,1},{8,10},{10,12},{12... | collective-permute-start | bytes 1966088 | tf_op jit(solution)/shard_map/ppermute | solution.py:22
  40.3 24.2 %collective-permute-start.8 = (bf16[4,320,256]{2,1,0:T(8,128)(2,1)}, bf16[4,320,256]{2,1,0:T(8,128)(2,1)}, u32[]{:S(2)}, u32[]{:S(2)}) collective-permute-start(bf16[4,320,256]{2,1,0:T(8,128)(2,1)} %get-tuple-element.49), channel_id=1, source_target_pairs={{0,6},{2,0},{4,2},{6,4},{1,7},{3,1},{5,3},{7,5},{8,14},{10,8},{12,... | collective-permute-start | bytes 1966088 | tf_op jit(solution)/shard_map/ppermute | solution.py:22
  40.6 18.9 %collective-permute-start.14 = (bf16[2,640,256]{2,1,0:T(8,128)(2,1)S(1)}, bf16[2,640,256]{2,1,0:T(8,128)(2,1)S(1)}, u32[]{:S(2)}, u32[]{:S(2)}) collective-permute-start(bf16[2,640,256]{2,1,0:T(8,128)(2,1)S(1)} %get-tuple-element.59), channel_id=1, source_target_pairs={{0,64},{64,128},{128,192},{192,0},{1,65},{65,129},{129,193},{193,1... | collective-permute-start | bytes 1966088 | tf_op jit(solution)/shard_map/ppermute | solution.py:22
  40.7 21.5 %collective-permute-start.12 = (bf16[2,640,256]{2,1,0:T(8,128)(2,1)S(1)}, bf16[2,640,256]{2,1,0:T(8,128)(2,1)S(1)}, u32[]{:S(2)}, u32[]{:S(2)}) collective-permute-start(bf16[2,640,256]{2,1,0:T(8,128)(2,1)S(1)} %get-tuple-element.57), channel_id=1, source_target_pairs={{0,192},{64,0},{128,64},{192,128},{1,193},{65,1},{129,65},{193,129... | collective-permute-start | bytes 1966088 | tf_op jit(solution)/shard_map/ppermute | solution.py:22
  50.3 21.0 %collective-permute-start.10 = (bf16[2,640,256]{2,1,0:T(8,128)(2,1)}, bf16[2,640,256]{2,1,0:T(8,128)(2,1)}, u32[]{:S(2)}, u32[]{:S(2)}) collective-permute-start(bf16[2,640,256]{2,1,0:T(8,128)(2,1)} %add_convert_fusion.2), channel_id=1, source_target_pairs={{0,64},{64,128},{128,192},{192,0},{1,65},{65,129},{129,193},{193,1... | collective-permute-start | bytes 1966088 | tf_op jit(solution)/shard_map/ppermute | solution.py:22
  59.5 4.4 %copy-start.8 = (bf16[2,640,256]{2,1,0:T(8,128)(2,1)}, bf16[2,640,256]{2,1,0:T(8,128)(2,1)S(1)}, u32[]{:S(2)}) copy-start(bf16[2,640,256]{2,1,0:T(8,128)(2,1)S(1)} %collective-permute-done.14) | copy-start | bytes 1966084
  59.5 12.3 %collective-permute-start.9 = (bf16[4,320,256]{2,1,0:T(8,128)(2,1)}, bf16[4,320,256]{2,1,0:T(8,128)(2,1)S(1)}, u32[]{:S(2)}, u32[]{:S(2)}) collective-permute-start(bf16[4,320,256]{2,1,0:T(8,128)(2,1)} %add_convert_fusion.3), channel_id=1, source_target_pairs={{0,6},{2,0},{4,2},{6,4},{1,7},{3,1},{5,3},{7,5},{8,14},{10,8},{12,... | collective-permute-start | bytes 1966088 | tf_op jit(solution)/shard_map/ppermute | solution.py:22
  62.2 11.2 %collective-permute-start.6 = (bf16[4,320,256]{2,1,0:T(8,128)(2,1)}, bf16[4,320,256]{2,1,0:T(8,128)(2,1)}, u32[]{:S(2)}, u32[]{:S(2)}) collective-permute-start(bf16[4,320,256]{2,1,0:T(8,128)(2,1)} %add_convert_fusion.4), channel_id=1, source_target_pairs={{0,2},{2,4},{4,6},{6,0},{1,3},{3,5},{5,7},{7,1},{8,10},{10,12},{12... | collective-permute-start | bytes 1966088 | tf_op jit(solution)/shard_map/ppermute | solution.py:22
  63.9 19.4 %collective-permute-start.15 = (bf16[2,640,256]{2,1,0:T(8,128)(2,1)}, bf16[2,640,256]{2,1,0:T(8,128)(2,1)}, u32[]{:S(2)}, u32[]{:S(2)}) collective-permute-start(bf16[2,640,256]{2,1,0:T(8,128)(2,1)} %add_convert_fusion.1), channel_id=1, source_target_pairs={{0,192},{64,0},{128,64},{192,128},{1,193},{65,1},{129,65},{193,129... | collective-permute-start | bytes 1966088 | tf_op jit(solution)/shard_map/ppermute | solution.py:22
  75.4 1.7 %copy-start.10 = (bf16[80,512]{1,0:T(8,128)(2,1)S(1)}, bf16[80,512]{1,0:T(8,128)(2,1)}, u32[]{:S(2)}) copy-start(bf16[80,512]{1,0:T(8,128)(2,1)} %weight_ref.1) | copy-start | bytes 245764
  76.4 6.9 %copy-start.9 = (bf16[2,640,256]{2,1,0:T(8,128)(2,1)S(1)}, bf16[2,640,256]{2,1,0:T(8,128)(2,1)}, u32[]{:S(2)}) copy-start(bf16[2,640,256]{2,1,0:T(8,128)(2,1)} %copy-done.8) | copy-start | bytes 1966084
  76.4 11.8 %collective-permute-start.18 = (bf16[640,256]{1,0:T(8,128)(2,1)}, bf16[640,256]{1,0:T(8,128)(2,1)}, u32[]{:S(2)}, u32[]{:S(2)}) collective-permute-start(bf16[640,256]{1,0:T(8,128)(2,1)} %get-tuple-element.72), channel_id=1, source_target_pairs={{0,128},{64,192},{128,0},{192,64},{1,129},{65,193},{129,1},{193,65... | collective-permute-start | bytes 983048 | tf_op jit(solution)/shard_map/ppermute | solution.py:22
  77.2 23.1 %collective-permute-start.19 = (bf16[640,256]{1,0:T(8,128)(2,1)}, bf16[640,256]{1,0:T(8,128)(2,1)}, u32[]{:S(2)}, u32[]{:S(2)}) collective-permute-start(bf16[640,256]{1,0:T(8,128)(2,1)} %get-tuple-element.74), channel_id=1, source_target_pairs={{0,64},{64,128},{128,192},{192,0},{1,65},{65,129},{129,193},{193,1... | collective-permute-start | bytes 983048 | tf_op jit(solution)/shard_map/ppermute | solution.py:22
  78.6 21.7 %collective-permute-start.20 = (bf16[640,256]{1,0:T(8,128)(2,1)}, bf16[640,256]{1,0:T(8,128)(2,1)}, u32[]{:S(2)}, u32[]{:S(2)}) collective-permute-start(bf16[640,256]{1,0:T(8,128)(2,1)} %get-tuple-element.73), channel_id=1, source_target_pairs={{0,192},{64,0},{128,64},{192,128},{1,193},{65,1},{129,65},{193,129... | collective-permute-start | bytes 983048 | tf_op jit(solution)/shard_map/ppermute | solution.py:22
  82.4 19.2 %collective-permute-start.11 = (bf16[640,256]{1,0:T(8,128)(2,1)}, bf16[640,256]{1,0:T(8,128)(2,1)}, u32[]{:S(2)}, u32[]{:S(2)}) collective-permute-start(bf16[640,256]{1,0:T(8,128)(2,1)} %fusion.6), channel_id=1, source_target_pairs={{0,4},{2,6},{4,0},{6,2},{1,5},{3,7},{5,1},{7,3},{8,12},{10,14},{12... | collective-permute-start | bytes 983048 | tf_op jit(solution)/shard_map/ppermute | solution.py:22
  83.3 5.6 %copy-start.11 = (bf16[4,8,640]{2,1,0:T(8,128)(2,1)S(1)}, bf16[4,8,640]{2,1,0:T(8,128)(2,1)}, u32[]{:S(2)}) copy-start(bf16[4,8,640]{2,1,0:T(8,128)(2,1)} %pad_maximum_fusion.2) | copy-start | bytes 122884
  85.5 16.2 %collective-permute-start.16 = (bf16[640,256]{1,0:T(8,128)(2,1)}, bf16[640,256]{1,0:T(8,128)(2,1)S(1)}, u32[]{:S(2)}, u32[]{:S(2)}) collective-permute-start(bf16[640,256]{1,0:T(8,128)(2,1)} %get-tuple-element.70), channel_id=1, source_target_pairs={{0,2},{2,4},{4,6},{6,0},{1,3},{3,5},{5,7},{7,1},{8,10},{10,12},{12... | collective-permute-start | bytes 983048 | tf_op jit(solution)/shard_map/ppermute | solution.py:22
  88.3 13.4 %collective-permute-start.17 = (bf16[640,256]{1,0:T(8,128)(2,1)}, bf16[640,256]{1,0:T(8,128)(2,1)S(1)}, u32[]{:S(2)}, u32[]{:S(2)}) collective-permute-start(bf16[640,256]{1,0:T(8,128)(2,1)} %get-tuple-element.71), channel_id=1, source_target_pairs={{0,6},{2,0},{4,2},{6,4},{1,7},{3,1},{5,3},{7,5},{8,14},{10,8},{12,... | collective-permute-start | bytes 983048 | tf_op jit(solution)/shard_map/ppermute | solution.py:22
  89.7 21.7 %all-to-all-start = ((bf16[32,8,640]{2,1,0:T(8,128)(2,1)}), bf16[32,8,640]{2,1,0:T(8,128)(2,1)}, u32[]{:S(2)}, u32[]{:S(2)}) async-start(bf16[32,8,640]{2,1,0:T(8,128)(2,1)} %bitcast.30), calls=%async_computation | async-start | bytes 655360 | tf_op jit(solution)/shard_map/all_to_all | solution.py:234
  113.6 12.1 %all-to-all-start.1 = ((bf16[8,32,512]{2,1,0:T(8,128)(2,1)}), bf16[8,32,512]{2,1,0:T(8,128)(2,1)S(1)}, u32[]{:S(2)}, u32[]{:S(2)}) async-start(bf16[8,32,512]{2,1,0:T(8,128)(2,1)} %reshape.149), calls=%async_computation.1 | async-start | bytes 524288 | tf_op jit(solution)/shard_map/all_to_all | solution.py:274
  125.8 4.8 %copy-start.6 = (s32[4]{0:T(128)S(1)}, s32[4]{0:T(128)}, u32[]{:S(2)}) copy-start(s32[4]{0:T(128)} %lengths.1) | copy-start | bytes 52
  126.7 19.4 %all-to-all-start.2 = ((bf16[8,84,512]{2,1,0:T(8,128)(2,1)}), bf16[8,84,512]{2,1,0:T(8,128)(2,1)S(1)}, u32[]{:S(2)}, u32[]{:S(2)}) async-start(bf16[8,84,512]{2,1,0:T(8,128)(2,1)} %pad_maximum_fusion), calls=%async_computation.2 | async-start | bytes 1441792 | tf_op jit(solution)/shard_map/all_to_all | solution.py:278
  130.7 2.2 %copy-start.1 = (bf16[4,1024,512]{2,1,0:T(8,128)(2,1)S(1)}, bf16[4,1024,512]{2,1,0:T(8,128)(2,1)}, u32[]{:S(2)}) copy-start(bf16[4,1024,512]{2,1,0:T(8,128)(2,1)} %cache_ref.1) | copy-start | bytes 12582916
  146.1 0.9 copy-start.7

commit v6 on v5

--- a/solution.py
+++ b/solution.py
@@ -223,9 +223,8 @@
     place = jnp.stack([y, jnp.where(xl == 0, xh, 1 - xh), c]).astype(jnp.int32)
     oth = product(rows, place, tokens_in, other_tokens, got)
     oth_y, (oth_x1a, oth_x1b, oth_x3a, oth_x3b) = oth[:4], oth[4:]
-    oth_y2, up, down, up_x, down_x, query = lax.optimization_barrier(
-        (oth_y[2], up, down, up_x, down_x, query)
-    )
+    oth_y2, up, down, query = lax.optimization_barrier((oth_y[2], up, down, query))
+    oth_x1b, up_x, down_x = lax.optimization_barrier((oth_x1b, up_x, down_x))
     far = shift(oth_y2, "y", ny, -1)
     past = attend_past(query, cache, lengths)
 
@@ -237,10 +236,10 @@
 
     oth_up = shift(oth_y[1], "y", ny, 1)
     own_up = shift(add(own_y[1], up), "y", ny, 1)
-    far, oth_up = lax.optimization_barrier((far, oth_up))
-    oth_down = shift(add(oth_y[3], far), "y", ny, -1)
     up_b = shift(oth_x1b, X, nx, 1)
     down_a = shift(oth_x3a, X, nx, -1)
+    far, oth_up, up_b, down_a = lax.optimization_barrier((far, oth_up, up_b, down_a))
+    oth_down = shift(add(oth_y[3], far), "y", ny, -1)
     up_a = shift(add(oth_x1a, up_x), X, nx, 1)
     down_b = shift(add(oth_x3b, down_x), X, nx, -1)
 

time: 150 us -> 152 us (1.013)
  starting transfers between devices: 43.2 us -> 47.1 us
    ppermute x18, starting transfers between devices: 22.1 us -> 25.9 us  [shift(): lax.ppermute(value, axis, [(i, (i + by) % size) for i in range(size)])]
    ppermute x18, waiting for transfers between devices: 18.4 us -> 16.9 us  [shift(): lax.ppermute(value, axis, [(i, (i + by) % size) for i in range(size)])]
    unnamed x26 -> x30, local copies, waits for them, and re-layouts: 8.17 us -> 8.25 us
  transfers between devices with their start and end apart: 24 -> 24, of which waited for: 8 -> 9; matrix products, arithmetic and copies ran while one was open for 16% -> 16% of each run, Pallas kernels for 16% -> 15%
where the time goes in v6:
time: 152 us; the launch traced here: 151 us
  starting transfers between devices  47.1 us (31%)
  waiting for transfers between devices  42.2 us (28%)
  Pallas kernels  25.3 us (17%)
  other arithmetic  18.4 us (12%)
  local copies, waits for them, and re-layouts  15.6 us (10%)
    ppermute x18, starting transfers between devices, shift(): lax.ppermute(value, axis, [(i, (i + by) % size) for i in range(size)])  25.9 us
    pallas_call x3, Pallas kernels, product(): pl.pallas_call(kernel, grid_spec=pltpu.PrefetchScalarGridSpec(num_scalar_...  20 us
    ppermute x18, waiting for transfers between devices, shift(): lax.ppermute(value, axis, [(i, (i + by) % size) for i in range(size)])  16.9 us
    all_to_all x1, starting transfers between devices, local(): lax.all_to_all(held.reshape(ny * nz, nh * count, nz * rows), ('y', 'z'),...  10.7 us
    all_to_all x1, waiting for transfers between devices, local(): lax.all_to_all(fresh.reshape(ny * nh, nz * count, columns), ('y', 'xh'),...  8.67 us
    all_to_all x1, waiting for transfers between devices, local(): lax.all_to_all(jnp.concatenate([both, fresh], axis=1), 'z', 0, 0, tiled=T...  8.62 us
    unnamed x30, local copies, waits for them, and re-layouts  8.25 us
    all_to_all x1, waiting for transfers between devices, local(): lax.all_to_all(held.reshape(ny * nz, nh * count, nz * rows), ('y', 'z'),...  7.99 us
  transfers between devices with their start and end apart: 24, of which 9 were waited for; matrix products, arithmetic and copies ran while one was open for 16% of the time, Pallas kernels for 15%

profile of v6, /device:TPU:2, one launch (start us, length us, event | category | flops | bytes accessed | tf_op | source)
XLA Modules:
  0.0 150.9 jit_solution(4245203424960398896)
XLA Ops:
  0.6 0.1 collective-permute-start
  0.7 2.2 %dynamic-slice_bitcast_fusion = bf16[2,384,512]{2,1,0:T(8,128)(2,1)} fusion(bf16[2,2,384,512]{3,2,1,0:T(8,128)(2,1)} %bitcast.67, s32[]{:T(128)S(6)} %select_n.105), kind=kLoop, calls=%fused_computation.7 | loop fusion | bytes 1572868 | tf_op jit(solution)/shard_map/jit(dynamic_index_in_dim)/squeeze | solution.py:30
  3.0 2.3 %collective-permute-start.1 = (bf16[2,384,512]{2,1,0:T(8,128)(2,1)}, bf16[2,384,512]{2,1,0:T(8,128)(2,1)}, u32[]{:S(2)}, u32[]{:S(2)}) collective-permute-start(bf16[2,384,512]{2,1,0:T(8,128)(2,1)} %dynamic-slice_bitcast_fusion), channel_id=1, source_target_pairs={{0,2},{2,0},{1,3},{3,1},{4,6},{6,4},{5,7},{7,5},{8,10},{10,8},{9,1... | collective-permute-start | bytes 2359304 | tf_op jit(solution)/shard_map/ppermute | solution.py:26
  5.3 2.1 %copy-done.2 = bf16[384,5120]{1,0:T(8,128)(2,1)S(1)} copy-done((bf16[384,5120]{1,0:T(8,128)(2,1)S(1)}, bf16[384,5120]{1,0:T(8,128)(2,1)}, u32[]{:S(2)}) %copy-start.2) | copy-done | bytes 3932184
  7.4 4.4 %head.1.head_ref = bf16[5120,512]{1,0:T(8,128)(2,1)S(1)} custom-call(s32[3]{0:T(128)S(1)} %pad_add_fusion.1.place, bf16[384,5120]{1,0:T(8,128)(2,1)S(1)} %copy-done.2, bf16[4,384,512]{2,1,0:T(8,128)(2,1)S(1)} %bitcast.68), custom_call_target="tpu_custom_call" | custom-call | flops 2013265920 | bytes 11796480 | tf_op jit(solution)/shard_map/head/pallas_call | solution.py:102
  11.9 7.6 %rest.1 = (bf16[2,640,256]{2,1,0:T(8,128)(2,1)S(1)}, bf16[2,640,256]{2,1,0:T(8,128)(2,1)S(1)}, bf16[2,640,256]{2,1,0:T(8,128)(2,1)}, bf16[2,640,256]{2,1,0:T(8,1...) custom-call(s32[3]{0:T(128)S(1)} %pad_add_fusion.1.place, ...), custom_call_target="tpu_custom_call" | custom-call | flops 2013265920 | bytes 11796480 | tf_op jit(solution)/shard_map/rest/pallas_call | solution.py:102
  19.5 0.8 copy-done.4
  20.4 3.2 %collective-permute-start.3 = (bf16[2,640,256]{2,1,0:T(8,128)(2,1)}, bf16[2,640,256]{2,1,0:T(8,128)(2,1)}, u32[]{:S(2)}, u32[]{:S(2)}) collective-permute-start(bf16[2,640,256]{2,1,0:T(8,128)(2,1)} %get-tuple-element.41), channel_id=1, source_target_pairs={{0,192},{64,0},{128,64},{192,128},{1,193},{65,1},{129,65},{193,129... | collective-permute-start | bytes 1966088 | tf_op jit(solution)/shard_map/ppermute | solution.py:22
  23.6 0.4 collective-permute-start.4
  24.0 1.6 %collective-permute-start.5 = (bf16[4,320,256]{2,1,0:T(8,128)(2,1)}, bf16[4,320,256]{2,1,0:T(8,128)(2,1)}, u32[]{:S(2)}, u32[]{:S(2)}) collective-permute-start(bf16[4,320,256]{2,1,0:T(8,128)(2,1)} %get-tuple-element.50), channel_id=1, source_target_pairs={{0,6},{2,0},{4,2},{6,4},{1,7},{3,1},{5,3},{7,5},{8,14},{10,8},{12,... | collective-permute-start | bytes 1966088 | tf_op jit(solution)/shard_map/ppermute | solution.py:22
  25.6 0.9 reshape.143
  26.6 0.1 reshape.144
  26.8 0.8 collective-permute-start.8
  27.6 2.1 %copy-done.3 = bf16[384,5120]{1,0:T(8,128)(2,1)S(1)} copy-done((bf16[384,5120]{1,0:T(8,128)(2,1)S(1)}, bf16[384,5120]{1,0:T(8,128)(2,1)}, u32[]{:S(2)}) %copy-start.3) | copy-done | bytes 3932184
  29.7 7.9 %product.1 = (bf16[2,640,256]{2,1,0:T(8,128)(2,1)S(1)}, bf16[2,640,256]{2,1,0:T(8,128)(2,1)S(1)}, bf16[2,640,256]{2,1,0:T(8,128)(2,1)S(1)}, bf16[2,640,256]{2,1,...) custom-call(s32[3]{0:T(128)S(1)} %pad_add_fusion.place, ...), custom_call_target="tpu_custom_call" | custom-call | flops 4026531840 | bytes 11796480 | tf_op jit(solution)/shard_map/product/pallas_call | solution.py:102
  37.6 1.0 collective-permute-done.2
  38.6 0.9 collective-permute-start.11
  39.5 0.4 collective-permute-start.9
  39.9 0.4 collective-permute-done.4
  40.3 2.4 %collective-permute-start.7 = (bf16[2,640,256]{2,1,0:T(8,128)(2,1)S(1)}, bf16[2,640,256]{2,1,0:T(8,128)(2,1)S(1)}, u32[]{:S(2)}, u32[]{:S(2)}) collective-permute-start(bf16[2,640,256]{2,1,0:T(8,128)(2,1)S(1)} %get-tuple-element.52), channel_id=1, source_target_pairs={{0,192},{64,0},{128,64},{192,128},{1,193},{65,1},{129,65},{193,129... | collective-permute-start | bytes 1966088 | tf_op jit(solution)/shard_map/ppermute | solution.py:22
  42.7 1.1 collective-permute-start.10
  43.9 2.1 %add_convert_fusion.2 = bf16[2,640,256]{2,1,0:T(8,128)(2,1)} fusion(bf16[2,640,256]{2,1,0:T(8,128)(2,1)} %collective-permute-done.2, bf16[2,640,256]{2,1,0:T(8,128)(2,1)S(1)} %copy-done.5), kind=kLoop, calls=%fused_computation.3 | loop fusion | flops 1310720 | bytes 1966080 | tf_op jit(solution)/shard_map/convert_element_type | solution.py:34
  46.0 2.1 %add_convert_fusion.3 = bf16[4,320,256]{2,1,0:T(8,128)(2,1)} fusion(bf16[4,320,256]{2,1,0:T(8,128)(2,1)} %collective-permute-done.5, bf16[4,320,256]{2,1,0:T(8,128)(2,1)S(1)} %get-tuple-element.59), kind=kLoop, calls=%fused_computation.4 | loop fusion | flops 1310720 | bytes 1966080 | tf_op jit(solution)/shard_map/convert_element_type | solution.py:34
  48.1 2.1 %add_convert_fusion.4 = bf16[4,320,256]{2,1,0:T(8,128)(2,1)} fusion(bf16[4,320,256]{2,1,0:T(8,128)(2,1)} %collective-permute-done.4, bf16[4,320,256]{2,1,0:T(8,128)(2,1)S(1)} %get-tuple-element.47), kind=kLoop, calls=%fused_computation.5 | loop fusion | flops 1310720 | bytes 1966080 | tf_op jit(solution)/shard_map/convert_element_type | solution.py:34
  50.2 4.5 %collective-permute-done.11 = bf16[4,320,256]{2,1,0:T(8,128)(2,1)S(1)} collective-permute-done((bf16[4,320,256]{2,1,0:T(8,128)(2,1)S(1)}, bf16[4,320,256]{2,1,0:T(8,128)(2,1)S(1)}, u32[]{:S(2)}, u32[]{:S(2)}) %collective-permute-start.11) | collective-permute-done | bytes 655392 | tf_op jit(solution)/shard_map/ppermute | solution.py:22
  54.7 1.5 collective-permute-start.12
  56.2 0.5 collective-permute-start.6
  56.7 0.6 pad_maximum_fusion.2
  57.4 1.0 collective-permute-done.9
  58.4 1.2 add_convert_fusion.1
  59.6 0.1 copy-done.9
  59.7 2.7 %collective-permute-start.15 = (bf16[2,640,256]{2,1,0:T(8,128)(2,1)}, bf16[2,640,256]{2,1,0:T(8,128)(2,1)}, u32[]{:S(2)}, u32[]{:S(2)}) collective-permute-start(bf16[2,640,256]{2,1,0:T(8,128)(2,1)} %add_convert_fusion.1), channel_id=1, source_target_pairs={{0,192},{64,0},{128,64},{192,128},{1,193},{65,1},{129,65},{193,129... | collective-permute-start | bytes 1966088 | tf_op jit(solution)/shard_map/ppermute | solution.py:22
  62.4 7.9 %collective-permute-done.13 = bf16[2,640,256]{2,1,0:T(8,128)(2,1)} collective-permute-done((bf16[2,640,256]{2,1,0:T(8,128)(2,1)}, bf16[2,640,256]{2,1,0:T(8,128)(2,1)}, u32[]{:S(2)}, u32[]{:S(2)}) %collective-permute-start.13) | collective-permute-done | bytes 655392 | tf_op jit(solution)/shard_map/ppermute | solution.py:22
  70.3 2.1 %collective-permute-done.6 = bf16[4,320,256]{2,1,0:T(8,128)(2,1)} collective-permute-done((bf16[4,320,256]{2,1,0:T(8,128)(2,1)}, bf16[4,320,256]{2,1,0:T(8,128)(2,1)}, u32[]{:S(2)}, u32[]{:S(2)}) %collective-permute-start.6) | collective-permute-done | bytes 655392 | tf_op jit(solution)/shard_map/ppermute | solution.py:22
  72.3 2.0 %add_convert_fusion = bf16[4,2,320,256]{3,2,0,1:T(8,128)(2,1)S(1)} fusion(bf16[4,1,320,256]{3,2,0,1:T(8,128)(2,1)S(1)} %bitcast.71, bf16[4,1,320,256]{3,2,0,1:T(8,128)(2,1)S(1)} %bitcast.70, bf16[4,1,320,256]{3,2,0,1:T(8,128)(2,1)} %bitcast.80, bf16[4,1,320,256]{3,2,0,1:T(8,128)(2,1)} %bitcast.20, bf16[4,1,320,256]{3,2,0,1:T(8,128)(2,1)S(1)} %bitcast.81, ...), kind=kLoop, calls=%fused_computation | loop fusion | flops 5898240 | bytes 5242880 | tf_op jit(solution)/shard_map/convert_element_type | solution.py:259
  74.4 1.0 dynamic-slice_bitcast_fusion.3
  75.4 2.1 %collective-permute-start.18 = (bf16[640,256]{1,0:T(8,128)(2,1)}, bf16[640,256]{1,0:T(8,128)(2,1)}, u32[]{:S(2)}, u32[]{:S(2)}) collective-permute-start(bf16[640,256]{1,0:T(8,128)(2,1)} %get-tuple-element.78), channel_id=1, source_target_pairs={{0,128},{64,192},{128,0},{192,64},{1,129},{65,193},{129,1},{193,65... | collective-permute-start | bytes 983048 | tf_op jit(solution)/shard_map/ppermute | solution.py:22
  77.5 0.8 collective-permute-start.19
  78.3 2.6 %collective-permute-start.20 = (bf16[640,256]{1,0:T(8,128)(2,1)}, bf16[640,256]{1,0:T(8,128)(2,1)}, u32[]{:S(2)}, u32[]{:S(2)}) collective-permute-start(bf16[640,256]{1,0:T(8,128)(2,1)} %get-tuple-element.79), channel_id=1, source_target_pairs={{0,192},{64,0},{128,64},{192,128},{1,193},{65,1},{129,65},{193,129... | collective-permute-start | bytes 983048 | tf_op jit(solution)/shard_map/ppermute | solution.py:22
  80.8 1.9 %fusion.6 = bf16[640,256]{1,0:T(8,128)(2,1)} fusion(bf16[2,640,256]{2,1,0:T(8,128)(2,1)} %collective-permute-done.3, s32[]{:T(128)S(6)} %select_n.116, bf16[2,640,256]{2,1,0:T(8,128)(2,1)} %collective-permute-done.13, bf16[2,640,256]{2,1,0:T(8,128)(2,1)S(1)} %get-tuple-element.46), kind=kLoop, calls=%fused_computation.21 | loop fusion | flops 983040 | bytes 1310724 | tf_op jit(solution)/shard_map/convert_element_type | solution.py:263
  82.8 2.0 %collective-permute-start.14 = (bf16[640,256]{1,0:T(8,128)(2,1)}, bf16[640,256]{1,0:T(8,128)(2,1)}, u32[]{:S(2)}, u32[]{:S(2)}) collective-permute-start(bf16[640,256]{1,0:T(8,128)(2,1)} %fusion.6), channel_id=1, source_target_pairs={{0,4},{2,6},{4,0},{6,2},{1,5},{3,7},{5,1},{7,3},{8,12},{10,14},{12... | collective-permute-start | bytes 983048 | tf_op jit(solution)/shard_map/ppermute | solution.py:22
  84.7 2.2 %fusion.7 = (bf16[640,256]{1,0:T(8,128)(2,1)}, bf16[640,256]{1,0:T(8,128)(2,1)}) fusion(bf16[2,640,256]{2,1,0:T(8,128)(2,1)} %collective-permute-done.15, s32[]{:T(128)S(6)} %select_n.119, bf16[2,640,256]{2,1,0:T(8,128)(2,1)S(1)} %copy-done.11, bf16[2,640,256]{2,1,0:T(8,128)(2,1)S(1)} %get-tuple-element.65, s32[]{:T(128)S(6)} %select_n.122), kind=kLoop, calls=%fused_computation.22 | loop fusion | flops 1966080 | bytes 2621448 | tf_op jit(solution)/shard_map/convert_element_type | solution.py:263
  86.9 2.5 %collective-permute-start.16 = (bf16[640,256]{1,0:T(8,128)(2,1)}, bf16[640,256]{1,0:T(8,128)(2,1)S(1)}, u32[]{:S(2)}, u32[]{:S(2)}) collective-permute-start(bf16[640,256]{1,0:T(8,128)(2,1)} %get-tuple-element.76), channel_id=1, source_target_pairs={{0,2},{2,4},{4,6},{6,0},{1,3},{3,5},{5,7},{7,1},{8,10},{10,12},{12... | collective-permute-start | bytes 983048 | tf_op jit(solution)/shard_map/ppermute | solution.py:22
  89.4 1.2 collective-permute-start.17
  90.6 0.8 broadcast_in_dim.2
  91.4 10.7 %all-to-all-start = ((bf16[32,8,640]{2,1,0:T(8,128)(2,1)}), bf16[32,8,640]{2,1,0:T(8,128)(2,1)}, u32[]{:S(2)}, u32[]{:S(2)}) async-start(bf16[32,8,640]{2,1,0:T(8,128)(2,1)} %bitcast.30), calls=%async_computation | async-start | bytes 655360 | tf_op jit(solution)/shard_map/all_to_all | solution.py:233
  102.1 1.3 fusion.2
  103.5 1.4 fusion.5
  104.9 0.2 subtract_convert_fusion
  105.2 8.0 %all-to-all-done = bf16[32,8,640]{2,1,0:T(8,128)(2,1)} async-done(((bf16[32,8,640]{2,1,0:T(8,128)(2,1)}), bf16[32,8,640]{2,1,0:T(8,128)(2,1)}, u32[]{:S(2)}, u32[]{:S(2)}) %all-to-all-start) | async-done | bytes 327712 | tf_op jit(solution)/shard_map/all_to_all | solution.py:233
  113.2 1.3 convolution_convert_fusion
  114.6 0.1 copy.20
  114.7 0.8 reshape.149
  115.5 3.4 %all-to-all-start.1 = ((bf16[8,32,512]{2,1,0:T(8,128)(2,1)}), bf16[8,32,512]{2,1,0:T(8,128)(2,1)S(1)}, u32[]{:S(2)}, u32[]{:S(2)}) async-start(bf16[8,32,512]{2,1,0:T(8,128)(2,1)} %reshape.149), calls=%async_computation.1 | async-start | bytes 524288 | tf_op jit(solution)/shard_map/all_to_all | solution.py:273
  119.0 8.7 %all-to-all-done.1 = bf16[8,32,512]{2,1,0:T(8,128)(2,1)S(1)} async-done(((bf16[8,32,512]{2,1,0:T(8,128)(2,1)}), bf16[8,32,512]{2,1,0:T(8,128)(2,1)S(1)}, u32[]{:S(2)}, u32[]{:S(2)}) %all-to-all-start.1) | async-done | bytes 262176 | tf_op jit(solution)/shard_map/all_to_all | solution.py:273
  127.7 0.9 pad_maximum_fusion
  128.6 3.9 %all-to-all-start.2 = ((bf16[8,84,512]{2,1,0:T(8,128)(2,1)}), bf16[8,84,512]{2,1,0:T(8,128)(2,1)S(1)}, u32[]{:S(2)}, u32[]{:S(2)}) async-start(bf16[8,84,512]{2,1,0:T(8,128)(2,1)} %pad_maximum_fusion), calls=%async_computation.2 | async-start | bytes 1441792 | tf_op jit(solution)/shard_map/all_to_all | solution.py:277
  132.6 2.2 %copy-done.1 = bf16[4,1024,512]{2,1,0:T(8,128)(2,1)S(1)} copy-done((bf16[4,1024,512]{2,1,0:T(8,128)(2,1)S(1)}, bf16[4,1024,512]{2,1,0:T(8,128)(2,1)}, u32[]{:S(2)}) %copy-start.1) | copy-done | bytes 4194328
  134.7 3.3 %past.1 = (f32[4,2,8,128]{3,2,1,0:T(8,128)S(1)}, f32[4,2,8,128]{3,2,1,0:T(8,128)S(1)}, f32[4,2,8,128]{3,2,1,0:T(8,128)S(1)}) custom-call(s32[4]{0:T(128)S(1)} %copy-done.6, bf16[4,2,8,128]{3,2,1,0:T(8,128)(2,1)S(1)} %pad.4.query_ref, bf16[4,1024,512]{2,1,0:T(8,128)(2,1)S(1)} %copy-done.1), custom_call_target="tpu_custom_call" | custom-call | flops 67108864 | bytes 4194304 | tf_op jit(solution)/shard_map/past/pallas_call | solution.py:141
  138.2 0.6 slice_bitcast_fusion.2.sum_ref
  138.8 0.6 slice_bitcast_fusion
  139.4 8.6 %all-to-all-done.2.parts_ref = bf16[8,84,512]{2,1,0:T(8,128)(2,1)S(1)} async-done(((bf16[8,84,512]{2,1,0:T(8,128)(2,1)}), bf16[8,84,512]{2,1,0:T(8,128)(2,1)S(1)}, u32[]{:S(2)}, u32[]{:S(2)}) %all-to-all-start.2) | async-done | bytes 688160 | tf_op jit(solution)/shard_map/all_to_all | solution.py:277
  148.0 0.9 copy-done.7
  148.9 2.0 %finish.1 = (bf16[80,512]{1,0:T(8,128)(2,1)}, bf16[4,1280]{1,0:T(4,128)(2,1)}) custom-call(bf16[80,512]{1,0:T(8,128)(2,1)} %weight_ref.1, bf16[4,1280]{1,0:T(4,128)(2,1)} %query_ref.1, f32[2,5,4,128]{3,2,1,0:T(4,128)} %slice_bitcast_fusion.2.sum_ref, f32[2,5,4,128]{3,2,1,0:T(4,128)} %get-tuple-element.84.top_ref, ...), custom_call_target="tpu_custom_call" | custom-call | tf_op jit(solution)/shard_map/finish/pallas_call | solution.py:280
  (58 shorter events, 0.6 us)
Async XLA Ops:
  0.6 4.7 %copy-start = (bf16[1536,512]{1,0:T(8,128)(2,1)S(1)}, bf16[1536,512]{1,0:T(8,128)(2,1)}, u32[]{:S(2)}) copy-start(bf16[1536,512]{1,0:T(8,128)(2,1)} %param.8) | copy-start | bytes 4718596
  0.6 11.3 %collective-permute-start = (bf16[384,5120]{1,0:T(8,128)(2,1)}, bf16[384,5120]{1,0:T(8,128)(2,1)}, u32[]{:S(2)}, u32[]{:S(2)}) collective-permute-start(bf16[384,5120]{1,0:T(8,128)(2,1)} %a_ref.3), channel_id=1, source_target_pairs={{0,1},{1,0},{2,3},{3,2},{4,5},{5,4},{6,7},{7,6},{8,9},{9,8},{10,11... | collective-permute-start | bytes 11796488 | tf_op jit(solution)/shard_map/ppermute | solution.py:26
  3.0 23.8 %collective-permute-start.1 = (bf16[2,384,512]{2,1,0:T(8,128)(2,1)}, bf16[2,384,512]{2,1,0:T(8,128)(2,1)}, u32[]{:S(2)}, u32[]{:S(2)}) collective-permute-start(bf16[2,384,512]{2,1,0:T(8,128)(2,1)} %dynamic-slice_bitcast_fusion), channel_id=1, source_target_pairs={{0,2},{2,0},{1,3},{3,1},{4,6},{6,4},{5,7},{7,5},{8,10},{10,8},{9,1... | collective-permute-start | bytes 2359304 | tf_op jit(solution)/shard_map/ppermute | solution.py:26
  5.3 2.1 %copy-start.2 = (bf16[384,5120]{1,0:T(8,128)(2,1)S(1)}, bf16[384,5120]{1,0:T(8,128)(2,1)}, u32[]{:S(2)}) copy-start(bf16[384,5120]{1,0:T(8,128)(2,1)} %a_ref.3) | copy-start | bytes 11796484
  11.9 13.7 %copy-start.14 = (bf16[4,1280]{1,0:T(4,128)(2,1)S(1)}, bf16[4,1280]{1,0:T(4,128)(2,1)}, u32[]{:S(2)}) copy-start(bf16[4,1280]{1,0:T(4,128)(2,1)} %query_ref.1) | copy-start | bytes 30724
  19.5 0.8 copy-start.4
  20.4 18.2 %collective-permute-start.2 = (bf16[2,640,256]{2,1,0:T(8,128)(2,1)}, bf16[2,640,256]{2,1,0:T(8,128)(2,1)}, u32[]{:S(2)}, u32[]{:S(2)}) collective-permute-start(bf16[2,640,256]{2,1,0:T(8,128)(2,1)} %get-tuple-element.40), channel_id=1, source_target_pairs={{0,64},{64,128},{128,192},{192,0},{1,65},{65,129},{129,193},{193,1... | collective-permute-start | bytes 1966088 | tf_op jit(solution)/shard_map/ppermute | solution.py:22
  20.4 19.1 %collective-permute-start.3 = (bf16[2,640,256]{2,1,0:T(8,128)(2,1)}, bf16[2,640,256]{2,1,0:T(8,128)(2,1)}, u32[]{:S(2)}, u32[]{:S(2)}) collective-permute-start(bf16[2,640,256]{2,1,0:T(8,128)(2,1)} %get-tuple-element.41), channel_id=1, source_target_pairs={{0,192},{64,0},{128,64},{192,128},{1,193},{65,1},{129,65},{193,129... | collective-permute-start | bytes 1966088 | tf_op jit(solution)/shard_map/ppermute | solution.py:22
  23.6 16.7 %collective-permute-start.4 = (bf16[4,320,256]{2,1,0:T(8,128)(2,1)}, bf16[4,320,256]{2,1,0:T(8,128)(2,1)}, u32[]{:S(2)}, u32[]{:S(2)}) collective-permute-start(bf16[4,320,256]{2,1,0:T(8,128)(2,1)} %get-tuple-element.49), channel_id=1, source_target_pairs={{0,2},{2,4},{4,6},{6,0},{1,3},{3,5},{5,7},{7,1},{8,10},{10,12},{12... | collective-permute-start | bytes 1966088 | tf_op jit(solution)/shard_map/ppermute | solution.py:22
  24.0 18.7 %collective-permute-start.5 = (bf16[4,320,256]{2,1,0:T(8,128)(2,1)}, bf16[4,320,256]{2,1,0:T(8,128)(2,1)}, u32[]{:S(2)}, u32[]{:S(2)}) collective-permute-start(bf16[4,320,256]{2,1,0:T(8,128)(2,1)} %get-tuple-element.50), channel_id=1, source_target_pairs={{0,6},{2,0},{4,2},{6,4},{1,7},{3,1},{5,3},{7,5},{8,14},{10,8},{12,... | collective-permute-start | bytes 1966088 | tf_op jit(solution)/shard_map/ppermute | solution.py:22
  26.8 23.4 %collective-permute-start.8 = (bf16[4,4,640]{2,1,0:T(4,128)(2,1)S(1)}, bf16[4,4,640]{2,1,0:T(4,128)(2,1)S(1)}, u32[]{:S(2)}, u32[]{:S(2)}) collective-permute-start(bf16[4,4,640]{2,1,0:T(4,128)(2,1)S(1)} %dynamic-slice_bitcast_fusion.4), channel_id=1, source_target_pairs={{0,4},{4,0},{1,5},{5,1},{2,6},{6,2},{3,7},{7,3},{8,12},{12,8},{9,1... | collective-permute-start | bytes 61448 | tf_op jit(solution)/shard_map/ppermute | solution.py:26
  27.6 2.1 %copy-start.3 = (bf16[384,5120]{1,0:T(8,128)(2,1)S(1)}, bf16[384,5120]{1,0:T(8,128)(2,1)}, u32[]{:S(2)}) copy-start(bf16[384,5120]{1,0:T(8,128)(2,1)} %a_ref.3) | copy-start | bytes 11796484
  29.7 14.2 %copy-start.5 = (bf16[2,640,256]{2,1,0:T(8,128)(2,1)S(1)}, bf16[2,640,256]{2,1,0:T(8,128)(2,1)}, u32[]{:S(2)}) copy-start(bf16[2,640,256]{2,1,0:T(8,128)(2,1)} %copy-done.4) | copy-start | bytes 1966084
  38.6 16.1 %collective-permute-start.11 = (bf16[4,320,256]{2,1,0:T(8,128)(2,1)S(1)}, bf16[4,320,256]{2,1,0:T(8,128)(2,1)S(1)}, u32[]{:S(2)}, u32[]{:S(2)}) collective-permute-start(bf16[4,320,256]{2,1,0:T(8,128)(2,1)S(1)} %get-tuple-element.56), channel_id=1, source_target_pairs={{0,6},{2,0},{4,2},{6,4},{1,7},{3,1},{5,3},{7,5},{8,14},{10,8},{12,... | collective-permute-start | bytes 1966088 | tf_op jit(solution)/shard_map/ppermute | solution.py:22
  39.5 18.9 %collective-permute-start.9 = (bf16[2,640,256]{2,1,0:T(8,128)(2,1)S(1)}, bf16[2,640,256]{2,1,0:T(8,128)(2,1)S(1)}, u32[]{:S(2)}, u32[]{:S(2)}) collective-permute-start(bf16[2,640,256]{2,1,0:T(8,128)(2,1)S(1)} %get-tuple-element.54), channel_id=1, source_target_pairs={{0,64},{64,128},{128,192},{192,0},{1,65},{65,129},{129,193},{193,1... | collective-permute-start | bytes 1966088 | tf_op jit(solution)/shard_map/ppermute | solution.py:22
  40.3 15.9 %collective-permute-start.7 = (bf16[2,640,256]{2,1,0:T(8,128)(2,1)S(1)}, bf16[2,640,256]{2,1,0:T(8,128)(2,1)S(1)}, u32[]{:S(2)}, u32[]{:S(2)}) collective-permute-start(bf16[2,640,256]{2,1,0:T(8,128)(2,1)S(1)} %get-tuple-element.52), channel_id=1, source_target_pairs={{0,192},{64,0},{128,64},{192,128},{1,193},{65,1},{129,65},{193,129... | collective-permute-start | bytes 1966088 | tf_op jit(solution)/shard_map/ppermute | solution.py:22
  42.7 15.6 %collective-permute-start.10 = (bf16[4,320,256]{2,1,0:T(8,128)(2,1)S(1)}, bf16[4,320,256]{2,1,0:T(8,128)(2,1)S(1)}, u32[]{:S(2)}, u32[]{:S(2)}) collective-permute-start(bf16[4,320,256]{2,1,0:T(8,128)(2,1)S(1)} %get-tuple-element.55), channel_id=1, source_target_pairs={{0,2},{2,4},{4,6},{6,0},{1,3},{3,5},{5,7},{7,1},{8,10},{10,12},{12... | collective-permute-start | bytes 1966088 | tf_op jit(solution)/shard_map/ppermute | solution.py:22
  50.2 20.1 %collective-permute-start.13 = (bf16[2,640,256]{2,1,0:T(8,128)(2,1)}, bf16[2,640,256]{2,1,0:T(8,128)(2,1)}, u32[]{:S(2)}, u32[]{:S(2)}) collective-permute-start(bf16[2,640,256]{2,1,0:T(8,128)(2,1)} %add_convert_fusion.2), channel_id=1, source_target_pairs={{0,64},{64,128},{128,192},{192,0},{1,65},{65,129},{129,193},{193,1... | collective-permute-start | bytes 1966088 | tf_op jit(solution)/shard_map/ppermute | solution.py:22
  54.7 4.9 %copy-start.8 = (bf16[4,320,256]{2,1,0:T(8,128)(2,1)}, bf16[4,320,256]{2,1,0:T(8,128)(2,1)S(1)}, u32[]{:S(2)}) copy-start(bf16[4,320,256]{2,1,0:T(8,128)(2,1)S(1)} %collective-permute-done.11) | copy-start | bytes 1966084
  54.7 15.6 %collective-permute-start.12 = (bf16[4,320,256]{2,1,0:T(8,128)(2,1)}, bf16[4,320,256]{2,1,0:T(8,128)(2,1)S(1)}, u32[]{:S(2)}, u32[]{:S(2)}) collective-permute-start(bf16[4,320,256]{2,1,0:T(8,128)(2,1)} %add_convert_fusion.3), channel_id=1, source_target_pairs={{0,6},{2,0},{4,2},{6,4},{1,7},{3,1},{5,3},{7,5},{8,14},{10,8},{12,... | collective-permute-start | bytes 1966088 | tf_op jit(solution)/shard_map/ppermute | solution.py:22
  56.2 16.1 %collective-permute-start.6 = (bf16[4,320,256]{2,1,0:T(8,128)(2,1)}, bf16[4,320,256]{2,1,0:T(8,128)(2,1)}, u32[]{:S(2)}, u32[]{:S(2)}) collective-permute-start(bf16[4,320,256]{2,1,0:T(8,128)(2,1)} %add_convert_fusion.4), channel_id=1, source_target_pairs={{0,2},{2,4},{4,6},{6,0},{1,3},{3,5},{5,7},{7,1},{8,10},{10,12},{12... | collective-permute-start | bytes 1966088 | tf_op jit(solution)/shard_map/ppermute | solution.py:22
  58.4 1.2 copy-start.10
  58.4 1.3 copy-start.9
  59.7 25.1 %collective-permute-start.15 = (bf16[2,640,256]{2,1,0:T(8,128)(2,1)}, bf16[2,640,256]{2,1,0:T(8,128)(2,1)}, u32[]{:S(2)}, u32[]{:S(2)}) collective-permute-start(bf16[2,640,256]{2,1,0:T(8,128)(2,1)} %add_convert_fusion.1), channel_id=1, source_target_pairs={{0,192},{64,0},{128,64},{192,128},{1,193},{65,1},{129,65},{193,129... | collective-permute-start | bytes 1966088 | tf_op jit(solution)/shard_map/ppermute | solution.py:22
  74.4 3.1 %copy-start.12 = (bf16[80,512]{1,0:T(8,128)(2,1)S(1)}, bf16[80,512]{1,0:T(8,128)(2,1)}, u32[]{:S(2)}) copy-start(bf16[80,512]{1,0:T(8,128)(2,1)} %weight_ref.1) | copy-start | bytes 245764
  75.4 9.3 %copy-start.11 = (bf16[2,640,256]{2,1,0:T(8,128)(2,1)S(1)}, bf16[2,640,256]{2,1,0:T(8,128)(2,1)}, u32[]{:S(2)}) copy-start(bf16[2,640,256]{2,1,0:T(8,128)(2,1)} %copy-done.10) | copy-start | bytes 1966084
  75.4 14.0 %collective-permute-start.18 = (bf16[640,256]{1,0:T(8,128)(2,1)}, bf16[640,256]{1,0:T(8,128)(2,1)}, u32[]{:S(2)}, u32[]{:S(2)}) collective-permute-start(bf16[640,256]{1,0:T(8,128)(2,1)} %get-tuple-element.78), channel_id=1, source_target_pairs={{0,128},{64,192},{128,0},{192,64},{1,129},{65,193},{129,1},{193,65... | collective-permute-start | bytes 983048 | tf_op jit(solution)/shard_map/ppermute | solution.py:22
  77.5 24.6 %collective-permute-start.19 = (bf16[640,256]{1,0:T(8,128)(2,1)}, bf16[640,256]{1,0:T(8,128)(2,1)}, u32[]{:S(2)}, u32[]{:S(2)}) collective-permute-start(bf16[640,256]{1,0:T(8,128)(2,1)} %get-tuple-element.80), channel_id=1, source_target_pairs={{0,64},{64,128},{128,192},{192,0},{1,65},{65,129},{129,193},{193,1... | collective-permute-start | bytes 983048 | tf_op jit(solution)/shard_map/ppermute | solution.py:22
  78.3 23.8 %collective-permute-start.20 = (bf16[640,256]{1,0:T(8,128)(2,1)}, bf16[640,256]{1,0:T(8,128)(2,1)}, u32[]{:S(2)}, u32[]{:S(2)}) collective-permute-start(bf16[640,256]{1,0:T(8,128)(2,1)} %get-tuple-element.79), channel_id=1, source_target_pairs={{0,192},{64,0},{128,64},{192,128},{1,193},{65,1},{129,65},{193,129... | collective-permute-start | bytes 983048 | tf_op jit(solution)/shard_map/ppermute | solution.py:22
  82.8 20.7 %collective-permute-start.14 = (bf16[640,256]{1,0:T(8,128)(2,1)}, bf16[640,256]{1,0:T(8,128)(2,1)}, u32[]{:S(2)}, u32[]{:S(2)}) collective-permute-start(bf16[640,256]{1,0:T(8,128)(2,1)} %fusion.6), channel_id=1, source_target_pairs={{0,4},{2,6},{4,0},{6,2},{1,5},{3,7},{5,1},{7,3},{8,12},{10,14},{12... | collective-permute-start | bytes 983048 | tf_op jit(solution)/shard_map/ppermute | solution.py:22
  84.7 5.9 %copy-start.13 = (bf16[4,8,640]{2,1,0:T(8,128)(2,1)S(1)}, bf16[4,8,640]{2,1,0:T(8,128)(2,1)}, u32[]{:S(2)}) copy-start(bf16[4,8,640]{2,1,0:T(8,128)(2,1)} %pad_maximum_fusion.2) | copy-start | bytes 122884
  86.9 16.6 %collective-permute-start.16 = (bf16[640,256]{1,0:T(8,128)(2,1)}, bf16[640,256]{1,0:T(8,128)(2,1)S(1)}, u32[]{:S(2)}, u32[]{:S(2)}) collective-permute-start(bf16[640,256]{1,0:T(8,128)(2,1)} %get-tuple-element.76), channel_id=1, source_target_pairs={{0,2},{2,4},{4,6},{6,0},{1,3},{3,5},{5,7},{7,1},{8,10},{10,12},{12... | collective-permute-start | bytes 983048 | tf_op jit(solution)/shard_map/ppermute | solution.py:22
  89.4 14.1 %collective-permute-start.17 = (bf16[640,256]{1,0:T(8,128)(2,1)}, bf16[640,256]{1,0:T(8,128)(2,1)S(1)}, u32[]{:S(2)}, u32[]{:S(2)}) collective-permute-start(bf16[640,256]{1,0:T(8,128)(2,1)} %get-tuple-element.77), channel_id=1, source_target_pairs={{0,6},{2,0},{4,2},{6,4},{1,7},{3,1},{5,3},{7,5},{8,14},{10,8},{12,... | collective-permute-start | bytes 983048 | tf_op jit(solution)/shard_map/ppermute | solution.py:22
  91.4 21.8 %all-to-all-start = ((bf16[32,8,640]{2,1,0:T(8,128)(2,1)}), bf16[32,8,640]{2,1,0:T(8,128)(2,1)}, u32[]{:S(2)}, u32[]{:S(2)}) async-start(bf16[32,8,640]{2,1,0:T(8,128)(2,1)} %bitcast.30), calls=%async_computation | async-start | bytes 655360 | tf_op jit(solution)/shard_map/all_to_all | solution.py:233
  115.5 12.1 %all-to-all-start.1 = ((bf16[8,32,512]{2,1,0:T(8,128)(2,1)}), bf16[8,32,512]{2,1,0:T(8,128)(2,1)S(1)}, u32[]{:S(2)}, u32[]{:S(2)}) async-start(bf16[8,32,512]{2,1,0:T(8,128)(2,1)} %reshape.149), calls=%async_computation.1 | async-start | bytes 524288 | tf_op jit(solution)/shard_map/all_to_all | solution.py:273
  127.7 4.9 %copy-start.6 = (s32[4]{0:T(128)S(1)}, s32[4]{0:T(128)}, u32[]{:S(2)}) copy-start(s32[4]{0:T(128)} %lengths.1) | copy-start | bytes 52
  128.6 19.4 %all-to-all-start.2 = ((bf16[8,84,512]{2,1,0:T(8,128)(2,1)}), bf16[8,84,512]{2,1,0:T(8,128)(2,1)S(1)}, u32[]{:S(2)}, u32[]{:S(2)}) async-start(bf16[8,84,512]{2,1,0:T(8,128)(2,1)} %pad_maximum_fusion), calls=%async_computation.2 | async-start | bytes 1441792 | tf_op jit(solution)/shard_map/all_to_all | solution.py:277
  132.6 2.2 %copy-start.1 = (bf16[4,1024,512]{2,1,0:T(8,128)(2,1)S(1)}, bf16[4,1024,512]{2,1,0:T(8,128)(2,1)}, u32[]{:S(2)}) copy-start(bf16[4,1024,512]{2,1,0:T(8,128)(2,1)} %cache_ref.1) | copy-start | bytes 12582916
  148.0 0.9 copy-start.7
